TPU v7x, 256 devices: a whole 4x4x8 slice. The times are simulated.
256 devices in a mesh: rows: 64 (over y, z, core), rep: 4 (over x).
Axes of the slice: x: 4, y: 4, z: 8, core: 2. Of those that a mesh axis runs over, the one named last changes fastest.
Arguments:
- tiles: bfloat16 [64, 4, 32, 256, 256], P('rows', 'rep'), may hold values from -6 to 6
- tile_row: int32 [64, 4, 32], P('rows', 'rep'), may hold values from 0 to 3
- tile_col: int32 [64, 4, 32], P('rows', 'rep'), may hold values from 0 to 3
- tile_round: int32 [64, 4, 32], P('rows', 'rep'), may hold values from 0 to 4
- tile_count: int32 [64, 4], P('rows', 'rep'), may hold values from 8 to 32, as said below
- start_block: float32 [32, 65536], P(None, ('rows', 'rep')), may hold values from -6 to 6
Outputs:
- next_block: float32 [32, 65536], P(None, ('rows', 'rep'))
- coefficients: float32 [2, 64, 32], replicated
- factors: float32 [2, 32, 32], replicated
Inputs may be any that keep to these rules, and one draw needn't show every extreme that they name: `tile_count`: slots at or above a device's count hold entries that are not part of the matrix; in every draw some device has count 32 and some has the least count.
All inputs are finite; a program needn't handle non-finite values.
Results may differ from a plain program's by a relative error of at most 0.0041.
Values may be sent and summed in bfloat16 or wider, within the bound.
No kernel may reach another device: no remote copies, remote signals or barrier semaphores. Data moves between devices by JAX's collectives and lax.ppermute only.
A program may use at most 64 MiB of HBM per device.

v0:
```python
import jax
import jax.numpy as jnp
from jax import lax
from jax.sharding import PartitionSpec as P

ROUNDS = 4
ITERS = 2


def passed_along(x, axis, by):
    size = lax.axis_size(axis)
    return lax.ppermute(x, axis, [(i, (i + by) % size) for i in range(size)])


def body(tiles, tile_row, tile_col, tile_round, tile_count, start_block):
    tile_mats = tiles[0, 0]
    tile_rows = tile_row[0, 0]
    tile_cols = tile_col[0, 0]
    tile_rounds = tile_round[0, 0]
    live_count = tile_count[0, 0]
    vec_width = start_block.shape[0]
    quarter = start_block.shape[1]
    members = lax.axis_size("rep")
    devices = lax.axis_size("rows")
    member = lax.axis_index("rep")
    slot_total = tile_mats.shape[0]
    edge_size = tile_mats.shape[1]
    blocks_owned = quarter * members // edge_size
    shifts = [max(1, devices // 2**round_index) for round_index in range(1, ROUNDS + 1)]
    live_mask = (jnp.arange(slot_total, dtype=jnp.int32) < live_count).astype(jnp.float32)
    block_ids = jnp.arange(blocks_owned, dtype=jnp.int32)
    target_ids = jnp.arange((ROUNDS + 1) * blocks_owned, dtype=jnp.int32)
    pick_row = (tile_rows[:, None] == block_ids[None, :]).astype(jnp.float32) * live_mask[:, None]
    pick_dest = ((tile_rounds * blocks_owned + tile_cols)[:, None] == target_ids[None, :]).astype(
        jnp.float32
    ) * live_mask[:, None]
    highest = lax.Precision.HIGHEST

    def pick_share(matrix):
        return lax.dynamic_slice_in_dim(matrix, member * quarter, quarter, 1)

    start_gram = lax.psum(jnp.dot(start_block, start_block.T, precision=highest), ("rows", "rep"))
    start_factor = jnp.linalg.cholesky(start_gram)
    basis_now = jax.scipy.linalg.solve_triangular(start_factor, start_block, lower=True)
    basis_now = lax.all_gather(basis_now, "rep", axis=1, tiled=True)
    previous = jnp.zeros_like(basis_now)
    coefficient_list = []
    factor_list = []
    for iteration in range(ITERS):
        basis_bf = basis_now.astype(jnp.bfloat16)
        blocks = basis_bf.reshape(vec_width, blocks_owned, edge_size)
        sources = [blocks] + [passed_along(blocks, "rows", -offset) for offset in shifts]
        stacked = jnp.stack(sources, 0)
        inputs = stacked[tile_rounds, :, tile_cols]
        own_blocks = blocks[:, tile_rows]
        forward = jnp.einsum("tkj,tij->tki", inputs, tile_mats, preferred_element_type=jnp.float32)
        backward = jnp.einsum(
            "kti,tij->tkj", own_blocks, tile_mats, preferred_element_type=jnp.float32
        )
        own_sum = jnp.einsum("tb,tki->kbi", pick_row, forward, precision=highest)
        targets = jnp.einsum("tc,tkj->kcj", pick_dest, backward, precision=highest)
        total_sum = own_sum + targets[:, :blocks_owned]
        for apply_round_index, offset in enumerate(shifts):
            outgoing = targets[
                :, (apply_round_index + 1) * blocks_owned : (apply_round_index + 2) * blocks_owned
            ].astype(jnp.bfloat16)
            arrived = passed_along(outgoing, "rows", offset)
            total_sum = total_sum + arrived.astype(jnp.float32)
        partial_value = total_sum.reshape(vec_width, blocks_owned * edge_size)
        stacked_basis = jnp.concatenate([basis_now, previous], axis=0)
        image_block = lax.psum(partial_value, "rep")
        image_share = pick_share(image_block)
        basis_share = pick_share(stacked_basis)
        coefficient = lax.psum(
            jnp.dot(basis_share, image_share.T, precision=highest), ("rows", "rep")
        )
        residue = image_block - jnp.dot(coefficient.T, stacked_basis, precision=highest)
        residue_share = pick_share(residue)
        gram_matrix = lax.psum(
            jnp.dot(residue_share, residue_share.T, precision=highest), ("rows", "rep")
        )
        lower_factor = jnp.linalg.cholesky(gram_matrix)
        new_basis = jax.scipy.linalg.solve_triangular(lower_factor, residue, lower=True)
        coefficient_list.append(coefficient)
        factor_list.append(lower_factor)
        previous = basis_now
        basis_now = new_basis
    result_block = pick_share(basis_now)
    return (result_block, jnp.stack(coefficient_list, 0), jnp.stack(factor_list, 0))


def solution(mesh):
    placed = (
        P("rows", "rep", None, None, None),
        P("rows", "rep", None),
        P("rows", "rep", None),
        P("rows", "rep", None),
        P("rows", "rep"),
        P(None, ("rows", "rep")),
    )
    return jax.shard_map(
        body,
        mesh=mesh,
        in_specs=placed,
        out_specs=(P(None, ("rows", "rep")), P(), P()),
        check_vma=False,
    )
```

profile of v0, /device:TPU:32, one launch (start us, length us, event | category | flops | bytes accessed | tf_op | source)
XLA Modules:
  0.0 578.6 jit_solution(2095422576652442080)
XLA Ops:
  8.1 79.9 %psum.49 = f32[32,32]{0,1:T(8,128)S(1)} all-reduce(f32[32,32]{0,1:T(8,128)S(1)} %fusion.99), channel_id=1, replica_groups=mesh['rows'=64,'rep'=4] {'rows','rep'}, use_global_device_ids=true, to_apply=%region_0.0 | all-reduce | flops 1024 | bytes 8192 | tf_op jit(solution)/shard_map/psum | solution.py:42
  88.0 2.9 cholesky.59
  92.3 2.4 custom-call.9
  95.0 12.0 %all_gather.3 = f32[32,1024]{1,0:T(8,128)S(1)} all-gather(f32[32,256]{1,0:T(8,128)S(1)} %fusion.34), channel_id=1, replica_groups=mesh['rows'=64,'rep'=4] {'rep'}, dimensions={1}, use_global_device_ids=true | all-gather | bytes 163840 | tf_op jit(solution)/shard_map/all_gather | solution.py:45
  107.0 1.4 collective-permute-start
  109.2 5.0 collective-permute-start.2
  114.2 1.5 collective-permute-start.3
  118.3 3.0 fusion.4
  121.3 1.5 fusion.96
  122.9 1.5 collective-permute-start.7
  126.8 2.5 collective-permute-start.4
  130.0 3.5 fusion.6
  136.9 43.4 %all-reduce.4.cloned.1.call-done = f32[32,1024]{1,0:T(8,128)} async-done(((f32[32,1024]{1,0:T(8,128)}), f32[32,1024]{1,0:T(8,128)}) %all-reduce.4.cloned.1.call-update) | async-done | bytes 131088 | tf_op jit(solution)/shard_map/psum | solution.py:71
  181.3 75.8 %psum.51 = f32[64,32]{0,1:T(8,128)S(1)} all-reduce(f32[64,32]{0,1:T(8,128)S(1)} %fusion.17), channel_id=1, replica_groups=mesh['rows'=64,'rep'=4] {'rows','rep'}, use_global_device_ids=true, to_apply=%region_4.6 | all-reduce | flops 2048 | bytes 16384 | tf_op jit(solution)/shard_map/psum | solution.py:74
  258.4 73.6 %psum.52 = f32[32,32]{0,1:T(8,128)S(1)} all-reduce(f32[32,32]{0,1:T(8,128)S(1)} %fusion.24), channel_id=1, replica_groups=mesh['rows'=64,'rep'=4] {'rows','rep'}, use_global_device_ids=true, to_apply=%region_5.7 | all-reduce | flops 1024 | bytes 8192 | tf_op jit(solution)/shard_map/psum | solution.py:79
  332.1 2.9 cholesky.70
  336.4 2.4 custom-call.15
  339.8 1.5 collective-permute-start.8
  341.3 1.7 collective-permute-start.9
  343.0 4.0 collective-permute-start.10
  347.0 1.5 collective-permute-start.11
  348.5 3.0 fusion
  351.5 1.5 fusion.98
  353.0 1.5 collective-permute-start.15
  354.6 2.0 collective-permute-start.14
  357.2 2.2 collective-permute-start.12
  360.1 3.5 fusion.2
  367.0 44.1 %all-reduce.6.cloned.1.call-done = f32[32,1024]{1,0:T(8,128)} async-done(((f32[32,1024]{1,0:T(8,128)}), f32[32,1024]{1,0:T(8,128)}) %all-reduce.6.cloned.1.call-update) | async-done | bytes 131088 | tf_op jit(solution)/shard_map/psum | solution.py:71
  412.0 75.8 %psum.54 = f32[64,32]{0,1:T(8,128)S(1)} all-reduce(f32[64,32]{0,1:T(8,128)S(1)} %fusion.19), channel_id=1, replica_groups=mesh['rows'=64,'rep'=4] {'rows','rep'}, use_global_device_ids=true, to_apply=%region_7.10 | all-reduce | flops 2048 | bytes 16384 | tf_op jit(solution)/shard_map/psum | solution.py:74
  489.1 73.6 %psum.55 = f32[32,32]{0,1:T(8,128)S(1)} all-reduce(f32[32,32]{0,1:T(8,128)S(1)} %fusion.21), channel_id=1, replica_groups=mesh['rows'=64,'rep'=4] {'rows','rep'}, use_global_device_ids=true, to_apply=%region_8.11 | all-reduce | flops 1024 | bytes 8192 | tf_op jit(solution)/shard_map/psum | solution.py:79
  562.8 2.9 cholesky.81
  567.1 2.4 custom-call.16
  (90 shorter events, 27.0 us)
Async XLA Ops:
  7.2 0.8 copy-start
  7.2 173.1 %all-reduce.4.cloned.1.call-start = ((), (), s32[]{:S(2)}) async-start(), calls=%async_computation | async-start | bytes 262144 | tf_op jit(solution)/shard_map/psum | solution.py:71
  107.0 17.5 %collective-permute-start = (bf16[32,4,256]{2,0,1:T(8,128)(2,1)S(1)}, bf16[32,4,256]{2,0,1:T(8,128)(2,1)S(1)}, u32[]{:S(2)}, u32[]{:S(2)}) collective-permute-start(bf16[32,4,256]{2,0,1:T(8,128)(2,1)S(1)} %bitcast.140), channel_id=1, source_target_pairs={{0,128},{4,132},{8,136},{12,140},{16,144},{20,148},{24,152},{28,15... | collective-permute-start | bytes 196616 | tf_op jit(solution)/shard_map/ppermute | solution.py:12
  108.4 17.2 %collective-permute-start.1 = (bf16[32,4,256]{2,0,1:T(8,128)(2,1)S(1)}, bf16[32,4,256]{2,0,1:T(8,128)(2,1)S(1)}, u32[]{:S(2)}, u32[]{:S(2)}) collective-permute-start(bf16[32,4,256]{2,0,1:T(8,128)(2,1)S(1)} %bitcast.141), channel_id=1, source_target_pairs={{0,192},{4,196},{8,200},{12,204},{16,208},{20,212},{24,216},{28,22... | collective-permute-start | bytes 196616 | tf_op jit(solution)/shard_map/ppermute | solution.py:12
  109.2 17.6 %collective-permute-start.2 = (bf16[32,4,256]{2,0,1:T(8,128)(2,1)S(1)}, bf16[32,4,256]{2,0,1:T(8,128)(2,1)S(1)}, u32[]{:S(2)}, u32[]{:S(2)}) collective-permute-start(bf16[32,4,256]{2,0,1:T(8,128)(2,1)S(1)} %bitcast.142), channel_id=1, source_target_pairs={{0,224},{4,228},{8,232},{12,236},{16,240},{20,244},{24,248},{28,25... | collective-permute-start | bytes 196616 | tf_op jit(solution)/shard_map/ppermute | solution.py:12
  114.2 15.2 %collective-permute-start.3 = (bf16[32,4,256]{2,0,1:T(8,128)(2,1)S(1)}, bf16[32,4,256]{2,0,1:T(8,128)(2,1)S(1)}, u32[]{:S(2)}, u32[]{:S(2)}) collective-permute-start(bf16[32,4,256]{2,0,1:T(8,128)(2,1)S(1)} %bitcast.143), channel_id=1, source_target_pairs={{0,240},{4,244},{8,248},{12,252},{16,0},{20,4},{24,8},{28,12},{32,... | collective-permute-start | bytes 196616 | tf_op jit(solution)/shard_map/ppermute | solution.py:12
  118.3 6.2 %copy-start.2 = (s32[1,1,32]{2,1,0:T(1,128)S(1)}, s32[1,1,32]{2,1,0:T(1,128)}, u32[]{:S(2)}) copy-start(s32[1,1,32]{2,1,0:T(1,128)} %param.11) | copy-start | bytes 388
  118.3 6.2 %copy-start.3 = (s32[1,1,32]{2,1,0:T(1,128)S(1)}, s32[1,1,32]{2,1,0:T(1,128)}, u32[]{:S(2)}) copy-start(s32[1,1,32]{2,1,0:T(1,128)} %param.12) | copy-start | bytes 388
  122.8 12.1 %copy-start.1 = (s32[1,1,32]{2,1,0:T(1,128)S(1)}, s32[1,1,32]{2,1,0:T(1,128)}, u32[]{:S(2)}) copy-start(s32[1,1,32]{2,1,0:T(1,128)} %param.10) | copy-start | bytes 388
  122.9 10.7 %collective-permute-start.7 = (bf16[32,4,256]{2,1,0:T(4,128)(2,1)S(1)}, bf16[32,4,256]{2,1,0:T(4,128)(2,1)S(1)}, u32[]{:S(2)}, u32[]{:S(2)}) collective-permute-start(bf16[32,4,256]{2,1,0:T(4,128)(2,1)S(1)} %get-tuple-element.10), channel_id=1, source_target_pairs={{0,16},{4,20},{8,24},{12,28},{16,32},{20,36},{24,40},{28,44},{32,4... | collective-permute-start | bytes 196616 | tf_op jit(solution)/shard_map/ppermute | solution.py:12
  124.5 10.4 %collective-permute-start.6 = (bf16[32,4,256]{2,1,0:T(4,128)(2,1)S(1)}, bf16[32,4,256]{2,1,0:T(4,128)(2,1)S(1)}, u32[]{:S(2)}, u32[]{:S(2)}) collective-permute-start(bf16[32,4,256]{2,1,0:T(4,128)(2,1)S(1)} %get-tuple-element.11), channel_id=1, source_target_pairs={{0,32},{4,36},{8,40},{12,44},{16,48},{20,52},{24,56},{28,60},{32,6... | collective-permute-start | bytes 196616 | tf_op jit(solution)/shard_map/ppermute | solution.py:12
  125.6 9.3 %collective-permute-start.5 = (bf16[32,4,256]{2,1,0:T(4,128)(2,1)S(1)}, bf16[32,4,256]{2,1,0:T(4,128)(2,1)S(1)}, u32[]{:S(2)}, u32[]{:S(2)}) collective-permute-start(bf16[32,4,256]{2,1,0:T(4,128)(2,1)S(1)} %get-tuple-element.12), channel_id=1, source_target_pairs={{0,64},{4,68},{8,72},{12,76},{16,80},{20,84},{24,88},{28,92},{32,9... | collective-permute-start | bytes 196616 | tf_op jit(solution)/shard_map/ppermute | solution.py:12
  126.8 8.0 %collective-permute-start.4 = (bf16[32,4,256]{2,1,0:T(4,128)(2,1)S(1)}, bf16[32,4,256]{2,1,0:T(4,128)(2,1)S(1)}, u32[]{:S(2)}, u32[]{:S(2)}) collective-permute-start(bf16[32,4,256]{2,1,0:T(4,128)(2,1)S(1)} %get-tuple-element.9), channel_id=1, source_target_pairs={{0,128},{4,132},{8,136},{12,140},{16,144},{20,148},{24,152},{28,15... | collective-permute-start | bytes 196616 | tf_op jit(solution)/shard_map/ppermute | solution.py:12
  136.9 274.1 %all-reduce.6.cloned.1.call-start = ((), (), s32[]{:S(2)}) async-start(), calls=%async_computation.1 | async-start | bytes 262144 | tf_op jit(solution)/shard_map/psum | solution.py:71
  339.8 14.8 %collective-permute-start.8 = (bf16[32,4,256]{2,0,1:T(8,128)(2,1)S(1)}, bf16[32,4,256]{2,0,1:T(8,128)(2,1)S(1)}, u32[]{:S(2)}, u32[]{:S(2)}) collective-permute-start(bf16[32,4,256]{2,0,1:T(8,128)(2,1)S(1)} %bitcast.146), channel_id=1, source_target_pairs={{0,128},{4,132},{8,136},{12,140},{16,144},{20,148},{24,152},{28,15... | collective-permute-start | bytes 196616 | tf_op jit(solution)/shard_map/ppermute | solution.py:12
  341.3 15.4 %collective-permute-start.9 = (bf16[32,4,256]{2,0,1:T(8,128)(2,1)S(1)}, bf16[32,4,256]{2,0,1:T(8,128)(2,1)S(1)}, u32[]{:S(2)}, u32[]{:S(2)}) collective-permute-start(bf16[32,4,256]{2,0,1:T(8,128)(2,1)S(1)} %bitcast.147), channel_id=1, source_target_pairs={{0,192},{4,196},{8,200},{12,204},{16,208},{20,212},{24,216},{28,22... | collective-permute-start | bytes 196616 | tf_op jit(solution)/shard_map/ppermute | solution.py:12
  343.0 14.2 %collective-permute-start.10 = (bf16[32,4,256]{2,0,1:T(8,128)(2,1)S(1)}, bf16[32,4,256]{2,0,1:T(8,128)(2,1)S(1)}, u32[]{:S(2)}, u32[]{:S(2)}) collective-permute-start(bf16[32,4,256]{2,0,1:T(8,128)(2,1)S(1)} %bitcast.148), channel_id=1, source_target_pairs={{0,224},{4,228},{8,232},{12,236},{16,240},{20,244},{24,248},{28,25... | collective-permute-start | bytes 196616 | tf_op jit(solution)/shard_map/ppermute | solution.py:12
  347.0 12.5 %collective-permute-start.11 = (bf16[32,4,256]{2,0,1:T(8,128)(2,1)S(1)}, bf16[32,4,256]{2,0,1:T(8,128)(2,1)S(1)}, u32[]{:S(2)}, u32[]{:S(2)}) collective-permute-start(bf16[32,4,256]{2,0,1:T(8,128)(2,1)S(1)} %bitcast.149), channel_id=1, source_target_pairs={{0,240},{4,244},{8,248},{12,252},{16,0},{20,4},{24,8},{28,12},{32,... | collective-permute-start | bytes 196616 | tf_op jit(solution)/shard_map/ppermute | solution.py:12
  353.0 10.6 %collective-permute-start.15 = (bf16[32,4,256]{2,1,0:T(4,128)(2,1)S(1)}, bf16[32,4,256]{2,1,0:T(4,128)(2,1)S(1)}, u32[]{:S(2)}, u32[]{:S(2)}) collective-permute-start(bf16[32,4,256]{2,1,0:T(4,128)(2,1)S(1)} %get-tuple-element.6), channel_id=1, source_target_pairs={{0,16},{4,20},{8,24},{12,28},{16,32},{20,36},{24,40},{28,44},{32,4... | collective-permute-start | bytes 196616 | tf_op jit(solution)/shard_map/ppermute | solution.py:12
  354.6 10.4 %collective-permute-start.14 = (bf16[32,4,256]{2,1,0:T(4,128)(2,1)S(1)}, bf16[32,4,256]{2,1,0:T(4,128)(2,1)S(1)}, u32[]{:S(2)}, u32[]{:S(2)}) collective-permute-start(bf16[32,4,256]{2,1,0:T(4,128)(2,1)S(1)} %get-tuple-element.7), channel_id=1, source_target_pairs={{0,32},{4,36},{8,40},{12,44},{16,48},{20,52},{24,56},{28,60},{32,6... | collective-permute-start | bytes 196616 | tf_op jit(solution)/shard_map/ppermute | solution.py:12
  356.6 8.3 %collective-permute-start.13 = (bf16[32,4,256]{2,1,0:T(4,128)(2,1)S(1)}, bf16[32,4,256]{2,1,0:T(4,128)(2,1)S(1)}, u32[]{:S(2)}, u32[]{:S(2)}) collective-permute-start(bf16[32,4,256]{2,1,0:T(4,128)(2,1)S(1)} %get-tuple-element.8), channel_id=1, source_target_pairs={{0,64},{4,68},{8,72},{12,76},{16,80},{20,84},{24,88},{28,92},{32,9... | collective-permute-start | bytes 196616 | tf_op jit(solution)/shard_map/ppermute | solution.py:12
  357.2 7.7 %collective-permute-start.12 = (bf16[32,4,256]{2,1,0:T(4,128)(2,1)S(1)}, bf16[32,4,256]{2,1,0:T(4,128)(2,1)S(1)}, u32[]{:S(2)}, u32[]{:S(2)}) collective-permute-start(bf16[32,4,256]{2,1,0:T(4,128)(2,1)S(1)} %get-tuple-element.5), channel_id=1, source_target_pairs={{0,128},{4,132},{8,136},{12,140},{16,144},{20,148},{24,152},{28,15... | collective-permute-start | bytes 196616 | tf_op jit(solution)/shard_map/ppermute | solution.py:12
Sparse Core Ops, SparseCore 0:
  137.0 43.2 all-reduce.3
  367.1 43.8 all-reduce.5
where the time goes:
time: 581 us; the launch traced here: 579 us
  blocking collectives  391 us (67%)
  waiting for transfers between devices  90.2 us (16%)
  starting transfers between devices  30.1 us (5%)
  matrix products  24.2 us (4%)
  other arithmetic  22.7 us (4%)
  between operations  15.1 us (3%)
    psum x2, blocking collectives, body(): lax.psum(jnp.dot(basis_share, image_share.T, precision=highest), ('rows',...  152 us
    psum x2, blocking collectives, body(): lax.psum(jnp.dot(residue_share, residue_share.T, precision=highest), ('ro...  147 us
    psum x2, waiting for transfers between devices, body(): image_block = lax.psum(partial_value, 'rep')  87.4 us
    psum x1, blocking collectives, body(): lax.psum(jnp.dot(start_block, start_block.T, precision=highest), ('rows',...  79.9 us
    ppermute x16, starting transfers between devices, passed_along(): return lax.ppermute(x, axis, [(i, (i + by) % size) for i in range(size)])  30 us
    all_gather x1, blocking collectives, body(): basis_now = lax.all_gather(basis_now, 'rep', axis=1, tiled=True)  12 us
  transfers between devices with their start and end apart: 18, of which 4 were waited for; matrix products, arithmetic and copies ran while one was open for 3% of the time, Pallas kernels for 0%

commit v1 on v0

v1 whole, which is shorter than its diff:
```python
import functools

import jax
import jax.numpy as jnp
from jax import lax
from jax.experimental import pallas as pl
from jax.experimental.pallas import tpu as pltpu
from jax.sharding import PartitionSpec as P

ROUNDS = 4
F32 = jnp.float32
BF16 = jnp.bfloat16
HIGHEST = lax.Precision.HIGHEST
CHUNK = 4
VMEM_LIMIT = 40 * 1024 * 1024


def dot(a, b, dims, precision=None):
    return lax.dot_general(a, b, (dims, ((), ())), precision=precision, preferred_element_type=F32)


NN = ((1,), (0,))
NT = ((1,), (1,))
TN = ((0,), (0,))


def split(x):
    high = x.astype(BF16)
    low = (x - high.astype(F32)).astype(BF16)
    return jnp.concatenate([high, low], axis=0)


def tile_copies(tiles_ref, held, sems):
    copies = []
    for i in range(held.shape[0] // CHUNK):
        part = pl.ds(i * CHUNK, CHUNK)
        copies.append(pltpu.make_async_copy(tiles_ref.at[part], held.at[part], sems.at[i]))
    return copies


def backward_kernel(row, col, rnd, count, tiles_ref, q_ref, *rest):
    outs, (held, terms, total, sems) = rest[:-4], rest[-4:]
    blocks = q_ref.shape[0]
    trash = total.shape[0] - 1
    copies = tile_copies(tiles_ref, held, sems)
    for copy in copies:
        copy.start()
    member = lax.axis_index("rep")
    for b in range(blocks):
        terms[b] = split(q_ref[b])
    total[...] = jnp.zeros_like(total)
    for t in range(held.shape[0]):
        if t % CHUNK == 0:
            copies[t // CHUNK].wait()
        source = lax.rem(member - row[t] + blocks, blocks)
        target = rnd[t] * blocks + lax.rem(member - col[t] + blocks, blocks)
        target = jnp.where(t < count[0], target, trash)
        product = dot(terms[source], held[t], NN)
        half = product.shape[0] // 2
        total[target] += product[:half] + product[half:]
    for i, out in enumerate(outs):
        out[...] = total[i * blocks : (i + 1) * blocks]


def forward_kernel(row, col, rnd, count, tiles_ref, kept_ref, *rest):
    sources, out, (held, terms, total, sems) = rest[: ROUNDS + 1], rest[ROUNDS + 1], rest[-4:]
    blocks = kept_ref.shape[0]
    trash = blocks
    copies = tile_copies(tiles_ref, held, sems)
    for copy in copies:
        copy.start()
    member = lax.axis_index("rep")
    for i, ref in enumerate(sources):
        for b in range(blocks):
            terms[i * blocks + b] = split(ref[b])
    total[:blocks] = kept_ref[...]
    total[trash] = jnp.zeros(total.shape[1:], F32)
    for t in range(held.shape[0]):
        if t % CHUNK == 0:
            copies[t // CHUNK].wait()
        source = rnd[t] * blocks + lax.rem(member - col[t] + blocks, blocks)
        target = lax.rem(member - row[t] + blocks, blocks)
        target = jnp.where(t < count[0], target, trash)
        product = dot(terms[source], held[t], NT)
        half = product.shape[0] // 2
        total[target] += product[:half] + product[half:]
    out[...] = total[:blocks]


def gram_kernel(s_ref, y_ref, z_ref, out):
    blocks, k, width = s_ref.shape
    grams = []
    for b in range(blocks):
        stack = jnp.concatenate([s_ref[b], y_ref[b], z_ref[b], jnp.zeros((k, width), F32)], axis=0)
        grams.append(dot(stack[: 3 * k], stack, NT, HIGHEST))
    half = blocks // 2
    pairs = [grams[i] + grams[i + half] for i in range(half)]
    out[...] = functools.reduce(lambda a, b: a + b, pairs)


def tail_kernel(gram_ref, s_ref, y_ref, z_ref, next_ref, coef_ref, fact_ref, upper, inverse):
    n, lanes = gram_ref.shape
    k = n // 3
    rows8 = 8
    tiles = n // rows8
    lane = lax.broadcasted_iota(jnp.int32, (rows8, lanes), 1)
    sub = lax.broadcasted_iota(jnp.int32, (rows8, lanes), 0)
    left = [gram_ref[i * rows8 : (i + 1) * rows8, :] for i in range(tiles)]
    right = [jnp.where(lane == sub + i * rows8, 1.0, 0.0).astype(F32) for i in range(tiles)]
    for step in range(n):
        j, r = divmod(step, rows8)
        row_left = left[j][r : r + 1, :]
        row_right = right[j][r : r + 1, :]
        pivot = row_left[:, step : step + 1]
        scale = 1.0 / pivot
        scaled_left = row_left * scale
        scaled_right = row_right * scale
        for i in range(j, tiles):
            factor = left[i][:, step : step + 1]
            if i == j:
                factor = jnp.where(sub[:, :1] > r, factor, 0.0)
            left[i] = left[i] - factor * scaled_left
            right[i] = right[i] - factor * scaled_right
        root = lax.rsqrt(pivot)
        upper[step : step + 1, :] = row_left * root
        inverse[step : step + 1, :] = row_right * root
    u11 = upper[:k, :]
    x = inverse[...]
    u = upper[...]
    u12, u13 = u[:k, k : 2 * k], u[:k, 2 * k : 3 * k]
    u22, u23 = u[k : 2 * k, k : 2 * k], u[k : 2 * k, 2 * k : 3 * k]
    u33 = u[2 * k : 3 * k, 2 * k : 3 * k]
    x11, x22 = x[:k, :k], x[k : 2 * k, k : 2 * k]
    fact_ref[0] = dot(x11, u22, NT, HIGHEST)
    fact_ref[1] = dot(x22, u33, NT, HIGHEST)
    coef_ref[0, :k] = dot(u12, x11, NT, HIGHEST)
    coef_ref[0, k:] = jnp.zeros((k, k), F32)
    v = dot(x11, u12, TN, HIGHEST)
    coef_ref[1, :k] = dot(u23 - dot(u22, v, NN, HIGHEST), x22, NT, HIGHEST)
    coef_ref[1, k:] = dot(u13 - dot(u12, v, NN, HIGHEST), x22, NT, HIGHEST)
    last = x[2 * k : 3 * k, : 3 * k]
    stack = jnp.concatenate([s_ref[0], y_ref[0], z_ref[0]], axis=0)
    next_ref[...] = dot(last, stack, NN, HIGHEST)


def moved(x, axis, target):
    size = lax.axis_size(axis)
    return lax.ppermute(x, axis, [(i, target(i) % size) for i in range(size)])


def shifted(x, axis, by):
    return moved(x, axis, lambda i: i + by)


def sum_of_ring(x, ring):
    first, second, third = ring(1), ring(2), ring(3)
    return (x + second) + (first + third)


def body(tiles, tile_row, tile_col, tile_round, tile_count, start_block):
    tiles = tiles[0, 0]
    meta = (tile_row[0, 0], tile_col[0, 0], tile_round[0, 0], tile_count[0])
    slots, edge = tiles.shape[0], tiles.shape[1]
    k = start_block.shape[0]
    members = lax.axis_size("rep")
    devices = lax.axis_size("rows")
    blocks = members
    offsets = [max(1, devices // 2**r) for r in range(1, ROUNDS + 1)]
    held_shape = (blocks, k, edge)
    smem = pl.BlockSpec(memory_space=pltpu.SMEM)
    vmem = pl.BlockSpec(memory_space=pltpu.VMEM)
    hbm = pl.BlockSpec(memory_space=pl.ANY)
    block_shape = jax.ShapeDtypeStruct(held_shape, F32)
    params = pltpu.CompilerParams(vmem_limit_bytes=VMEM_LIMIT)
    cost = pl.CostEstimate(
        flops=4 * slots * edge * edge * k, bytes_accessed=2 * slots * edge * edge, transcendentals=0
    )

    def scratch(sources, targets):
        return [
            pltpu.VMEM((slots, edge, edge), BF16),
            pltpu.VMEM((sources, 2 * k, edge), BF16),
            pltpu.VMEM((targets + 1, k, edge), F32),
            pltpu.SemaphoreType.DMA((slots // CHUNK,)),
        ]

    backward = pl.pallas_call(
        backward_kernel,
        out_shape=[block_shape] * (ROUNDS + 1),
        in_specs=[smem] * 4 + [hbm, vmem],
        out_specs=[vmem] * (ROUNDS + 1),
        scratch_shapes=scratch(blocks, (ROUNDS + 1) * blocks),
        compiler_params=params,
        cost_estimate=cost,
    )
    forward = pl.pallas_call(
        forward_kernel,
        out_shape=block_shape,
        in_specs=[smem] * 4 + [hbm] + [vmem] * (ROUNDS + 2),
        out_specs=vmem,
        scratch_shapes=scratch((ROUNDS + 1) * blocks, blocks),
        compiler_params=params,
        cost_estimate=cost,
    )

    def rep_sum(part):
        return sum_of_ring(part, lambda by: jnp.roll(shifted(part, "rep", by), by, axis=0))

    def apply(q):
        sources = [shifted(q, "rows", -offset) for offset in offsets]
        kept, *outgoing = backward(*meta, tiles, q)
        arrived = [shifted(x, "rows", offset) for x, offset in zip(outgoing, offsets)]
        part = forward(*meta, tiles, kept, q, *sources)
        for x in arrived:
            part = part + x
        return rep_sum(part)

    start = jnp.stack([start_block] + [shifted(start_block, "rep", by) for by in range(1, members)], 0)
    first = apply(start)
    second = apply(first)
    gram = pl.pallas_call(
        gram_kernel,
        out_shape=jax.ShapeDtypeStruct((3 * k, 4 * k), F32),
        in_specs=[vmem] * 3,
        out_specs=vmem,
        compiler_params=params,
    )(start, first, second)
    gram = gram + moved(gram, "rows", lambda i: i ^ 1)
    gram = sum_of_ring(gram, lambda by: shifted(gram, "rows", by * (devices // 4)))
    gram = gram + moved(gram, "rows", lambda i: i ^ 8)
    gram = sum_of_ring(gram, lambda by: moved(gram, "rows", lambda i: (i & ~7) | ((i + 2 * by) & 7)))
    result, coefficients, factors = pl.pallas_call(
        tail_kernel,
        out_shape=[
            jax.ShapeDtypeStruct((k, edge), F32),
            jax.ShapeDtypeStruct((2, 2 * k, k), F32),
            jax.ShapeDtypeStruct((2, k, k), F32),
        ],
        in_specs=[vmem] * 4,
        out_specs=[vmem] * 3,
        scratch_shapes=[pltpu.VMEM((3 * k, 4 * k), F32), pltpu.VMEM((3 * k, 4 * k), F32)],
        compiler_params=params,
    )(gram, start, first, second)
    return result, coefficients, factors


def solution(mesh):
    placed = (
        P("rows", "rep", None, None, None),
        P("rows", "rep", None),
        P("rows", "rep", None),
        P("rows", "rep", None),
        P("rows", "rep"),
        P(None, ("rows", "rep")),
    )
    return jax.shard_map(
        body,
        mesh=mesh,
        in_specs=placed,
        out_specs=(P(None, ("rows", "rep")), P(), P()),
        check_vma=False,
    )
```

time: 581 us -> 132 us (0.23)
  blocking collectives: 391 us -> 0 us
  waiting for transfers between devices: 90.2 us -> 47.4 us
  starting transfers between devices: 30.1 us -> 54.5 us
  matrix products: 24.2 us -> 0 us
  Pallas kernels: 0 us -> 22.1 us
  other arithmetic: 22.7 us -> 0.97 us
  between operations: 15.1 us -> 1.49 us
    psum x5 -> x0, blocking collectives: 379 us -> none  [the longest x2 152 us: body(): lax.psum(jnp.dot(basis_share, image_share.T, precision=highest), ('rows',...]
    psum x2 -> x0, waiting for transfers between devices: 87.4 us -> none  [body(): image_block = lax.psum(partial_value, 'rep')]
    ppermute x16 -> x33, waiting for transfers between devices: 2.71 us -> 47.4 us  [moved(): return lax.ppermute(x, axis, [(i, target(i) % size) for i in range(size)])]
    ppermute x16 -> x33, starting transfers between devices: 30 us -> 54.5 us  [moved(): return lax.ppermute(x, axis, [(i, target(i) % size) for i in range(size)])]
    dot_general x15 -> x0, matrix products: 23.2 us -> none  [the longest x2 7.01 us: body(): jnp.einsum('tkj,tij->tki', inputs, tile_mats, preferred_element_type=jnp....]
    pallas_call x0 -> x6, Pallas kernels: none -> 22.1 us  [the longest x1 9.48 us: body(): pl.pallas_call(tail_kernel, out_shape=[jax.ShapeDtypeStruct((k, edge), F3...]
    another operation x17 -> x1, other arithmetic: 21.3 us -> 0.77 us  [body(): jnp.stack([start_block] + [shifted(start_block, 'rep', by) for by in rang...]
    all_gather x1 -> x0, blocking collectives: 12 us -> none  [body(): basis_now = lax.all_gather(basis_now, 'rep', axis=1, tiled=True)]
  transfers between devices with their start and end apart: 18 -> 33, of which waited for: 4 -> 19; matrix products, arithmetic and copies ran while one was open for 3% -> 0% of each run, Pallas kernels for 0% -> 9%
where the time goes in v1:
time: 132 us; the launch traced here: 131 us
  starting transfers between devices  54.5 us (41%)
  waiting for transfers between devices  47.4 us (36%)
  Pallas kernels  22.1 us (17%)
  local copies, waits for them, and re-layouts  4.91 us (4%)
  between operations  1.49 us (1%)
    ppermute x33, starting transfers between devices, moved(): return lax.ppermute(x, axis, [(i, target(i) % size) for i in range(size)])  54.5 us
    ppermute x33, waiting for transfers between devices, moved(): return lax.ppermute(x, axis, [(i, target(i) % size) for i in range(size)])  47.4 us
    pallas_call x1, Pallas kernels, body(): pl.pallas_call(tail_kernel, out_shape=[jax.ShapeDtypeStruct((k, edge), F3...  9.48 us
    pallas_call x2, Pallas kernels, apply(): part = forward(*meta, tiles, kept, q, *sources)  6.73 us
    pallas_call x2, Pallas kernels, apply(): kept, *outgoing = backward(*meta, tiles, q)  5.47 us
    unnamed x8, local copies, waits for them, and re-layouts  4.15 us
  transfers between devices with their start and end apart: 33, of which 19 were waited for; matrix products, arithmetic and copies ran while one was open for 0% of the time, Pallas kernels for 9%

profile of v1, /device:TPU:32, one launch (start us, length us, event | category | flops | bytes accessed | tf_op | source)
XLA Modules:
  0.0 131.3 jit_solution(9870713342778545768)
XLA Ops:
  0.6 1.6 %collective-permute-start = (f32[32,256]{1,0:T(8,128)}, f32[32,256]{1,0:T(8,128)S(1)}, u32[]{:S(2)}, u32[]{:S(2)}) collective-permute-start(f32[32,256]{1,0:T(8,128)} %param.11), channel_id=1, source_target_pairs={{0,1},{1,2},{2,3},{3,0},{4,5},{5,6},{6,7},{7,4},{8,9},{9,10},{10,1... | collective-permute-start | bytes 98312 | tf_op jit(solution)/shard_map/ppermute | solution.py:148
  2.2 1.7 %collective-permute-start.2 = (f32[32,256]{1,0:T(8,128)}, f32[32,256]{1,0:T(8,128)S(1)}, u32[]{:S(2)}, u32[]{:S(2)}) collective-permute-start(f32[32,256]{1,0:T(8,128)} %param.11), channel_id=1, source_target_pairs={{0,3},{1,0},{2,1},{3,2},{4,7},{5,4},{6,5},{7,6},{8,11},{9,8},{10,9... | collective-permute-start | bytes 98312 | tf_op jit(solution)/shard_map/ppermute | solution.py:148
  3.9 1.8 %collective-permute-start.1 = (f32[32,256]{1,0:T(8,128)}, f32[32,256]{1,0:T(8,128)S(1)}, u32[]{:S(2)}, u32[]{:S(2)}) collective-permute-start(f32[32,256]{1,0:T(8,128)} %param.11), channel_id=1, source_target_pairs={{0,2},{1,3},{2,0},{3,1},{4,6},{5,7},{6,4},{7,5},{8,10},{9,11},{10,... | collective-permute-start | bytes 98312 | tf_op jit(solution)/shard_map/ppermute | solution.py:148
  6.3 3.2 %collective-permute-done.1 = f32[32,256]{1,0:T(8,128)S(1)} collective-permute-done((f32[32,256]{1,0:T(8,128)}, f32[32,256]{1,0:T(8,128)S(1)}, u32[]{:S(2)}, u32[]{:S(2)}) %collective-permute-start.1) | collective-permute-done | bytes 32800 | tf_op jit(solution)/shard_map/ppermute | solution.py:148
  10.3 7.9 %collective-permute-start.6 = (f32[4,32,256]{2,1,0:T(8,128)S(1)}, f32[4,32,256]{2,1,0:T(8,128)S(1)}, u32[]{:S(2)}, u32[]{:S(2)}) collective-permute-start(f32[4,32,256]{2,1,0:T(8,128)S(1)} %pad_maximum_fusion.q_ref.rest_0_.s_ref), channel_id=1, source_target_pairs={{0,240},{4,244},{8,248},{12,252},{16,0},{20,4},{24,8},{28,12},{32,... | collective-permute-start | bytes 393224 | tf_op jit(solution)/shard_map/ppermute | solution.py:148
  21.5 2.2 %copy-done = bf16[1,1,32,256,256]{4,3,2,1,0:T(8,128)(2,1)S(1)} copy-done((bf16[1,1,32,256,256]{4,3,2,1,0:T(8,128)(2,1)S(1)}, bf16[1,1,32,256,256]{4,3,2,1,0:T(8,128)(2,1)}, u32[]{:S(2)}) %copy-start) | copy-done | bytes 4194328
  25.7 2.7 %shard_map.85 = (f32[4,32,256]{2,1,0:T(8,128)S(1)}, f32[4,32,256]{2,1,0:T(8,128)S(1)}, f32[4,32,256]{2,1,0:T(8,128)S(1)}, f32[4,32,256]{2,1,0:T(8,128)S(1)}, f32[4,32,256]{2,1,0:T(8,128)S(1)}) custom-call(s32[32]{0:T(128)S(1)} %bitcast.17, s32[32]{0:T(128)S(1)} %bitcast.21, s32[32]{0:T(128)S(1)} %bitcast.25, s32[1]{0:T(128)} %bitcast.9.count, ...), custom_call_target="tpu_custom_call" | custom-call | flops 268435456 | bytes 4194304 | tf_op jit(solution)/shard_map/pallas_call | solution.py:211
  28.4 3.3 %collective-permute-start.7 = (f32[4,32,256]{2,1,0:T(8,128)S(1)}, f32[4,32,256]{2,1,0:T(8,128)S(1)}, u32[]{:S(2)}, u32[]{:S(2)}) collective-permute-start(f32[4,32,256]{2,1,0:T(8,128)S(1)} %get-tuple-element.14), channel_id=1, source_target_pairs={{0,128},{4,132},{8,136},{12,140},{16,144},{20,148},{24,152},{28,15... | collective-permute-start | bytes 393224 | tf_op jit(solution)/shard_map/ppermute | solution.py:148
  33.0 4.5 %collective-permute-start.9 = (f32[4,32,256]{2,1,0:T(8,128)S(1)}, f32[4,32,256]{2,1,0:T(8,128)S(1)}, u32[]{:S(2)}, u32[]{:S(2)}) collective-permute-start(f32[4,32,256]{2,1,0:T(8,128)S(1)} %get-tuple-element.16), channel_id=1, source_target_pairs={{0,32},{4,36},{8,40},{12,44},{16,48},{20,52},{24,56},{28,60},{32,6... | collective-permute-start | bytes 393224 | tf_op jit(solution)/shard_map/ppermute | solution.py:148
  37.5 3.4 %shard_map.86 = f32[4,32,256]{2,1,0:T(8,128)S(1)} custom-call(s32[32]{0:T(128)S(1)} %bitcast.18, s32[32]{0:T(128)S(1)} %bitcast.22, s32[32]{0:T(128)S(1)} %bitcast.26, s32[1]{0:T(128)} %bitcast.10.count, bf16[32,256,256]{2,1,0:T(8,128)(2,1)S(1)} %bitcast.14, f32[4,32,256]{2,1,0:T(8,128)S(1)} %get-tuple-element.13.kept_ref, ...), custom_call_target="tpu_custom_call" | custom-call | flops 268435456 | bytes 4194304 | tf_op jit(solution)/shard_map/pallas_call | solution.py:213
  40.9 3.1 %collective-permute-done.9 = f32[4,32,256]{2,1,0:T(8,128)S(1)} collective-permute-done((f32[4,32,256]{2,1,0:T(8,128)S(1)}, f32[4,32,256]{2,1,0:T(8,128)S(1)}, u32[]{:S(2)}, u32[]{:S(2)}) %collective-permute-start.9) | collective-permute-done | bytes 131104 | tf_op jit(solution)/shard_map/ppermute | solution.py:148
  44.0 5.6 %collective-permute-done.10 = f32[4,32,256]{2,1,0:T(8,128)S(1)} collective-permute-done((f32[4,32,256]{2,1,0:T(8,128)S(1)}, f32[4,32,256]{2,1,0:T(8,128)S(1)}, u32[]{:S(2)}, u32[]{:S(2)}) %collective-permute-start.10) | collective-permute-done | bytes 131104 | tf_op jit(solution)/shard_map/ppermute | solution.py:148
  49.6 2.0 %collective-permute-start.13 = (f32[4,32,256]{2,1,0:T(8,128)S(1)}, f32[4,32,256]{2,1,0:T(8,128)S(1)}, u32[]{:S(2)}, u32[]{:S(2)}) collective-permute-start(f32[4,32,256]{2,1,0:T(8,128)S(1)} %add_add_fusion.1), channel_id=1, source_target_pairs={{0,3},{1,0},{2,1},{3,2},{4,7},{5,4},{6,5},{7,6},{8,11},{9,8},{10,9... | collective-permute-start | bytes 393224 | tf_op jit(solution)/shard_map/ppermute | solution.py:148
  51.8 2.1 %collective-permute-start.11 = (f32[4,32,256]{2,1,0:T(8,128)S(1)}, f32[4,32,256]{2,1,0:T(8,128)S(1)}, u32[]{:S(2)}, u32[]{:S(2)}) collective-permute-start(f32[4,32,256]{2,1,0:T(8,128)S(1)} %add_add_fusion.1), channel_id=1, source_target_pairs={{0,2},{1,3},{2,0},{3,1},{4,6},{5,7},{6,4},{7,5},{8,10},{9,11},{10,... | collective-permute-start | bytes 393224 | tf_op jit(solution)/shard_map/ppermute | solution.py:148
  54.7 5.4 %collective-permute-done.12 = f32[4,32,256]{2,1,0:T(8,128)S(1)} collective-permute-done((f32[4,32,256]{2,1,0:T(8,128)S(1)}, f32[4,32,256]{2,1,0:T(8,128)S(1)}, u32[]{:S(2)}, u32[]{:S(2)}) %collective-permute-start.12) | collective-permute-done | bytes 131104 | tf_op jit(solution)/shard_map/ppermute | solution.py:148
  60.6 3.2 %collective-permute-start.16 = (f32[4,32,256]{2,1,0:T(8,128)S(1)}, f32[4,32,256]{2,1,0:T(8,128)S(1)}, u32[]{:S(2)}, u32[]{:S(2)}) collective-permute-start(f32[4,32,256]{2,1,0:T(8,128)S(1)} %fusion.q_ref.rest_0_.y_ref), channel_id=1, source_target_pairs={{0,224},{4,228},{8,232},{12,236},{16,240},{20,244},{24,248},{28,25... | collective-permute-start | bytes 393224 | tf_op jit(solution)/shard_map/ppermute | solution.py:148
  63.9 2.2 %collective-permute-start.14 = (f32[4,32,256]{2,1,0:T(8,128)S(1)}, f32[4,32,256]{2,1,0:T(8,128)S(1)}, u32[]{:S(2)}, u32[]{:S(2)}) collective-permute-start(f32[4,32,256]{2,1,0:T(8,128)S(1)} %fusion.q_ref.rest_0_.y_ref), channel_id=1, source_target_pairs={{0,128},{4,132},{8,136},{12,140},{16,144},{20,148},{24,152},{28,15... | collective-permute-start | bytes 393224 | tf_op jit(solution)/shard_map/ppermute | solution.py:148
  66.1 2.7 %shard_map.87 = (f32[4,32,256]{2,1,0:T(8,128)S(1)}, f32[4,32,256]{2,1,0:T(8,128)S(1)}, f32[4,32,256]{2,1,0:T(8,128)S(1)}, f32[4,32,256]{2,1,0:T(8,128)S(1)}, f32[4,32,256]{2,1,0:T(8,128)S(1)}) custom-call(s32[32]{0:T(128)S(1)} %bitcast.19, s32[32]{0:T(128)S(1)} %bitcast.23, s32[32]{0:T(128)S(1)} %bitcast.27, s32[1]{0:T(128)} %bitcast.11.count, ...), custom_call_target="tpu_custom_call" | custom-call | flops 268435456 | bytes 4194304 | tf_op jit(solution)/shard_map/pallas_call | solution.py:211
  70.2 2.0 %collective-permute-start.19 = (f32[4,32,256]{2,1,0:T(8,128)S(1)}, f32[4,32,256]{2,1,0:T(8,128)S(1)}, u32[]{:S(2)}, u32[]{:S(2)}) collective-permute-start(f32[4,32,256]{2,1,0:T(8,128)S(1)} %get-tuple-element.20), channel_id=1, source_target_pairs={{0,64},{4,68},{8,72},{12,76},{16,80},{20,84},{24,88},{28,92},{32,9... | collective-permute-start | bytes 393224 | tf_op jit(solution)/shard_map/ppermute | solution.py:148
  72.3 2.7 %collective-permute-start.20 = (f32[4,32,256]{2,1,0:T(8,128)S(1)}, f32[4,32,256]{2,1,0:T(8,128)S(1)}, u32[]{:S(2)}, u32[]{:S(2)}) collective-permute-start(f32[4,32,256]{2,1,0:T(8,128)S(1)} %get-tuple-element.21), channel_id=1, source_target_pairs={{0,32},{4,36},{8,40},{12,44},{16,48},{20,52},{24,56},{28,60},{32,6... | collective-permute-start | bytes 393224 | tf_op jit(solution)/shard_map/ppermute | solution.py:148
  75.0 2.6 %collective-permute-start.21 = (f32[4,32,256]{2,1,0:T(8,128)S(1)}, f32[4,32,256]{2,1,0:T(8,128)S(1)}, u32[]{:S(2)}, u32[]{:S(2)}) collective-permute-start(f32[4,32,256]{2,1,0:T(8,128)S(1)} %get-tuple-element.22), channel_id=1, source_target_pairs={{0,16},{4,20},{8,24},{12,28},{16,32},{20,36},{24,40},{28,44},{32,4... | collective-permute-start | bytes 393224 | tf_op jit(solution)/shard_map/ppermute | solution.py:148
  77.6 3.4 %shard_map.88 = f32[4,32,256]{2,1,0:T(8,128)S(1)} custom-call(s32[32]{0:T(128)S(1)} %bitcast.20, s32[32]{0:T(128)S(1)} %bitcast.24, s32[32]{0:T(128)S(1)} %bitcast.28, s32[1]{0:T(128)} %bitcast.12.count, bf16[32,256,256]{2,1,0:T(8,128)(2,1)S(1)} %bitcast.16, f32[4,32,256]{2,1,0:T(8,128)S(1)} %get-tuple-element.18.kept_ref, ...), custom_call_target="tpu_custom_call" | custom-call | flops 268435456 | bytes 4194304 | tf_op jit(solution)/shard_map/pallas_call | solution.py:213
  81.0 3.7 %collective-permute-done.20 = f32[4,32,256]{2,1,0:T(8,128)S(1)} collective-permute-done((f32[4,32,256]{2,1,0:T(8,128)S(1)}, f32[4,32,256]{2,1,0:T(8,128)S(1)}, u32[]{:S(2)}, u32[]{:S(2)}) %collective-permute-start.20) | collective-permute-done | bytes 131104 | tf_op jit(solution)/shard_map/ppermute | solution.py:148
  84.7 2.7 %collective-permute-done.21 = f32[4,32,256]{2,1,0:T(8,128)S(1)} collective-permute-done((f32[4,32,256]{2,1,0:T(8,128)S(1)}, f32[4,32,256]{2,1,0:T(8,128)S(1)}, u32[]{:S(2)}, u32[]{:S(2)}) %collective-permute-start.21) | collective-permute-done | bytes 131104 | tf_op jit(solution)/shard_map/ppermute | solution.py:148
  90.3 2.1 %collective-permute-done.24 = f32[4,32,256]{2,1,0:T(8,128)S(1)} collective-permute-done((f32[4,32,256]{2,1,0:T(8,128)S(1)}, f32[4,32,256]{2,1,0:T(8,128)S(1)}, u32[]{:S(2)}, u32[]{:S(2)}) %collective-permute-start.24) | collective-permute-done | bytes 131104 | tf_op jit(solution)/shard_map/ppermute | solution.py:148
  92.5 3.9 %collective-permute-done.23 = f32[4,32,256]{2,1,0:T(8,128)S(1)} collective-permute-done((f32[4,32,256]{2,1,0:T(8,128)S(1)}, f32[4,32,256]{2,1,0:T(8,128)S(1)}, u32[]{:S(2)}, u32[]{:S(2)}) %collective-permute-start.23) | collective-permute-done | bytes 131104 | tf_op jit(solution)/shard_map/ppermute | solution.py:148
  102.4 2.3 %collective-permute-done.27 = f32[96,128]{1,0:T(8,128)S(1)} collective-permute-done((f32[96,128]{1,0:T(8,128)S(1)}, f32[96,128]{1,0:T(8,128)S(1)}, u32[]{:S(2)}, u32[]{:S(2)}) %collective-permute-start.27) | collective-permute-done | bytes 49184 | tf_op jit(solution)/shard_map/ppermute | solution.py:148
  106.0 1.6 %collective-permute-start.29 = (f32[96,128]{1,0:T(8,128)S(1)}, f32[96,128]{1,0:T(8,128)S(1)}, u32[]{:S(2)}, u32[]{:S(2)}) collective-permute-start(f32[96,128]{1,0:T(8,128)S(1)} %add_add_fusion.3), channel_id=1, source_target_pairs={{0,32},{4,36},{8,40},{12,44},{16,48},{20,52},{24,56},{28,60},{32,0... | collective-permute-start | bytes 147464 | tf_op jit(solution)/shard_map/ppermute | solution.py:148
  107.6 6.5 %collective-permute-done.29 = f32[96,128]{1,0:T(8,128)S(1)} collective-permute-done((f32[96,128]{1,0:T(8,128)S(1)}, f32[96,128]{1,0:T(8,128)S(1)}, u32[]{:S(2)}, u32[]{:S(2)}) %collective-permute-start.29) | collective-permute-done | bytes 49184 | tf_op jit(solution)/shard_map/ppermute | solution.py:148
  114.1 2.0 %collective-permute-start.31 = (f32[96,128]{1,0:T(8,128)S(1)}, f32[96,128]{1,0:T(8,128)S(1)}, u32[]{:S(2)}, u32[]{:S(2)}) collective-permute-start(f32[96,128]{1,0:T(8,128)S(1)} %add.84), channel_id=1, source_target_pairs={{0,8},{4,12},{8,16},{12,20},{16,24},{20,28},{24,0},{28,4},{32,40},... | collective-permute-start | bytes 147464 | tf_op jit(solution)/shard_map/ppermute | solution.py:148
  118.3 2.8 %collective-permute-done.30 = f32[96,128]{1,0:T(8,128)S(1)} collective-permute-done((f32[96,128]{1,0:T(8,128)S(1)}, f32[96,128]{1,0:T(8,128)S(1)}, u32[]{:S(2)}, u32[]{:S(2)}) %collective-permute-start.30) | collective-permute-done | bytes 49184 | tf_op jit(solution)/shard_map/ppermute | solution.py:148
  121.2 9.5 %shard_map.90 = (f32[32,256]{1,0:T(8,128)}, f32[2,64,32]{2,1,0:T(8,128)S(1)}, f32[2,32,32]{2,1,0:T(8,128)}) custom-call(f32[96,128]{1,0:T(8,128)S(1)} %add_add_fusion.2.gram_ref, f32[4,32,256]{2,1,0:T(8,128)S(1)} %pad_maximum_fusion.q_ref.rest_0_.s_ref, f32[4,32,256]{2,1,0:T(8,128)S(1)} %fusion.q_ref.rest_0_.y_ref, f32[4,32,256]{2,1,0:T(8,128)S(1)} %fusion.1.z_ref), custom_call_target="tpu_custom_call" | custom-call | tf_op jit(solution)/shard_map/pallas_call | solution.py:232
  (68 shorter events, 23.2 us)
Async XLA Ops:
  0.6 5.4 %collective-permute-start = (f32[32,256]{1,0:T(8,128)}, f32[32,256]{1,0:T(8,128)S(1)}, u32[]{:S(2)}, u32[]{:S(2)}) collective-permute-start(f32[32,256]{1,0:T(8,128)} %param.11), channel_id=1, source_target_pairs={{0,1},{1,2},{2,3},{3,0},{4,5},{5,6},{6,7},{7,4},{8,9},{9,10},{10,1... | collective-permute-start | bytes 98312 | tf_op jit(solution)/shard_map/ppermute | solution.py:148
  2.2 4.1 %collective-permute-start.2 = (f32[32,256]{1,0:T(8,128)}, f32[32,256]{1,0:T(8,128)S(1)}, u32[]{:S(2)}, u32[]{:S(2)}) collective-permute-start(f32[32,256]{1,0:T(8,128)} %param.11), channel_id=1, source_target_pairs={{0,3},{1,0},{2,1},{3,2},{4,7},{5,4},{6,5},{7,6},{8,11},{9,8},{10,9... | collective-permute-start | bytes 98312 | tf_op jit(solution)/shard_map/ppermute | solution.py:148
  3.9 5.6 %collective-permute-start.1 = (f32[32,256]{1,0:T(8,128)}, f32[32,256]{1,0:T(8,128)S(1)}, u32[]{:S(2)}, u32[]{:S(2)}) collective-permute-start(f32[32,256]{1,0:T(8,128)} %param.11), channel_id=1, source_target_pairs={{0,2},{1,3},{2,0},{3,1},{4,6},{5,7},{6,4},{7,5},{8,10},{9,11},{10,... | collective-permute-start | bytes 98312 | tf_op jit(solution)/shard_map/ppermute | solution.py:148
  10.3 21.4 %collective-permute-start.6 = (f32[4,32,256]{2,1,0:T(8,128)S(1)}, f32[4,32,256]{2,1,0:T(8,128)S(1)}, u32[]{:S(2)}, u32[]{:S(2)}) collective-permute-start(f32[4,32,256]{2,1,0:T(8,128)S(1)} %pad_maximum_fusion.q_ref.rest_0_.s_ref), channel_id=1, source_target_pairs={{0,240},{4,244},{8,248},{12,252},{16,0},{20,4},{24,8},{28,12},{32,... | collective-permute-start | bytes 393224 | tf_op jit(solution)/shard_map/ppermute | solution.py:148
  18.3 14.7 %collective-permute-start.5 = (f32[4,32,256]{2,1,0:T(8,128)S(1)}, f32[4,32,256]{2,1,0:T(8,128)S(1)}, u32[]{:S(2)}, u32[]{:S(2)}) collective-permute-start(f32[4,32,256]{2,1,0:T(8,128)S(1)} %pad_maximum_fusion.q_ref.rest_0_.s_ref), channel_id=1, source_target_pairs={{0,224},{4,228},{8,232},{12,236},{16,240},{20,244},{24,248},{28,25... | collective-permute-start | bytes 393224 | tf_op jit(solution)/shard_map/ppermute | solution.py:148
  19.7 17.8 %collective-permute-start.4 = (f32[4,32,256]{2,1,0:T(8,128)S(1)}, f32[4,32,256]{2,1,0:T(8,128)S(1)}, u32[]{:S(2)}, u32[]{:S(2)}) collective-permute-start(f32[4,32,256]{2,1,0:T(8,128)S(1)} %pad_maximum_fusion.q_ref.rest_0_.s_ref), channel_id=1, source_target_pairs={{0,192},{4,196},{8,200},{12,204},{16,208},{20,212},{24,216},{28,22... | collective-permute-start | bytes 393224 | tf_op jit(solution)/shard_map/ppermute | solution.py:148
  21.1 16.4 %collective-permute-start.3 = (f32[4,32,256]{2,1,0:T(8,128)S(1)}, f32[4,32,256]{2,1,0:T(8,128)S(1)}, u32[]{:S(2)}, u32[]{:S(2)}) collective-permute-start(f32[4,32,256]{2,1,0:T(8,128)S(1)} %pad_maximum_fusion.q_ref.rest_0_.s_ref), channel_id=1, source_target_pairs={{0,128},{4,132},{8,136},{12,140},{16,144},{20,148},{24,152},{28,15... | collective-permute-start | bytes 393224 | tf_op jit(solution)/shard_map/ppermute | solution.py:148
  28.4 12.5 %collective-permute-start.7 = (f32[4,32,256]{2,1,0:T(8,128)S(1)}, f32[4,32,256]{2,1,0:T(8,128)S(1)}, u32[]{:S(2)}, u32[]{:S(2)}) collective-permute-start(f32[4,32,256]{2,1,0:T(8,128)S(1)} %get-tuple-element.14), channel_id=1, source_target_pairs={{0,128},{4,132},{8,136},{12,140},{16,144},{20,148},{24,152},{28,15... | collective-permute-start | bytes 393224 | tf_op jit(solution)/shard_map/ppermute | solution.py:148
  31.7 9.2 %collective-permute-start.8 = (f32[4,32,256]{2,1,0:T(8,128)S(1)}, f32[4,32,256]{2,1,0:T(8,128)S(1)}, u32[]{:S(2)}, u32[]{:S(2)}) collective-permute-start(f32[4,32,256]{2,1,0:T(8,128)S(1)} %get-tuple-element.15), channel_id=1, source_target_pairs={{0,64},{4,68},{8,72},{12,76},{16,80},{20,84},{24,88},{28,92},{32,9... | collective-permute-start | bytes 393224 | tf_op jit(solution)/shard_map/ppermute | solution.py:148
  33.0 11.0 %collective-permute-start.9 = (f32[4,32,256]{2,1,0:T(8,128)S(1)}, f32[4,32,256]{2,1,0:T(8,128)S(1)}, u32[]{:S(2)}, u32[]{:S(2)}) collective-permute-start(f32[4,32,256]{2,1,0:T(8,128)S(1)} %get-tuple-element.16), channel_id=1, source_target_pairs={{0,32},{4,36},{8,40},{12,44},{16,48},{20,52},{24,56},{28,60},{32,6... | collective-permute-start | bytes 393224 | tf_op jit(solution)/shard_map/ppermute | solution.py:148
  37.5 12.1 %collective-permute-start.10 = (f32[4,32,256]{2,1,0:T(8,128)S(1)}, f32[4,32,256]{2,1,0:T(8,128)S(1)}, u32[]{:S(2)}, u32[]{:S(2)}) collective-permute-start(f32[4,32,256]{2,1,0:T(8,128)S(1)} %get-tuple-element.17), channel_id=1, source_target_pairs={{0,16},{4,20},{8,24},{12,28},{16,32},{20,36},{24,40},{28,44},{32,4... | collective-permute-start | bytes 393224 | tf_op jit(solution)/shard_map/ppermute | solution.py:148
  49.6 5.0 %collective-permute-start.13 = (f32[4,32,256]{2,1,0:T(8,128)S(1)}, f32[4,32,256]{2,1,0:T(8,128)S(1)}, u32[]{:S(2)}, u32[]{:S(2)}) collective-permute-start(f32[4,32,256]{2,1,0:T(8,128)S(1)} %add_add_fusion.1), channel_id=1, source_target_pairs={{0,3},{1,0},{2,1},{3,2},{4,7},{5,4},{6,5},{7,6},{8,11},{9,8},{10,9... | collective-permute-start | bytes 393224 | tf_op jit(solution)/shard_map/ppermute | solution.py:148
  51.7 8.5 %collective-permute-start.12 = (f32[4,32,256]{2,1,0:T(8,128)S(1)}, f32[4,32,256]{2,1,0:T(8,128)S(1)}, u32[]{:S(2)}, u32[]{:S(2)}) collective-permute-start(f32[4,32,256]{2,1,0:T(8,128)S(1)} %add_add_fusion.1), channel_id=1, source_target_pairs={{0,1},{1,2},{2,3},{3,0},{4,5},{5,6},{6,7},{7,4},{8,9},{9,10},{10,1... | collective-permute-start | bytes 393224 | tf_op jit(solution)/shard_map/ppermute | solution.py:148
  51.8 8.4 %collective-permute-start.11 = (f32[4,32,256]{2,1,0:T(8,128)S(1)}, f32[4,32,256]{2,1,0:T(8,128)S(1)}, u32[]{:S(2)}, u32[]{:S(2)}) collective-permute-start(f32[4,32,256]{2,1,0:T(8,128)S(1)} %add_add_fusion.1), channel_id=1, source_target_pairs={{0,2},{1,3},{2,0},{3,1},{4,6},{5,7},{6,4},{7,5},{8,10},{9,11},{10,... | collective-permute-start | bytes 393224 | tf_op jit(solution)/shard_map/ppermute | solution.py:148
  60.2 10.0 %collective-permute-start.17 = (f32[4,32,256]{2,1,0:T(8,128)S(1)}, f32[4,32,256]{2,1,0:T(8,128)S(1)}, u32[]{:S(2)}, u32[]{:S(2)}) collective-permute-start(f32[4,32,256]{2,1,0:T(8,128)S(1)} %fusion.q_ref.rest_0_.y_ref), channel_id=1, source_target_pairs={{0,240},{4,244},{8,248},{12,252},{16,0},{20,4},{24,8},{28,12},{32,... | collective-permute-start | bytes 393224 | tf_op jit(solution)/shard_map/ppermute | solution.py:148
  60.6 11.6 %collective-permute-start.16 = (f32[4,32,256]{2,1,0:T(8,128)S(1)}, f32[4,32,256]{2,1,0:T(8,128)S(1)}, u32[]{:S(2)}, u32[]{:S(2)}) collective-permute-start(f32[4,32,256]{2,1,0:T(8,128)S(1)} %fusion.q_ref.rest_0_.y_ref), channel_id=1, source_target_pairs={{0,224},{4,228},{8,232},{12,236},{16,240},{20,244},{24,248},{28,25... | collective-permute-start | bytes 393224 | tf_op jit(solution)/shard_map/ppermute | solution.py:148
  63.9 11.1 %collective-permute-start.15 = (f32[4,32,256]{2,1,0:T(8,128)S(1)}, f32[4,32,256]{2,1,0:T(8,128)S(1)}, u32[]{:S(2)}, u32[]{:S(2)}) collective-permute-start(f32[4,32,256]{2,1,0:T(8,128)S(1)} %fusion.q_ref.rest_0_.y_ref), channel_id=1, source_target_pairs={{0,192},{4,196},{8,200},{12,204},{16,208},{20,212},{24,216},{28,22... | collective-permute-start | bytes 393224 | tf_op jit(solution)/shard_map/ppermute | solution.py:148
  63.9 13.7 %collective-permute-start.14 = (f32[4,32,256]{2,1,0:T(8,128)S(1)}, f32[4,32,256]{2,1,0:T(8,128)S(1)}, u32[]{:S(2)}, u32[]{:S(2)}) collective-permute-start(f32[4,32,256]{2,1,0:T(8,128)S(1)} %fusion.q_ref.rest_0_.y_ref), channel_id=1, source_target_pairs={{0,128},{4,132},{8,136},{12,140},{16,144},{20,148},{24,152},{28,15... | collective-permute-start | bytes 393224 | tf_op jit(solution)/shard_map/ppermute | solution.py:148
  68.8 12.2 %collective-permute-start.18 = (f32[4,32,256]{2,1,0:T(8,128)S(1)}, f32[4,32,256]{2,1,0:T(8,128)S(1)}, u32[]{:S(2)}, u32[]{:S(2)}) collective-permute-start(f32[4,32,256]{2,1,0:T(8,128)S(1)} %get-tuple-element.19), channel_id=1, source_target_pairs={{0,128},{4,132},{8,136},{12,140},{16,144},{20,148},{24,152},{28,15... | collective-permute-start | bytes 393224 | tf_op jit(solution)/shard_map/ppermute | solution.py:148
  70.2 10.8 %collective-permute-start.19 = (f32[4,32,256]{2,1,0:T(8,128)S(1)}, f32[4,32,256]{2,1,0:T(8,128)S(1)}, u32[]{:S(2)}, u32[]{:S(2)}) collective-permute-start(f32[4,32,256]{2,1,0:T(8,128)S(1)} %get-tuple-element.20), channel_id=1, source_target_pairs={{0,64},{4,68},{8,72},{12,76},{16,80},{20,84},{24,88},{28,92},{32,9... | collective-permute-start | bytes 393224 | tf_op jit(solution)/shard_map/ppermute | solution.py:148
  72.3 12.4 %collective-permute-start.20 = (f32[4,32,256]{2,1,0:T(8,128)S(1)}, f32[4,32,256]{2,1,0:T(8,128)S(1)}, u32[]{:S(2)}, u32[]{:S(2)}) collective-permute-start(f32[4,32,256]{2,1,0:T(8,128)S(1)} %get-tuple-element.21), channel_id=1, source_target_pairs={{0,32},{4,36},{8,40},{12,44},{16,48},{20,52},{24,56},{28,60},{32,6... | collective-permute-start | bytes 393224 | tf_op jit(solution)/shard_map/ppermute | solution.py:148
  75.0 12.4 %collective-permute-start.21 = (f32[4,32,256]{2,1,0:T(8,128)S(1)}, f32[4,32,256]{2,1,0:T(8,128)S(1)}, u32[]{:S(2)}, u32[]{:S(2)}) collective-permute-start(f32[4,32,256]{2,1,0:T(8,128)S(1)} %get-tuple-element.22), channel_id=1, source_target_pairs={{0,16},{4,20},{8,24},{12,28},{16,32},{20,36},{24,40},{28,44},{32,4... | collective-permute-start | bytes 393224 | tf_op jit(solution)/shard_map/ppermute | solution.py:148
  87.4 5.0 %collective-permute-start.24 = (f32[4,32,256]{2,1,0:T(8,128)S(1)}, f32[4,32,256]{2,1,0:T(8,128)S(1)}, u32[]{:S(2)}, u32[]{:S(2)}) collective-permute-start(f32[4,32,256]{2,1,0:T(8,128)S(1)} %add_add_fusion), channel_id=1, source_target_pairs={{0,3},{1,0},{2,1},{3,2},{4,7},{5,4},{6,5},{7,6},{8,11},{9,8},{10,9... | collective-permute-start | bytes 393224 | tf_op jit(solution)/shard_map/ppermute | solution.py:148
  88.8 7.6 %collective-permute-start.23 = (f32[4,32,256]{2,1,0:T(8,128)S(1)}, f32[4,32,256]{2,1,0:T(8,128)S(1)}, u32[]{:S(2)}, u32[]{:S(2)}) collective-permute-start(f32[4,32,256]{2,1,0:T(8,128)S(1)} %add_add_fusion), channel_id=1, source_target_pairs={{0,1},{1,2},{2,3},{3,0},{4,5},{5,6},{6,7},{7,4},{8,9},{9,10},{10,1... | collective-permute-start | bytes 393224 | tf_op jit(solution)/shard_map/ppermute | solution.py:148
  89.5 6.9 %collective-permute-start.22 = (f32[4,32,256]{2,1,0:T(8,128)S(1)}, f32[4,32,256]{2,1,0:T(8,128)S(1)}, u32[]{:S(2)}, u32[]{:S(2)}) collective-permute-start(f32[4,32,256]{2,1,0:T(8,128)S(1)} %add_add_fusion), channel_id=1, source_target_pairs={{0,2},{1,3},{2,0},{3,1},{4,6},{5,7},{6,4},{7,5},{8,10},{9,11},{10,... | collective-permute-start | bytes 393224 | tf_op jit(solution)/shard_map/ppermute | solution.py:148
  98.2 4.2 %collective-permute-start.28 = (f32[96,128]{1,0:T(8,128)S(1)}, f32[96,128]{1,0:T(8,128)S(1)}, u32[]{:S(2)}, u32[]{:S(2)}) collective-permute-start(f32[96,128]{1,0:T(8,128)S(1)} %add.80), channel_id=1, source_target_pairs={{0,192},{4,196},{8,200},{12,204},{16,208},{20,212},{24,216},{28,22... | collective-permute-start | bytes 147464 | tf_op jit(solution)/shard_map/ppermute | solution.py:148
  98.9 5.8 %collective-permute-start.27 = (f32[96,128]{1,0:T(8,128)S(1)}, f32[96,128]{1,0:T(8,128)S(1)}, u32[]{:S(2)}, u32[]{:S(2)}) collective-permute-start(f32[96,128]{1,0:T(8,128)S(1)} %add.80), channel_id=1, source_target_pairs={{0,64},{4,68},{8,72},{12,76},{16,80},{20,84},{24,88},{28,92},{32,9... | collective-permute-start | bytes 147464 | tf_op jit(solution)/shard_map/ppermute | solution.py:148
  100.3 5.6 %collective-permute-start.26 = (f32[96,128]{1,0:T(8,128)S(1)}, f32[96,128]{1,0:T(8,128)S(1)}, u32[]{:S(2)}, u32[]{:S(2)}) collective-permute-start(f32[96,128]{1,0:T(8,128)S(1)} %add.80), channel_id=1, source_target_pairs={{0,128},{4,132},{8,136},{12,140},{16,144},{20,148},{24,152},{28,15... | collective-permute-start | bytes 147464 | tf_op jit(solution)/shard_map/ppermute | solution.py:148
  106.0 8.1 %collective-permute-start.29 = (f32[96,128]{1,0:T(8,128)S(1)}, f32[96,128]{1,0:T(8,128)S(1)}, u32[]{:S(2)}, u32[]{:S(2)}) collective-permute-start(f32[96,128]{1,0:T(8,128)S(1)} %add_add_fusion.3), channel_id=1, source_target_pairs={{0,32},{4,36},{8,40},{12,44},{16,48},{20,52},{24,56},{28,60},{32,0... | collective-permute-start | bytes 147464 | tf_op jit(solution)/shard_map/ppermute | solution.py:148
  114.0 4.2 %collective-permute-start.32 = (f32[96,128]{1,0:T(8,128)S(1)}, f32[96,128]{1,0:T(8,128)S(1)}, u32[]{:S(2)}, u32[]{:S(2)}) collective-permute-start(f32[96,128]{1,0:T(8,128)S(1)} %add.84), channel_id=1, source_target_pairs={{0,24},{4,28},{8,0},{12,4},{16,8},{20,12},{24,16},{28,20},{32,56},... | collective-permute-start | bytes 147464 | tf_op jit(solution)/shard_map/ppermute | solution.py:148
  114.1 4.2 %collective-permute-start.31 = (f32[96,128]{1,0:T(8,128)S(1)}, f32[96,128]{1,0:T(8,128)S(1)}, u32[]{:S(2)}, u32[]{:S(2)}) collective-permute-start(f32[96,128]{1,0:T(8,128)S(1)} %add.84), channel_id=1, source_target_pairs={{0,8},{4,12},{8,16},{12,20},{16,24},{20,28},{24,0},{28,4},{32,40},... | collective-permute-start | bytes 147464 | tf_op jit(solution)/shard_map/ppermute | solution.py:148
  116.1 5.0 %collective-permute-start.30 = (f32[96,128]{1,0:T(8,128)S(1)}, f32[96,128]{1,0:T(8,128)S(1)}, u32[]{:S(2)}, u32[]{:S(2)}) collective-permute-start(f32[96,128]{1,0:T(8,128)S(1)} %add.84), channel_id=1, source_target_pairs={{0,16},{4,20},{8,24},{12,28},{16,0},{20,4},{24,8},{28,12},{32,48},... | collective-permute-start | bytes 147464 | tf_op jit(solution)/shard_map/ppermute | solution.py:148
  (5 other events, 5.5 us)

commit v2 on v1

v2 whole, which is shorter than its diff:
```python
import functools

import jax
import jax.numpy as jnp
from jax import lax
from jax.experimental import pallas as pl
from jax.experimental.pallas import tpu as pltpu
from jax.sharding import PartitionSpec as P

ROUNDS = 4
F32 = jnp.float32
BF16 = jnp.bfloat16
HIGHEST = lax.Precision.HIGHEST
VMEM_LIMIT = 40 * 1024 * 1024


def dot(a, b, dims, precision=None):
    return lax.dot_general(a, b, (dims, ((), ())), precision=precision, preferred_element_type=F32)


NN = ((1,), (0,))
NT = ((1,), (1,))
TN = ((0,), (0,))


def split(x):
    high = x.astype(BF16)
    low = (x - high.astype(F32)).astype(BF16)
    return jnp.concatenate([high, low], axis=0)


def stage_kernel(row_in, col_in, rnd_in, count_in, tiles_ref, held, meta, row, col, rnd, count, sems):
    pairs = [(tiles_ref, held), (row_in, row), (col_in, col), (rnd_in, rnd), (count_in, count)]
    copies = [pltpu.make_async_copy(a, b, sems.at[i]) for i, (a, b) in enumerate(pairs)]
    for copy in copies:
        copy.start()
    member = lax.axis_index("rep")
    blocks = lax.axis_size("rep")
    for copy in copies[1:]:
        copy.wait()
    for t in range(held.shape[0]):
        meta[0, t] = rnd[0, 0, t] * blocks + lax.rem(member - col[0, 0, t] + blocks, blocks)
        meta[1, t] = lax.rem(member - row[0, 0, t] + blocks, blocks)
        meta[2, t] = jnp.where(t < count[0, 0], 1, 0)
    copies[0].wait()


def backward_kernel(meta, held, q_ref, *rest):
    outs, (terms, total) = rest[:-2], rest[-2:]
    blocks = q_ref.shape[0]
    trash = total.shape[0] - 1
    for b in range(blocks):
        terms[b] = split(q_ref[b])
    total[...] = jnp.zeros_like(total)
    for t in range(held.shape[0]):
        source = meta[1, t]
        target = jnp.where(meta[2, t] > 0, meta[0, t], trash)
        product = dot(terms[source], held[t], NN)
        half = product.shape[0] // 2
        total[target] += product[:half] + product[half:]
    for i, out in enumerate(outs):
        out[...] = total[i * blocks : (i + 1) * blocks]


def forward_kernel(meta, held, kept_ref, *rest):
    sources, out, (terms, total) = rest[: ROUNDS + 1], rest[ROUNDS + 1], rest[-2:]
    blocks = kept_ref.shape[0]
    trash = blocks
    for i, ref in enumerate(sources):
        for b in range(blocks):
            terms[i * blocks + b] = split(ref[b])
    total[:blocks] = kept_ref[...]
    total[trash] = jnp.zeros(total.shape[1:], F32)
    for t in range(held.shape[0]):
        source = meta[0, t]
        target = jnp.where(meta[2, t] > 0, meta[1, t], trash)
        product = dot(terms[source], held[t], NT)
        half = product.shape[0] // 2
        total[target] += product[:half] + product[half:]
    out[...] = total[:blocks]


def gram_kernel(s_ref, y_ref, z_ref, out):
    blocks, k, width = s_ref.shape
    grams = []
    for b in range(blocks):
        stack = jnp.concatenate([s_ref[b], y_ref[b], z_ref[b], jnp.zeros((k, width), F32)], axis=0)
        grams.append(dot(stack[: 3 * k], stack, NT, HIGHEST))
    half = blocks // 2
    pairs = [grams[i] + grams[i + half] for i in range(half)]
    out[...] = functools.reduce(lambda a, b: a + b, pairs)


def tail_kernel(gram_ref, s_ref, y_ref, z_ref, next_ref, coef_ref, fact_ref, upper, inverse):
    n, lanes = gram_ref.shape
    k, w = n // 3, 8
    shape = (w, lanes)
    lane = lax.broadcasted_iota(jnp.int32, shape, 1)
    held = [gram_ref[i * w : (i + 1) * w, :] for i in range(n // w)]

    def spread(x):
        return jnp.broadcast_to(x, shape)

    for j in range(n // w):
        at = j * w
        inside = (lane >= at) & (lane < at + w)
        columns = [spread(held[j][:, at + c : at + c + 1]) for c in range(w)]
        p = [[spread(columns[b][a : a + 1, :]) if a <= b else None for b in range(w)] for a in range(w)]
        rows = [
            jnp.where(inside, jnp.where(lane == at + a, 1.0, 0.0), spread(held[j][a : a + 1, :]))
            for a in range(w)
        ]
        inv, m = [], [[None] * w for _ in range(w)]
        for c in range(w):
            inv.append(1.0 / p[c][c])
            for a in range(c + 1, w):
                m[a][c] = p[c][a] * inv[c]
                for b in range(a, w):
                    p[a][b] = p[a][b] - m[a][c] * p[c][b]
                rows[a] = rows[a] - m[a][c] * rows[c]
        for i in range(j + 1, n // w):
            f = []
            for c in range(w):
                value = spread(held[i][:, at + c : at + c + 1])
                for d in range(c):
                    value = value - f[d] * m[c][d]
                f.append(value)
            new = jnp.where(inside, 0.0, held[i])
            for c in range(w):
                new = new - (f[c] * inv[c]) * rows[c]
            held[i] = new
        for a in range(w):
            root = lax.rsqrt(p[a][a])
            row = rows[a] * root
            diag = jnp.zeros(shape, F32)
            for b in range(a, w):
                diag = jnp.where(lane == at + b, p[a][b], diag)
            inverse[at + a : at + a + 1, :] = jnp.where(lane < at + w, row, 0.0)[:1]
            upper[at + a : at + a + 1, :] = jnp.where(lane >= at + w, row, diag * root)[:1]
    x, u = inverse[...], upper[...]
    u12, u13 = u[:k, k : 2 * k], u[:k, 2 * k : 3 * k]
    u22, u23 = u[k : 2 * k, k : 2 * k], u[k : 2 * k, 2 * k : 3 * k]
    u33 = u[2 * k : 3 * k, 2 * k : 3 * k]
    x11, x22 = x[:k, :k], x[k : 2 * k, k : 2 * k]
    fact_ref[0] = dot(x11, u22, NT, HIGHEST)
    fact_ref[1] = dot(x22, u33, NT, HIGHEST)
    coef_ref[0, :, :k] = dot(x11, u12, NT, HIGHEST)
    coef_ref[0, :, k:] = jnp.zeros((k, k), F32)
    v = dot(x11, u12, TN, HIGHEST)
    coef_ref[1, :, :k] = dot(x22, u23 - dot(u22, v, NN, HIGHEST), NT, HIGHEST)
    coef_ref[1, :, k:] = dot(x22, u13 - dot(u12, v, NN, HIGHEST), NT, HIGHEST)
    stack = jnp.concatenate([s_ref[0], y_ref[0], z_ref[0]], axis=0)
    next_ref[...] = dot(x[2 * k : 3 * k, : 3 * k], stack, NN, HIGHEST)


def moved(x, axis, target):
    size = lax.axis_size(axis)
    return lax.ppermute(x, axis, [(i, target(i) % size) for i in range(size)])


def shifted(x, axis, by):
    return moved(x, axis, lambda i: i + by)


def sum_of_ring(x, ring):
    first, second, third = ring(1), ring(2), ring(3)
    return (x + second) + (first + third)


def body(tiles, tile_row, tile_col, tile_round, tile_count, start_block):
    tiles = tiles[0, 0]
    slots, edge = tiles.shape[0], tiles.shape[1]
    k = start_block.shape[0]
    members = lax.axis_size("rep")
    devices = lax.axis_size("rows")
    blocks = members
    offsets = [max(1, devices // 2**r) for r in range(1, ROUNDS + 1)]
    held_shape = (blocks, k, edge)
    smem = pl.BlockSpec(memory_space=pltpu.SMEM)
    vmem = pl.BlockSpec(memory_space=pltpu.VMEM)
    hbm = pl.BlockSpec(memory_space=pltpu.HBM)
    block_shape = jax.ShapeDtypeStruct(held_shape, F32)
    params = pltpu.CompilerParams(vmem_limit_bytes=VMEM_LIMIT)
    cost = pl.CostEstimate(
        flops=4 * slots * edge * edge * k, bytes_accessed=2 * slots * edge * edge, transcendentals=0
    )

    def scratch(sources, targets):
        return [pltpu.VMEM((sources, 2 * k, edge), BF16), pltpu.VMEM((targets + 1, k, edge), F32)]

    held, meta = pl.pallas_call(
        stage_kernel,
        out_shape=[jax.ShapeDtypeStruct(tiles.shape, BF16), jax.ShapeDtypeStruct((3, slots), jnp.int32)],
        in_specs=[hbm] * 5,
        out_specs=[vmem, smem],
        scratch_shapes=[pltpu.SMEM((1, 1, slots), jnp.int32)] * 3
        + [pltpu.SMEM((1, 1), jnp.int32), pltpu.SemaphoreType.DMA((5,))],
        compiler_params=params,
        cost_estimate=pl.CostEstimate(flops=0, bytes_accessed=2 * slots * edge * edge, transcendentals=0),
    )(tile_row, tile_col, tile_round, tile_count, tiles)

    backward = pl.pallas_call(
        backward_kernel,
        out_shape=[block_shape] * (ROUNDS + 1),
        in_specs=[smem, vmem, vmem],
        out_specs=[vmem] * (ROUNDS + 1),
        scratch_shapes=scratch(blocks, (ROUNDS + 1) * blocks),
        compiler_params=params,
        cost_estimate=cost,
    )
    forward = pl.pallas_call(
        forward_kernel,
        out_shape=block_shape,
        in_specs=[smem] + [vmem] * (ROUNDS + 3),
        out_specs=vmem,
        scratch_shapes=scratch((ROUNDS + 1) * blocks, blocks),
        compiler_params=params,
        cost_estimate=cost,
    )

    def rep_sum(part):
        return sum_of_ring(part, lambda by: jnp.roll(shifted(part, "rep", by), by, axis=0))

    def apply(q):
        _, quarter, _, last = offsets
        kept, out32, out16, out8, out4 = backward(meta, held, q)
        got4 = shifted(q, "rows", -last)
        got16 = shifted(q, "rows", -quarter)
        u = shifted(out8, "rows", last)
        w = shifted(out32, "rows", quarter)
        got8 = shifted(got4, "rows", -last)
        got32 = shifted(got16, "rows", -quarter)
        v = shifted(out4 + u, "rows", last)
        x = shifted(out16 + w, "rows", quarter)
        part = forward(meta, held, kept, q, got32, got16, got8, got4)
        return rep_sum(part + v + x)

    start = jnp.stack([start_block] + [shifted(start_block, "rep", by) for by in range(1, members)], 0)
    first = apply(start)
    second = apply(first)
    gram = pl.pallas_call(
        gram_kernel,
        out_shape=jax.ShapeDtypeStruct((3 * k, 4 * k), F32),
        in_specs=[vmem] * 3,
        out_specs=vmem,
        compiler_params=params,
    )(start, first, second)
    gram = gram + moved(gram, "rows", lambda i: i ^ 1)
    gram = sum_of_ring(gram, lambda by: shifted(gram, "rows", by * (devices // 4)))
    gram = gram + moved(gram, "rows", lambda i: i ^ 8)
    gram = sum_of_ring(gram, lambda by: moved(gram, "rows", lambda i: (i & ~7) | ((i + 2 * by) & 7)))
    result, coefficients, factors = pl.pallas_call(
        tail_kernel,
        out_shape=[
            jax.ShapeDtypeStruct((k, edge), F32),
            jax.ShapeDtypeStruct((2, k, 2 * k), F32),
            jax.ShapeDtypeStruct((2, k, k), F32),
        ],
        in_specs=[vmem] * 4,
        out_specs=[vmem] * 3,
        scratch_shapes=[pltpu.VMEM((3 * k, 4 * k), F32), pltpu.VMEM((3 * k, 4 * k), F32)],
        compiler_params=params,
    )(gram, start, first, second)
    return result, jnp.swapaxes(coefficients, 1, 2), factors


def solution(mesh):
    placed = (
        P("rows", "rep", None, None, None),
        P("rows", "rep", None),
        P("rows", "rep", None),
        P("rows", "rep", None),
        P("rows", "rep"),
        P(None, ("rows", "rep")),
    )
    return jax.shard_map(
        body,
        mesh=mesh,
        in_specs=placed,
        out_specs=(P(None, ("rows", "rep")), P(), P()),
        check_vma=False,
    )
```

time: 132 us -> 117 us (0.89)
  Pallas kernels: 22.1 us -> 13.9 us
  starting transfers between devices: 54.5 us -> 49.1 us
    ppermute x33, starting transfers between devices: 54.5 us -> 49.1 us  [moved(): return lax.ppermute(x, axis, [(i, target(i) % size) for i in range(size)])]
    pallas_call x1, Pallas kernels: 9.48 us -> 4.75 us  [body(): pl.pallas_call(tail_kernel, out_shape=[jax.ShapeDtypeStruct((k, edge), F3...]
    pallas_call x4 -> x5, Pallas kernels: 12.2 us -> 8.65 us  [the longest x2 4 us: apply(): part = forward(meta, held, kept, q, got32, got16, got8, got4)]
    unnamed x8 -> x10, local copies, waits for them, and re-layouts: 4.15 us -> 4.15 us
  transfers between devices with their start and end apart: 33 -> 33, of which waited for: 19 -> 17; matrix products, arithmetic and copies ran while one was open for 0% -> 0% of each run, Pallas kernels for 9% -> 7%
where the time goes in v2:
time: 117 us; the launch traced here: 116 us
  starting transfers between devices  49.1 us (42%)
  waiting for transfers between devices  46.6 us (40%)
  Pallas kernels  13.9 us (12%)
  local copies, waits for them, and re-layouts  4.21 us (4%)
  between operations  1.63 us (1%)
    ppermute x33, starting transfers between devices, moved(): return lax.ppermute(x, axis, [(i, target(i) % size) for i in range(size)])  49.1 us
    ppermute x33, waiting for transfers between devices, moved(): return lax.ppermute(x, axis, [(i, target(i) % size) for i in range(size)])  46.6 us
    pallas_call x1, Pallas kernels, body(): pl.pallas_call(tail_kernel, out_shape=[jax.ShapeDtypeStruct((k, edge), F3...  4.75 us
    unnamed x10, local copies, waits for them, and re-layouts  4.15 us
    pallas_call x2, Pallas kernels, apply(): part = forward(meta, held, kept, q, got32, got16, got8, got4)  4 us
    pallas_call x2, Pallas kernels, apply(): kept, out32, out16, out8, out4 = backward(meta, held, q)  2.92 us
  transfers between devices with their start and end apart: 33, of which 17 were waited for; matrix products, arithmetic and copies ran while one was open for 0% of the time, Pallas kernels for 7%

profile of v2, /device:TPU:32, one launch (start us, length us, event | category | flops | bytes accessed | tf_op | source)
XLA Modules:
  0.0 115.7 jit_solution(5223037621766722532)
XLA Ops:
  0.6 1.6 %collective-permute-start = (f32[32,256]{1,0:T(8,128)}, f32[32,256]{1,0:T(8,128)S(1)}, u32[]{:S(2)}, u32[]{:S(2)}) collective-permute-start(f32[32,256]{1,0:T(8,128)} %param.11), channel_id=1, source_target_pairs={{0,1},{1,2},{2,3},{3,0},{4,5},{5,6},{6,7},{7,4},{8,9},{9,10},{10,1... | collective-permute-start | bytes 98312 | tf_op jit(solution)/shard_map/ppermute | solution.py:158
  2.2 2.7 %collective-permute-start.1 = (f32[32,256]{1,0:T(8,128)}, f32[32,256]{1,0:T(8,128)S(1)}, u32[]{:S(2)}, u32[]{:S(2)}) collective-permute-start(f32[32,256]{1,0:T(8,128)} %param.11), channel_id=1, source_target_pairs={{0,2},{1,3},{2,0},{3,1},{4,6},{5,7},{6,4},{7,5},{8,10},{9,11},{10,... | collective-permute-start | bytes 98312 | tf_op jit(solution)/shard_map/ppermute | solution.py:158
  4.9 1.4 %collective-permute-start.2 = (f32[32,256]{1,0:T(8,128)}, f32[32,256]{1,0:T(8,128)S(1)}, u32[]{:S(2)}, u32[]{:S(2)}) collective-permute-start(f32[32,256]{1,0:T(8,128)} %param.11), channel_id=1, source_target_pairs={{0,3},{1,0},{2,1},{3,2},{4,7},{5,4},{6,5},{7,6},{8,11},{9,8},{10,9... | collective-permute-start | bytes 98312 | tf_op jit(solution)/shard_map/ppermute | solution.py:158
  7.0 2.2 %copy-done = bf16[1,1,32,256,256]{4,3,2,1,0:T(8,128)(2,1)S(1)} copy-done((bf16[1,1,32,256,256]{4,3,2,1,0:T(8,128)(2,1)S(1)}, bf16[1,1,32,256,256]{4,3,2,1,0:T(8,128)(2,1)}, u32[]{:S(2)}) %copy-start) | copy-done | bytes 4194328
  11.2 1.7 %shard_map.85 = (bf16[32,256,256]{2,1,0:T(8,128)(2,1)S(1)}, s32[3,32]{1,0:T(4,128)S(1)}) custom-call(s32[1,1,32]{2,1,0:T(1,128)S(1)} %copy-done.1, s32[1,1,32]{2,1,0:T(1,128)S(1)} %copy-done.2, s32[1,1,32]{2,1,0:T(1,128)S(1)} %copy-done.3, s32[1,1]{1,0:T(1,128)S(6)} %copy.9.count_in, bf16[32,256,256]{2,1,0:T(8,128)(2,1)S(1)} %bitcast.6), custom_call_target="tpu_custom_call" | custom-call | bytes 4194304 | tf_op jit(solution)/shard_map/pallas_call | solution.py:191
  13.0 3.1 %collective-permute-start.3 = (f32[4,32,256]{2,1,0:T(8,128)S(1)}, f32[4,32,256]{2,1,0:T(8,128)S(1)}, u32[]{:S(2)}, u32[]{:S(2)}) collective-permute-start(f32[4,32,256]{2,1,0:T(8,128)S(1)} %pad_maximum_fusion.q_ref.rest_0_.s_ref), channel_id=1, source_target_pairs={{0,192},{4,196},{8,200},{12,204},{16,208},{20,212},{24,216},{28,22... | collective-permute-start | bytes 393224 | tf_op jit(solution)/shard_map/ppermute | solution.py:158
  16.1 5.6 %collective-permute-start.5 = (f32[4,32,256]{2,1,0:T(8,128)S(1)}, f32[4,32,256]{2,1,0:T(8,128)S(1)}, u32[]{:S(2)}, u32[]{:S(2)}) collective-permute-start(f32[4,32,256]{2,1,0:T(8,128)S(1)} %pad_maximum_fusion.q_ref.rest_0_.s_ref), channel_id=1, source_target_pairs={{0,240},{4,244},{8,248},{12,252},{16,0},{20,4},{24,8},{28,12},{32,... | collective-permute-start | bytes 393224 | tf_op jit(solution)/shard_map/ppermute | solution.py:158
  21.7 1.5 %shard_map.86 = (f32[4,32,256]{2,1,0:T(8,128)S(1)}, f32[4,32,256]{2,1,0:T(8,128)S(1)}, f32[4,32,256]{2,1,0:T(8,128)S(1)}, f32[4,32,256]{2,1,0:T(8,128)S(1)}, f32[4,32,256]{2,1,0:T(8,128)S(1)}) custom-call(s32[3,32]{1,0:T(4,128)S(1)} %get-tuple-element.18.meta, bf16[32,256,256]{2,1,0:T(8,128)(2,1)S(1)} %get-tuple-element.19.held, ...), custom_call_target="tpu_custom_call" | custom-call | flops 268435456 | bytes 4194304 | tf_op jit(solution)/shard_map/pallas_call | solution.py:226
  23.2 1.4 %collective-permute-start.9 = (f32[4,32,256]{2,1,0:T(8,128)S(1)}, f32[4,32,256]{2,1,0:T(8,128)S(1)}, u32[]{:S(2)}, u32[]{:S(2)}) collective-permute-start(f32[4,32,256]{2,1,0:T(8,128)S(1)} %get-tuple-element.24), channel_id=1, source_target_pairs={{0,64},{4,68},{8,72},{12,76},{16,80},{20,84},{24,88},{28,92},{32,9... | collective-permute-start | bytes 393224 | tf_op jit(solution)/shard_map/ppermute | solution.py:158
  24.6 2.0 %collective-permute-start.4 = (f32[4,32,256]{2,1,0:T(8,128)S(1)}, f32[4,32,256]{2,1,0:T(8,128)S(1)}, u32[]{:S(2)}, u32[]{:S(2)}) collective-permute-start(f32[4,32,256]{2,1,0:T(8,128)S(1)} %collective-permute-done.3.rest_2_), channel_id=1, source_target_pairs={{0,192},{4,196},{8,200},{12,204},{16,208},{20,212},{24,216},{28,22... | collective-permute-start | bytes 393224 | tf_op jit(solution)/shard_map/ppermute | solution.py:158
  26.5 4.9 %collective-permute-start.6 = (f32[4,32,256]{2,1,0:T(8,128)S(1)}, f32[4,32,256]{2,1,0:T(8,128)S(1)}, u32[]{:S(2)}, u32[]{:S(2)}) collective-permute-start(f32[4,32,256]{2,1,0:T(8,128)S(1)} %collective-permute-done.5.rest_4_), channel_id=1, source_target_pairs={{0,240},{4,244},{8,248},{12,252},{16,0},{20,4},{24,8},{28,12},{32,... | collective-permute-start | bytes 393224 | tf_op jit(solution)/shard_map/ppermute | solution.py:158
  31.5 3.1 %collective-permute-done.7 = f32[4,32,256]{2,1,0:T(8,128)S(1)} collective-permute-done((f32[4,32,256]{2,1,0:T(8,128)S(1)}, f32[4,32,256]{2,1,0:T(8,128)S(1)}, u32[]{:S(2)}, u32[]{:S(2)}) %collective-permute-start.7) | collective-permute-done | bytes 131104 | tf_op jit(solution)/shard_map/ppermute | solution.py:158
  35.2 2.0 %shard_map.87 = f32[4,32,256]{2,1,0:T(8,128)S(1)} custom-call(s32[3,32]{1,0:T(4,128)S(1)} %get-tuple-element.18.meta, bf16[32,256,256]{2,1,0:T(8,128)(2,1)S(1)} %get-tuple-element.19.held, f32[4,32,256]{2,1,0:T(8,128)S(1)} %get-tuple-element.20.kept_ref, f32[4,32,256]{2,1,0:T(8,128)S(1)} %pad_maximum_fusion.q_ref.rest_0_.s_ref, ...), custom_call_target="tpu_custom_call" | custom-call | flops 268435456 | bytes 4194304 | tf_op jit(solution)/shard_map/pallas_call | solution.py:235
  37.2 7.1 %collective-permute-done.8 = f32[4,32,256]{2,1,0:T(8,128)S(1)} collective-permute-done((f32[4,32,256]{2,1,0:T(8,128)S(1)}, f32[4,32,256]{2,1,0:T(8,128)S(1)}, u32[]{:S(2)}, u32[]{:S(2)}) %collective-permute-start.8) | collective-permute-done | bytes 131104 | tf_op jit(solution)/shard_map/ppermute | solution.py:158
  45.0 2.7 %collective-permute-start.13 = (f32[4,32,256]{2,1,0:T(8,128)S(1)}, f32[4,32,256]{2,1,0:T(8,128)S(1)}, u32[]{:S(2)}, u32[]{:S(2)}) collective-permute-start(f32[4,32,256]{2,1,0:T(8,128)S(1)} %add_add_fusion.1), channel_id=1, source_target_pairs={{0,3},{1,0},{2,1},{3,2},{4,7},{5,4},{6,5},{7,6},{8,11},{9,8},{10,9... | collective-permute-start | bytes 393224 | tf_op jit(solution)/shard_map/ppermute | solution.py:158
  47.7 2.9 %collective-permute-done.12 = f32[4,32,256]{2,1,0:T(8,128)S(1)} collective-permute-done((f32[4,32,256]{2,1,0:T(8,128)S(1)}, f32[4,32,256]{2,1,0:T(8,128)S(1)}, u32[]{:S(2)}, u32[]{:S(2)}) %collective-permute-start.12) | collective-permute-done | bytes 131104 | tf_op jit(solution)/shard_map/ppermute | solution.py:158
  51.6 2.5 %collective-permute-done.11 = f32[4,32,256]{2,1,0:T(8,128)S(1)} collective-permute-done((f32[4,32,256]{2,1,0:T(8,128)S(1)}, f32[4,32,256]{2,1,0:T(8,128)S(1)}, u32[]{:S(2)}, u32[]{:S(2)}) %collective-permute-start.11) | collective-permute-done | bytes 131104 | tf_op jit(solution)/shard_map/ppermute | solution.py:158
  54.3 1.7 %collective-permute-start.16 = (f32[4,32,256]{2,1,0:T(8,128)S(1)}, f32[4,32,256]{2,1,0:T(8,128)S(1)}, u32[]{:S(2)}, u32[]{:S(2)}) collective-permute-start(f32[4,32,256]{2,1,0:T(8,128)S(1)} %fusion.q_ref.rest_0_.y_ref), channel_id=1, source_target_pairs={{0,240},{4,244},{8,248},{12,252},{16,0},{20,4},{24,8},{28,12},{32,... | collective-permute-start | bytes 393224 | tf_op jit(solution)/shard_map/ppermute | solution.py:158
  56.0 1.5 %shard_map.88 = (f32[4,32,256]{2,1,0:T(8,128)S(1)}, f32[4,32,256]{2,1,0:T(8,128)S(1)}, f32[4,32,256]{2,1,0:T(8,128)S(1)}, f32[4,32,256]{2,1,0:T(8,128)S(1)}, f32[4,32,256]{2,1,0:T(8,128)S(1)}) custom-call(s32[3,32]{1,0:T(4,128)S(1)} %get-tuple-element.18.meta, bf16[32,256,256]{2,1,0:T(8,128)(2,1)S(1)} %get-tuple-element.19.held, ...), custom_call_target="tpu_custom_call" | custom-call | flops 268435456 | bytes 4194304 | tf_op jit(solution)/shard_map/pallas_call | solution.py:226
  57.5 1.4 %collective-permute-start.18 = (f32[4,32,256]{2,1,0:T(8,128)S(1)}, f32[4,32,256]{2,1,0:T(8,128)S(1)}, u32[]{:S(2)}, u32[]{:S(2)}) collective-permute-start(f32[4,32,256]{2,1,0:T(8,128)S(1)} %get-tuple-element.27), channel_id=1, source_target_pairs={{0,16},{4,20},{8,24},{12,28},{16,32},{20,36},{24,40},{28,44},{32,4... | collective-permute-start | bytes 393224 | tf_op jit(solution)/shard_map/ppermute | solution.py:158
  58.9 1.9 %collective-permute-start.20 = (f32[4,32,256]{2,1,0:T(8,128)S(1)}, f32[4,32,256]{2,1,0:T(8,128)S(1)}, u32[]{:S(2)}, u32[]{:S(2)}) collective-permute-start(f32[4,32,256]{2,1,0:T(8,128)S(1)} %get-tuple-element.29), channel_id=1, source_target_pairs={{0,64},{4,68},{8,72},{12,76},{16,80},{20,84},{24,88},{28,92},{32,9... | collective-permute-start | bytes 393224 | tf_op jit(solution)/shard_map/ppermute | solution.py:158
  62.1 6.4 %collective-permute-start.17 = (f32[4,32,256]{2,1,0:T(8,128)S(1)}, f32[4,32,256]{2,1,0:T(8,128)S(1)}, u32[]{:S(2)}, u32[]{:S(2)}) collective-permute-start(f32[4,32,256]{2,1,0:T(8,128)S(1)} %collective-permute-done.16.rest_4_), channel_id=1, source_target_pairs={{0,240},{4,244},{8,248},{12,252},{16,0},{20,4},{24,8},{28,12},{32,... | collective-permute-start | bytes 393224 | tf_op jit(solution)/shard_map/ppermute | solution.py:158
  71.0 2.0 %shard_map.89 = f32[4,32,256]{2,1,0:T(8,128)S(1)} custom-call(s32[3,32]{1,0:T(4,128)S(1)} %get-tuple-element.18.meta, bf16[32,256,256]{2,1,0:T(8,128)(2,1)S(1)} %get-tuple-element.19.held, f32[4,32,256]{2,1,0:T(8,128)S(1)} %get-tuple-element.25.kept_ref, f32[4,32,256]{2,1,0:T(8,128)S(1)} %fusion.q_ref.rest_0_.y_ref, ...), custom_call_target="tpu_custom_call" | custom-call | flops 268435456 | bytes 4194304 | tf_op jit(solution)/shard_map/pallas_call | solution.py:235
  73.0 5.8 %collective-permute-done.19 = f32[4,32,256]{2,1,0:T(8,128)S(1)} collective-permute-done((f32[4,32,256]{2,1,0:T(8,128)S(1)}, f32[4,32,256]{2,1,0:T(8,128)S(1)}, u32[]{:S(2)}, u32[]{:S(2)}) %collective-permute-start.19) | collective-permute-done | bytes 131104 | tf_op jit(solution)/shard_map/ppermute | solution.py:158
  79.4 2.8 %collective-permute-start.24 = (f32[4,32,256]{2,1,0:T(8,128)S(1)}, f32[4,32,256]{2,1,0:T(8,128)S(1)}, u32[]{:S(2)}, u32[]{:S(2)}) collective-permute-start(f32[4,32,256]{2,1,0:T(8,128)S(1)} %add_add_fusion), channel_id=1, source_target_pairs={{0,3},{1,0},{2,1},{3,2},{4,7},{5,4},{6,5},{7,6},{8,11},{9,8},{10,9... | collective-permute-start | bytes 393224 | tf_op jit(solution)/shard_map/ppermute | solution.py:158
  83.0 2.1 %collective-permute-done.23 = f32[4,32,256]{2,1,0:T(8,128)S(1)} collective-permute-done((f32[4,32,256]{2,1,0:T(8,128)S(1)}, f32[4,32,256]{2,1,0:T(8,128)S(1)}, u32[]{:S(2)}, u32[]{:S(2)}) %collective-permute-start.23) | collective-permute-done | bytes 131104 | tf_op jit(solution)/shard_map/ppermute | solution.py:158
  85.2 3.5 %collective-permute-done.22 = f32[4,32,256]{2,1,0:T(8,128)S(1)} collective-permute-done((f32[4,32,256]{2,1,0:T(8,128)S(1)}, f32[4,32,256]{2,1,0:T(8,128)S(1)}, u32[]{:S(2)}, u32[]{:S(2)}) %collective-permute-start.22) | collective-permute-done | bytes 131104 | tf_op jit(solution)/shard_map/ppermute | solution.py:158
  90.7 3.2 %collective-permute-start.28 = (f32[96,128]{1,0:T(8,128)S(1)}, f32[96,128]{1,0:T(8,128)S(1)}, u32[]{:S(2)}, u32[]{:S(2)}) collective-permute-start(f32[96,128]{1,0:T(8,128)S(1)} %add.80), channel_id=1, source_target_pairs={{0,192},{4,196},{8,200},{12,204},{16,208},{20,212},{24,216},{28,22... | collective-permute-start | bytes 147464 | tf_op jit(solution)/shard_map/ppermute | solution.py:158
  93.9 2.5 %collective-permute-done.26 = f32[96,128]{1,0:T(8,128)S(1)} collective-permute-done((f32[96,128]{1,0:T(8,128)S(1)}, f32[96,128]{1,0:T(8,128)S(1)}, u32[]{:S(2)}, u32[]{:S(2)}) %collective-permute-start.26) | collective-permute-done | bytes 49184 | tf_op jit(solution)/shard_map/ppermute | solution.py:158
  96.8 8.0 %collective-permute-done.29 = f32[96,128]{1,0:T(8,128)S(1)} collective-permute-done((f32[96,128]{1,0:T(8,128)S(1)}, f32[96,128]{1,0:T(8,128)S(1)}, u32[]{:S(2)}, u32[]{:S(2)}) %collective-permute-start.29) | collective-permute-done | bytes 49184 | tf_op jit(solution)/shard_map/ppermute | solution.py:158
  107.0 2.9 %collective-permute-done.30 = f32[96,128]{1,0:T(8,128)S(1)} collective-permute-done((f32[96,128]{1,0:T(8,128)S(1)}, f32[96,128]{1,0:T(8,128)S(1)}, u32[]{:S(2)}, u32[]{:S(2)}) %collective-permute-start.30) | collective-permute-done | bytes 49184 | tf_op jit(solution)/shard_map/ppermute | solution.py:158
  110.9 4.7 %shard_map.91 = (f32[32,256]{1,0:T(8,128)}, f32[2,32,64]{2,1,0:T(8,128)}, f32[2,32,32]{2,1,0:T(8,128)}) custom-call(f32[96,128]{1,0:T(8,128)S(1)} %add_add_fusion.2.gram_ref, f32[4,32,256]{2,1,0:T(8,128)S(1)} %pad_maximum_fusion.q_ref.rest_0_.s_ref, f32[4,32,256]{2,1,0:T(8,128)S(1)} %fusion.q_ref.rest_0_.y_ref, f32[4,32,256]{2,1,0:T(8,128)S(1)} %fusion.1.z_ref), custom_call_target="tpu_custom_call" | custom-call | tf_op jit(solution)/shard_map/pallas_call | solution.py:252
  (74 shorter events, 15.3 us)
Async XLA Ops:
  0.6 12.3 %collective-permute-start = (f32[32,256]{1,0:T(8,128)}, f32[32,256]{1,0:T(8,128)S(1)}, u32[]{:S(2)}, u32[]{:S(2)}) collective-permute-start(f32[32,256]{1,0:T(8,128)} %param.11), channel_id=1, source_target_pairs={{0,1},{1,2},{2,3},{3,0},{4,5},{5,6},{6,7},{7,4},{8,9},{9,10},{10,1... | collective-permute-start | bytes 98312 | tf_op jit(solution)/shard_map/ppermute | solution.py:158
  2.2 10.7 %collective-permute-start.1 = (f32[32,256]{1,0:T(8,128)}, f32[32,256]{1,0:T(8,128)S(1)}, u32[]{:S(2)}, u32[]{:S(2)}) collective-permute-start(f32[32,256]{1,0:T(8,128)} %param.11), channel_id=1, source_target_pairs={{0,2},{1,3},{2,0},{3,1},{4,6},{5,7},{6,4},{7,5},{8,10},{9,11},{10,... | collective-permute-start | bytes 98312 | tf_op jit(solution)/shard_map/ppermute | solution.py:158
  4.9 8.0 %collective-permute-start.2 = (f32[32,256]{1,0:T(8,128)}, f32[32,256]{1,0:T(8,128)S(1)}, u32[]{:S(2)}, u32[]{:S(2)}) collective-permute-start(f32[32,256]{1,0:T(8,128)} %param.11), channel_id=1, source_target_pairs={{0,3},{1,0},{2,1},{3,2},{4,7},{5,4},{6,5},{7,6},{8,11},{9,8},{10,9... | collective-permute-start | bytes 98312 | tf_op jit(solution)/shard_map/ppermute | solution.py:158
  13.0 11.6 %collective-permute-start.3 = (f32[4,32,256]{2,1,0:T(8,128)S(1)}, f32[4,32,256]{2,1,0:T(8,128)S(1)}, u32[]{:S(2)}, u32[]{:S(2)}) collective-permute-start(f32[4,32,256]{2,1,0:T(8,128)S(1)} %pad_maximum_fusion.q_ref.rest_0_.s_ref), channel_id=1, source_target_pairs={{0,192},{4,196},{8,200},{12,204},{16,208},{20,212},{24,216},{28,22... | collective-permute-start | bytes 393224 | tf_op jit(solution)/shard_map/ppermute | solution.py:158
  16.1 10.5 %collective-permute-start.5 = (f32[4,32,256]{2,1,0:T(8,128)S(1)}, f32[4,32,256]{2,1,0:T(8,128)S(1)}, u32[]{:S(2)}, u32[]{:S(2)}) collective-permute-start(f32[4,32,256]{2,1,0:T(8,128)S(1)} %pad_maximum_fusion.q_ref.rest_0_.s_ref), channel_id=1, source_target_pairs={{0,240},{4,244},{8,248},{12,252},{16,0},{20,4},{24,8},{28,12},{32,... | collective-permute-start | bytes 393224 | tf_op jit(solution)/shard_map/ppermute | solution.py:158
  23.1 11.5 %collective-permute-start.7 = (f32[4,32,256]{2,1,0:T(8,128)S(1)}, f32[4,32,256]{2,1,0:T(8,128)S(1)}, u32[]{:S(2)}, u32[]{:S(2)}) collective-permute-start(f32[4,32,256]{2,1,0:T(8,128)S(1)} %get-tuple-element.22), channel_id=1, source_target_pairs={{0,16},{4,20},{8,24},{12,28},{16,32},{20,36},{24,40},{28,44},{32,4... | collective-permute-start | bytes 393224 | tf_op jit(solution)/shard_map/ppermute | solution.py:158
  23.2 11.5 %collective-permute-start.9 = (f32[4,32,256]{2,1,0:T(8,128)S(1)}, f32[4,32,256]{2,1,0:T(8,128)S(1)}, u32[]{:S(2)}, u32[]{:S(2)}) collective-permute-start(f32[4,32,256]{2,1,0:T(8,128)S(1)} %get-tuple-element.24), channel_id=1, source_target_pairs={{0,64},{4,68},{8,72},{12,76},{16,80},{20,84},{24,88},{28,92},{32,9... | collective-permute-start | bytes 393224 | tf_op jit(solution)/shard_map/ppermute | solution.py:158
  24.6 10.2 %collective-permute-start.4 = (f32[4,32,256]{2,1,0:T(8,128)S(1)}, f32[4,32,256]{2,1,0:T(8,128)S(1)}, u32[]{:S(2)}, u32[]{:S(2)}) collective-permute-start(f32[4,32,256]{2,1,0:T(8,128)S(1)} %collective-permute-done.3.rest_2_), channel_id=1, source_target_pairs={{0,192},{4,196},{8,200},{12,204},{16,208},{20,212},{24,216},{28,22... | collective-permute-start | bytes 393224 | tf_op jit(solution)/shard_map/ppermute | solution.py:158
  26.5 8.7 %collective-permute-start.6 = (f32[4,32,256]{2,1,0:T(8,128)S(1)}, f32[4,32,256]{2,1,0:T(8,128)S(1)}, u32[]{:S(2)}, u32[]{:S(2)}) collective-permute-start(f32[4,32,256]{2,1,0:T(8,128)S(1)} %collective-permute-done.5.rest_4_), channel_id=1, source_target_pairs={{0,240},{4,244},{8,248},{12,252},{16,0},{20,4},{24,8},{28,12},{32,... | collective-permute-start | bytes 393224 | tf_op jit(solution)/shard_map/ppermute | solution.py:158
  34.6 9.7 %collective-permute-start.8 = (f32[4,32,256]{2,1,0:T(8,128)S(1)}, f32[4,32,256]{2,1,0:T(8,128)S(1)}, u32[]{:S(2)}, u32[]{:S(2)}) collective-permute-start(f32[4,32,256]{2,1,0:T(8,128)S(1)} %add.66), channel_id=1, source_target_pairs={{0,16},{4,20},{8,24},{12,28},{16,32},{20,36},{24,40},{28,44},{32,4... | collective-permute-start | bytes 393224 | tf_op jit(solution)/shard_map/ppermute | solution.py:158
  34.7 9.6 %collective-permute-start.10 = (f32[4,32,256]{2,1,0:T(8,128)S(1)}, f32[4,32,256]{2,1,0:T(8,128)S(1)}, u32[]{:S(2)}, u32[]{:S(2)}) collective-permute-start(f32[4,32,256]{2,1,0:T(8,128)S(1)} %add.68), channel_id=1, source_target_pairs={{0,64},{4,68},{8,72},{12,76},{16,80},{20,84},{24,88},{28,92},{32,9... | collective-permute-start | bytes 393224 | tf_op jit(solution)/shard_map/ppermute | solution.py:158
  44.4 6.3 %collective-permute-start.12 = (f32[4,32,256]{2,1,0:T(8,128)S(1)}, f32[4,32,256]{2,1,0:T(8,128)S(1)}, u32[]{:S(2)}, u32[]{:S(2)}) collective-permute-start(f32[4,32,256]{2,1,0:T(8,128)S(1)} %add_add_fusion.1), channel_id=1, source_target_pairs={{0,1},{1,2},{2,3},{3,0},{4,5},{5,6},{6,7},{7,4},{8,9},{9,10},{10,1... | collective-permute-start | bytes 393224 | tf_op jit(solution)/shard_map/ppermute | solution.py:158
  45.0 6.6 %collective-permute-start.13 = (f32[4,32,256]{2,1,0:T(8,128)S(1)}, f32[4,32,256]{2,1,0:T(8,128)S(1)}, u32[]{:S(2)}, u32[]{:S(2)}) collective-permute-start(f32[4,32,256]{2,1,0:T(8,128)S(1)} %add_add_fusion.1), channel_id=1, source_target_pairs={{0,3},{1,0},{2,1},{3,2},{4,7},{5,4},{6,5},{7,6},{8,11},{9,8},{10,9... | collective-permute-start | bytes 393224 | tf_op jit(solution)/shard_map/ppermute | solution.py:158
  47.7 6.5 %collective-permute-start.11 = (f32[4,32,256]{2,1,0:T(8,128)S(1)}, f32[4,32,256]{2,1,0:T(8,128)S(1)}, u32[]{:S(2)}, u32[]{:S(2)}) collective-permute-start(f32[4,32,256]{2,1,0:T(8,128)S(1)} %add_add_fusion.1), channel_id=1, source_target_pairs={{0,2},{1,3},{2,0},{3,1},{4,6},{5,7},{6,4},{7,5},{8,10},{9,11},{10,... | collective-permute-start | bytes 393224 | tf_op jit(solution)/shard_map/ppermute | solution.py:158
  54.2 6.6 %collective-permute-start.14 = (f32[4,32,256]{2,1,0:T(8,128)S(1)}, f32[4,32,256]{2,1,0:T(8,128)S(1)}, u32[]{:S(2)}, u32[]{:S(2)}) collective-permute-start(f32[4,32,256]{2,1,0:T(8,128)S(1)} %fusion.q_ref.rest_0_.y_ref), channel_id=1, source_target_pairs={{0,192},{4,196},{8,200},{12,204},{16,208},{20,212},{24,216},{28,22... | collective-permute-start | bytes 393224 | tf_op jit(solution)/shard_map/ppermute | solution.py:158
  54.3 7.8 %collective-permute-start.16 = (f32[4,32,256]{2,1,0:T(8,128)S(1)}, f32[4,32,256]{2,1,0:T(8,128)S(1)}, u32[]{:S(2)}, u32[]{:S(2)}) collective-permute-start(f32[4,32,256]{2,1,0:T(8,128)S(1)} %fusion.q_ref.rest_0_.y_ref), channel_id=1, source_target_pairs={{0,240},{4,244},{8,248},{12,252},{16,0},{20,4},{24,8},{28,12},{32,... | collective-permute-start | bytes 393224 | tf_op jit(solution)/shard_map/ppermute | solution.py:158
  57.5 12.0 %collective-permute-start.18 = (f32[4,32,256]{2,1,0:T(8,128)S(1)}, f32[4,32,256]{2,1,0:T(8,128)S(1)}, u32[]{:S(2)}, u32[]{:S(2)}) collective-permute-start(f32[4,32,256]{2,1,0:T(8,128)S(1)} %get-tuple-element.27), channel_id=1, source_target_pairs={{0,16},{4,20},{8,24},{12,28},{16,32},{20,36},{24,40},{28,44},{32,4... | collective-permute-start | bytes 393224 | tf_op jit(solution)/shard_map/ppermute | solution.py:158
  58.9 10.8 %collective-permute-start.20 = (f32[4,32,256]{2,1,0:T(8,128)S(1)}, f32[4,32,256]{2,1,0:T(8,128)S(1)}, u32[]{:S(2)}, u32[]{:S(2)}) collective-permute-start(f32[4,32,256]{2,1,0:T(8,128)S(1)} %get-tuple-element.29), channel_id=1, source_target_pairs={{0,64},{4,68},{8,72},{12,76},{16,80},{20,84},{24,88},{28,92},{32,9... | collective-permute-start | bytes 393224 | tf_op jit(solution)/shard_map/ppermute | solution.py:158
  60.8 9.0 %collective-permute-start.15 = (f32[4,32,256]{2,1,0:T(8,128)S(1)}, f32[4,32,256]{2,1,0:T(8,128)S(1)}, u32[]{:S(2)}, u32[]{:S(2)}) collective-permute-start(f32[4,32,256]{2,1,0:T(8,128)S(1)} %collective-permute-done.14.rest_2_), channel_id=1, source_target_pairs={{0,192},{4,196},{8,200},{12,204},{16,208},{20,212},{24,216},{28,22... | collective-permute-start | bytes 393224 | tf_op jit(solution)/shard_map/ppermute | solution.py:158
  62.1 8.9 %collective-permute-start.17 = (f32[4,32,256]{2,1,0:T(8,128)S(1)}, f32[4,32,256]{2,1,0:T(8,128)S(1)}, u32[]{:S(2)}, u32[]{:S(2)}) collective-permute-start(f32[4,32,256]{2,1,0:T(8,128)S(1)} %collective-permute-done.16.rest_4_), channel_id=1, source_target_pairs={{0,240},{4,244},{8,248},{12,252},{16,0},{20,4},{24,8},{28,12},{32,... | collective-permute-start | bytes 393224 | tf_op jit(solution)/shard_map/ppermute | solution.py:158
  69.6 9.3 %collective-permute-start.19 = (f32[4,32,256]{2,1,0:T(8,128)S(1)}, f32[4,32,256]{2,1,0:T(8,128)S(1)}, u32[]{:S(2)}, u32[]{:S(2)}) collective-permute-start(f32[4,32,256]{2,1,0:T(8,128)S(1)} %add.73), channel_id=1, source_target_pairs={{0,16},{4,20},{8,24},{12,28},{16,32},{20,36},{24,40},{28,44},{32,4... | collective-permute-start | bytes 393224 | tf_op jit(solution)/shard_map/ppermute | solution.py:158
  69.7 9.1 %collective-permute-start.21 = (f32[4,32,256]{2,1,0:T(8,128)S(1)}, f32[4,32,256]{2,1,0:T(8,128)S(1)}, u32[]{:S(2)}, u32[]{:S(2)}) collective-permute-start(f32[4,32,256]{2,1,0:T(8,128)S(1)} %add.75), channel_id=1, source_target_pairs={{0,64},{4,68},{8,72},{12,76},{16,80},{20,84},{24,88},{28,92},{32,9... | collective-permute-start | bytes 393224 | tf_op jit(solution)/shard_map/ppermute | solution.py:158
  78.9 6.3 %collective-permute-start.23 = (f32[4,32,256]{2,1,0:T(8,128)S(1)}, f32[4,32,256]{2,1,0:T(8,128)S(1)}, u32[]{:S(2)}, u32[]{:S(2)}) collective-permute-start(f32[4,32,256]{2,1,0:T(8,128)S(1)} %add_add_fusion), channel_id=1, source_target_pairs={{0,1},{1,2},{2,3},{3,0},{4,5},{5,6},{6,7},{7,4},{8,9},{9,10},{10,1... | collective-permute-start | bytes 393224 | tf_op jit(solution)/shard_map/ppermute | solution.py:158
  79.4 5.8 %collective-permute-start.24 = (f32[4,32,256]{2,1,0:T(8,128)S(1)}, f32[4,32,256]{2,1,0:T(8,128)S(1)}, u32[]{:S(2)}, u32[]{:S(2)}) collective-permute-start(f32[4,32,256]{2,1,0:T(8,128)S(1)} %add_add_fusion), channel_id=1, source_target_pairs={{0,3},{1,0},{2,1},{3,2},{4,7},{5,4},{6,5},{7,6},{8,11},{9,8},{10,9... | collective-permute-start | bytes 393224 | tf_op jit(solution)/shard_map/ppermute | solution.py:158
  82.2 6.5 %collective-permute-start.22 = (f32[4,32,256]{2,1,0:T(8,128)S(1)}, f32[4,32,256]{2,1,0:T(8,128)S(1)}, u32[]{:S(2)}, u32[]{:S(2)}) collective-permute-start(f32[4,32,256]{2,1,0:T(8,128)S(1)} %add_add_fusion), channel_id=1, source_target_pairs={{0,2},{1,3},{2,0},{3,1},{4,6},{5,7},{6,4},{7,5},{8,10},{9,11},{10,... | collective-permute-start | bytes 393224 | tf_op jit(solution)/shard_map/ppermute | solution.py:158
  90.5 5.9 %collective-permute-start.26 = (f32[96,128]{1,0:T(8,128)S(1)}, f32[96,128]{1,0:T(8,128)S(1)}, u32[]{:S(2)}, u32[]{:S(2)}) collective-permute-start(f32[96,128]{1,0:T(8,128)S(1)} %add.80), channel_id=1, source_target_pairs={{0,128},{4,132},{8,136},{12,140},{16,144},{20,148},{24,152},{28,15... | collective-permute-start | bytes 147464 | tf_op jit(solution)/shard_map/ppermute | solution.py:158
  90.6 6.1 %collective-permute-start.27 = (f32[96,128]{1,0:T(8,128)S(1)}, f32[96,128]{1,0:T(8,128)S(1)}, u32[]{:S(2)}, u32[]{:S(2)}) collective-permute-start(f32[96,128]{1,0:T(8,128)S(1)} %add.80), channel_id=1, source_target_pairs={{0,64},{4,68},{8,72},{12,76},{16,80},{20,84},{24,88},{28,92},{32,9... | collective-permute-start | bytes 147464 | tf_op jit(solution)/shard_map/ppermute | solution.py:158
  90.7 6.0 %collective-permute-start.28 = (f32[96,128]{1,0:T(8,128)S(1)}, f32[96,128]{1,0:T(8,128)S(1)}, u32[]{:S(2)}, u32[]{:S(2)}) collective-permute-start(f32[96,128]{1,0:T(8,128)S(1)} %add.80), channel_id=1, source_target_pairs={{0,192},{4,196},{8,200},{12,204},{16,208},{20,212},{24,216},{28,22... | collective-permute-start | bytes 147464 | tf_op jit(solution)/shard_map/ppermute | solution.py:158
  96.7 8.1 %collective-permute-start.29 = (f32[96,128]{1,0:T(8,128)S(1)}, f32[96,128]{1,0:T(8,128)S(1)}, u32[]{:S(2)}, u32[]{:S(2)}) collective-permute-start(f32[96,128]{1,0:T(8,128)S(1)} %add_add_fusion.3), channel_id=1, source_target_pairs={{0,32},{4,36},{8,40},{12,44},{16,48},{20,52},{24,56},{28,60},{32,0... | collective-permute-start | bytes 147464 | tf_op jit(solution)/shard_map/ppermute | solution.py:158
  104.8 5.1 %collective-permute-start.30 = (f32[96,128]{1,0:T(8,128)S(1)}, f32[96,128]{1,0:T(8,128)S(1)}, u32[]{:S(2)}, u32[]{:S(2)}) collective-permute-start(f32[96,128]{1,0:T(8,128)S(1)} %add.84), channel_id=1, source_target_pairs={{0,16},{4,20},{8,24},{12,28},{16,0},{20,4},{24,8},{28,12},{32,48},... | collective-permute-start | bytes 147464 | tf_op jit(solution)/shard_map/ppermute | solution.py:158
  104.9 5.0 %collective-permute-start.31 = (f32[96,128]{1,0:T(8,128)S(1)}, f32[96,128]{1,0:T(8,128)S(1)}, u32[]{:S(2)}, u32[]{:S(2)}) collective-permute-start(f32[96,128]{1,0:T(8,128)S(1)} %add.84), channel_id=1, source_target_pairs={{0,8},{4,12},{8,16},{12,20},{16,24},{20,28},{24,0},{28,4},{32,40},... | collective-permute-start | bytes 147464 | tf_op jit(solution)/shard_map/ppermute | solution.py:158
  105.9 5.0 %collective-permute-start.32 = (f32[96,128]{1,0:T(8,128)S(1)}, f32[96,128]{1,0:T(8,128)S(1)}, u32[]{:S(2)}, u32[]{:S(2)}) collective-permute-start(f32[96,128]{1,0:T(8,128)S(1)} %add.84), channel_id=1, source_target_pairs={{0,24},{4,28},{8,0},{12,4},{16,8},{20,12},{24,16},{28,20},{32,56},... | collective-permute-start | bytes 147464 | tf_op jit(solution)/shard_map/ppermute | solution.py:158
  (6 other events, 7.3 us)

commit v3 on v2

--- a/solution.py
+++ b/solution.py
@@ -27,22 +27,6 @@
     high = x.astype(BF16)
     low = (x - high.astype(F32)).astype(BF16)
     return jnp.concatenate([high, low], axis=0)
-
-
-def stage_kernel(row_in, col_in, rnd_in, count_in, tiles_ref, held, meta, row, col, rnd, count, sems):
-    pairs = [(tiles_ref, held), (row_in, row), (col_in, col), (rnd_in, rnd), (count_in, count)]
-    copies = [pltpu.make_async_copy(a, b, sems.at[i]) for i, (a, b) in enumerate(pairs)]
-    for copy in copies:
-        copy.start()
-    member = lax.axis_index("rep")
-    blocks = lax.axis_size("rep")
-    for copy in copies[1:]:
-        copy.wait()
-    for t in range(held.shape[0]):
-        meta[0, t] = rnd[0, 0, t] * blocks + lax.rem(member - col[0, 0, t] + blocks, blocks)
-        meta[1, t] = lax.rem(member - row[0, 0, t] + blocks, blocks)
-        meta[2, t] = jnp.where(t < count[0, 0], 1, 0)
-    copies[0].wait()
 
 
 def backward_kernel(meta, held, q_ref, *rest):
@@ -88,15 +72,30 @@
         grams.append(dot(stack[: 3 * k], stack, NT, HIGHEST))
     half = blocks // 2
     pairs = [grams[i] + grams[i + half] for i in range(half)]
-    out[...] = functools.reduce(lambda a, b: a + b, pairs)
+    gram = functools.reduce(lambda a, b: a + b, pairs)
+    out[:k] = jnp.concatenate([gram[:k, : 3 * k], gram[2 * k :, 2 * k : 3 * k]], axis=1)
+    rows = k // 2
+    cut = [gram[k + i * rows : k + (i + 1) * rows, k : 3 * k] for i in range(2)]
+    out[k:] = jnp.concatenate(cut, axis=1)
 
 
 def tail_kernel(gram_ref, s_ref, y_ref, z_ref, next_ref, coef_ref, fact_ref, upper, inverse):
-    n, lanes = gram_ref.shape
-    k, w = n // 3, 8
+    lanes, w = gram_ref.shape[1], 8
+    k = lanes // 4
+    n = 3 * k
     shape = (w, lanes)
     lane = lax.broadcasted_iota(jnp.int32, shape, 1)
-    held = [gram_ref[i * w : (i + 1) * w, :] for i in range(n // w)]
+    main, below = gram_ref[:k, :], gram_ref[k:, :]
+    sy, sz, zz = main[:, k : 2 * k], main[:, 2 * k : 3 * k], main[:, 3 * k :]
+    cut = jnp.concatenate([below[:, : 2 * k], below[:, 2 * k :]], axis=0)
+    yz = cut[:, k:]
+    zero = jnp.zeros((k, k), F32)
+    upper[:k] = main
+    upper[k : 2 * k] = jnp.concatenate([sy.T, cut, zero], axis=1)
+    upper[2 * k :] = jnp.concatenate([sz.T, yz.T, zz, zero], axis=1)
+    held = [upper[i * w : (i + 1) * w, :] for i in range(n // w)]
+    for i in range(k // w):
+        held[i] = jnp.where(lane < n, held[i], 0.0)
 
     def spread(x):
         return jnp.broadcast_to(x, shape)
@@ -178,7 +177,6 @@
     held_shape = (blocks, k, edge)
     smem = pl.BlockSpec(memory_space=pltpu.SMEM)
     vmem = pl.BlockSpec(memory_space=pltpu.VMEM)
-    hbm = pl.BlockSpec(memory_space=pltpu.HBM)
     block_shape = jax.ShapeDtypeStruct(held_shape, F32)
     params = pltpu.CompilerParams(vmem_limit_bytes=VMEM_LIMIT)
     cost = pl.CostEstimate(
@@ -188,17 +186,11 @@
     def scratch(sources, targets):
         return [pltpu.VMEM((sources, 2 * k, edge), BF16), pltpu.VMEM((targets + 1, k, edge), F32)]
 
-    held, meta = pl.pallas_call(
-        stage_kernel,
-        out_shape=[jax.ShapeDtypeStruct(tiles.shape, BF16), jax.ShapeDtypeStruct((3, slots), jnp.int32)],
-        in_specs=[hbm] * 5,
-        out_specs=[vmem, smem],
-        scratch_shapes=[pltpu.SMEM((1, 1, slots), jnp.int32)] * 3
-        + [pltpu.SMEM((1, 1), jnp.int32), pltpu.SemaphoreType.DMA((5,))],
-        compiler_params=params,
-        cost_estimate=pl.CostEstimate(flops=0, bytes_accessed=2 * slots * edge * edge, transcendentals=0),
-    )(tile_row, tile_col, tile_round, tile_count, tiles)
-
+    member = lax.axis_index("rep")
+    column = lax.rem(member - tile_col[0, 0] + blocks, blocks)
+    row = lax.rem(member - tile_row[0, 0] + blocks, blocks)
+    live = (jnp.arange(slots, dtype=jnp.int32) < tile_count[0]).astype(jnp.int32)
+    meta = jnp.stack([tile_round[0, 0] * blocks + column, row, live], 0)
     backward = pl.pallas_call(
         backward_kernel,
         out_shape=[block_shape] * (ROUNDS + 1),
@@ -223,7 +215,7 @@
 
     def apply(q):
         _, quarter, _, last = offsets
-        kept, out32, out16, out8, out4 = backward(meta, held, q)
+        kept, out32, out16, out8, out4 = backward(meta, tiles, q)
         got4 = shifted(q, "rows", -last)
         got16 = shifted(q, "rows", -quarter)
         u = shifted(out8, "rows", last)
@@ -232,7 +224,7 @@
         got32 = shifted(got16, "rows", -quarter)
         v = shifted(out4 + u, "rows", last)
         x = shifted(out16 + w, "rows", quarter)
-        part = forward(meta, held, kept, q, got32, got16, got8, got4)
+        part = forward(meta, tiles, kept, q, got32, got16, got8, got4)
         return rep_sum(part + v + x)
 
     start = jnp.stack([start_block] + [shifted(start_block, "rep", by) for by in range(1, members)], 0)
@@ -240,15 +232,19 @@
     second = apply(first)
     gram = pl.pallas_call(
         gram_kernel,
-        out_shape=jax.ShapeDtypeStruct((3 * k, 4 * k), F32),
+        out_shape=jax.ShapeDtypeStruct((k + k // 2, 4 * k), F32),
         in_specs=[vmem] * 3,
         out_specs=vmem,
         compiler_params=params,
     )(start, first, second)
     gram = gram + moved(gram, "rows", lambda i: i ^ 1)
     gram = sum_of_ring(gram, lambda by: shifted(gram, "rows", by * (devices // 4)))
-    gram = gram + moved(gram, "rows", lambda i: i ^ 8)
-    gram = sum_of_ring(gram, lambda by: moved(gram, "rows", lambda i: (i & ~7) | ((i + 2 * by) & 7)))
+    def along_z(by):
+        return moved(gram, "rows", lambda i: (i & ~14) | ((i + (2 * by if i & 1 else -2 * by)) & 14))
+
+    near, middle, far, opposite = along_z(1), along_z(2), along_z(3), along_z(4)
+    near2, middle2, far2 = [moved(x, "rows", lambda i: i ^ 1) for x in (near, middle, far)]
+    gram = ((gram + opposite) + (middle + middle2)) + ((near + far2) + (far + near2))
     result, coefficients, factors = pl.pallas_call(
         tail_kernel,
         out_shape=[

time: 117 us -> 112 us (0.957)
  waiting for transfers between devices: 46.6 us -> 34 us
  starting transfers between devices: 49.1 us -> 58.3 us
  local copies, waits for them, and re-layouts: 4.21 us -> 2.25 us
  other arithmetic: 0.27 us -> 1.72 us
  Pallas kernels: 13.9 us -> 12.5 us
    ppermute x33 -> x36, waiting for transfers between devices: 46.6 us -> 34 us  [moved(): return lax.ppermute(x, axis, [(i, target(i) % size) for i in range(size)])]
    ppermute x33 -> x36, starting transfers between devices: 49.1 us -> 58.3 us  [moved(): return lax.ppermute(x, axis, [(i, target(i) % size) for i in range(size)])]
    unnamed x10 -> x2, local copies, waits for them, and re-layouts: 4.15 us -> 2.19 us
    pallas_call x6 -> x5, Pallas kernels: 9.12 us -> 7.54 us  [the longest x2 4.02 us: apply(): part = forward(meta, tiles, kept, q, got32, got16, got8, got4)]
  transfers between devices with their start and end apart: 33 -> 36, of which waited for: 17 -> 18; matrix products, arithmetic and copies ran while one was open for 0% -> 1% of each run, Pallas kernels for 7% -> 6%
where the time goes in v3:
time: 112 us; the launch traced here: 110 us
  starting transfers between devices  58.3 us (52%)
  waiting for transfers between devices  34 us (30%)
  Pallas kernels  12.5 us (11%)
  local copies, waits for them, and re-layouts  2.25 us (2%)
  other arithmetic  1.72 us (2%)
  between operations  1.51 us (1%)
    ppermute x36, starting transfers between devices, moved(): return lax.ppermute(x, axis, [(i, target(i) % size) for i in range(size)])  58.3 us
    ppermute x36, waiting for transfers between devices, moved(): return lax.ppermute(x, axis, [(i, target(i) % size) for i in range(size)])  34 us
    pallas_call x1, Pallas kernels, body(): pl.pallas_call(tail_kernel, out_shape=[jax.ShapeDtypeStruct((k, edge), F3...  4.92 us
    pallas_call x2, Pallas kernels, apply(): part = forward(meta, tiles, kept, q, got32, got16, got8, got4)  4.02 us
    pallas_call x2, Pallas kernels, apply(): kept, out32, out16, out8, out4 = backward(meta, tiles, q)  3 us
  transfers between devices with their start and end apart: 36, of which 18 were waited for; matrix products, arithmetic and copies ran while one was open for 1% of the time, Pallas kernels for 6%

profile of v3, /device:TPU:32, one launch (start us, length us, event | category | flops | bytes accessed | tf_op | source)
XLA Modules:
  0.0 110.3 jit_solution(506944862086708537)
XLA Ops:
  0.6 1.6 %collective-permute-start = (f32[32,256]{1,0:T(8,128)}, f32[32,256]{1,0:T(8,128)S(1)}, u32[]{:S(2)}, u32[]{:S(2)}) collective-permute-start(f32[32,256]{1,0:T(8,128)} %param.11), channel_id=1, source_target_pairs={{0,1},{1,2},{2,3},{3,0},{4,5},{5,6},{6,7},{7,4},{8,9},{9,10},{10,1... | collective-permute-start | bytes 98312 | tf_op jit(solution)/shard_map/ppermute | solution.py:157
  2.2 2.7 %collective-permute-start.1 = (f32[32,256]{1,0:T(8,128)}, f32[32,256]{1,0:T(8,128)S(1)}, u32[]{:S(2)}, u32[]{:S(2)}) collective-permute-start(f32[32,256]{1,0:T(8,128)} %param.11), channel_id=1, source_target_pairs={{0,2},{1,3},{2,0},{3,1},{4,6},{5,7},{6,4},{7,5},{8,10},{9,11},{10,... | collective-permute-start | bytes 98312 | tf_op jit(solution)/shard_map/ppermute | solution.py:157
  4.9 1.4 %collective-permute-start.2 = (f32[32,256]{1,0:T(8,128)}, f32[32,256]{1,0:T(8,128)S(1)}, u32[]{:S(2)}, u32[]{:S(2)}) collective-permute-start(f32[32,256]{1,0:T(8,128)} %param.11), channel_id=1, source_target_pairs={{0,3},{1,0},{2,1},{3,2},{4,7},{5,4},{6,5},{7,6},{8,11},{9,8},{10,9... | collective-permute-start | bytes 98312 | tf_op jit(solution)/shard_map/ppermute | solution.py:157
  9.8 3.1 %collective-permute-start.3 = (f32[4,32,256]{2,1,0:T(8,128)S(1)}, f32[4,32,256]{2,1,0:T(8,128)S(1)}, u32[]{:S(2)}, u32[]{:S(2)}) collective-permute-start(f32[4,32,256]{2,1,0:T(8,128)S(1)} %pad_maximum_fusion.q_ref.rest_0_.s_ref), channel_id=1, source_target_pairs={{0,192},{4,196},{8,200},{12,204},{16,208},{20,212},{24,216},{28,22... | collective-permute-start | bytes 393224 | tf_op jit(solution)/shard_map/ppermute | solution.py:157
  12.9 5.6 %collective-permute-start.5 = (f32[4,32,256]{2,1,0:T(8,128)S(1)}, f32[4,32,256]{2,1,0:T(8,128)S(1)}, u32[]{:S(2)}, u32[]{:S(2)}) collective-permute-start(f32[4,32,256]{2,1,0:T(8,128)S(1)} %pad_maximum_fusion.q_ref.rest_0_.s_ref), channel_id=1, source_target_pairs={{0,240},{4,244},{8,248},{12,252},{16,0},{20,4},{24,8},{28,12},{32,... | collective-permute-start | bytes 393224 | tf_op jit(solution)/shard_map/ppermute | solution.py:157
  18.5 2.2 %copy-done = bf16[1,1,32,256,256]{4,3,2,1,0:T(8,128)(2,1)S(1)} copy-done((bf16[1,1,32,256,256]{4,3,2,1,0:T(8,128)(2,1)S(1)}, bf16[1,1,32,256,256]{4,3,2,1,0:T(8,128)(2,1)}, u32[]{:S(2)}) %copy-start) | copy-done | bytes 4194328
  20.7 1.5 %shard_map.85 = (f32[4,32,256]{2,1,0:T(8,128)S(1)}, f32[4,32,256]{2,1,0:T(8,128)S(1)}, f32[4,32,256]{2,1,0:T(8,128)S(1)}, f32[4,32,256]{2,1,0:T(8,128)S(1)}, f32[4,32,256]{2,1,0:T(8,128)S(1)}) custom-call(s32[3,32]{1,0:T(4,128)S(1)} %pad_add_fusion.meta, bf16[32,256,256]{2,1,0:T(8,128)(2,1)S(1)} %bitcast.14, ...), custom_call_target="tpu_custom_call" | custom-call | flops 268435456 | bytes 4194304 | tf_op jit(solution)/shard_map/pallas_call | solution.py:218
  22.3 1.4 %collective-permute-start.9 = (f32[4,32,256]{2,1,0:T(8,128)S(1)}, f32[4,32,256]{2,1,0:T(8,128)S(1)}, u32[]{:S(2)}, u32[]{:S(2)}) collective-permute-start(f32[4,32,256]{2,1,0:T(8,128)S(1)} %get-tuple-element.20), channel_id=1, source_target_pairs={{0,64},{4,68},{8,72},{12,76},{16,80},{20,84},{24,88},{28,92},{32,9... | collective-permute-start | bytes 393224 | tf_op jit(solution)/shard_map/ppermute | solution.py:157
  23.6 2.0 %collective-permute-start.4 = (f32[4,32,256]{2,1,0:T(8,128)S(1)}, f32[4,32,256]{2,1,0:T(8,128)S(1)}, u32[]{:S(2)}, u32[]{:S(2)}) collective-permute-start(f32[4,32,256]{2,1,0:T(8,128)S(1)} %collective-permute-done.3.rest_2_), channel_id=1, source_target_pairs={{0,192},{4,196},{8,200},{12,204},{16,208},{20,212},{24,216},{28,22... | collective-permute-start | bytes 393224 | tf_op jit(solution)/shard_map/ppermute | solution.py:157
  25.6 4.9 %collective-permute-start.6 = (f32[4,32,256]{2,1,0:T(8,128)S(1)}, f32[4,32,256]{2,1,0:T(8,128)S(1)}, u32[]{:S(2)}, u32[]{:S(2)}) collective-permute-start(f32[4,32,256]{2,1,0:T(8,128)S(1)} %collective-permute-done.5.rest_4_), channel_id=1, source_target_pairs={{0,240},{4,244},{8,248},{12,252},{16,0},{20,4},{24,8},{28,12},{32,... | collective-permute-start | bytes 393224 | tf_op jit(solution)/shard_map/ppermute | solution.py:157
  30.6 2.1 %collective-permute-done.7 = f32[4,32,256]{2,1,0:T(8,128)S(1)} collective-permute-done((f32[4,32,256]{2,1,0:T(8,128)S(1)}, f32[4,32,256]{2,1,0:T(8,128)S(1)}, u32[]{:S(2)}, u32[]{:S(2)}) %collective-permute-start.7) | collective-permute-done | bytes 131104 | tf_op jit(solution)/shard_map/ppermute | solution.py:157
  33.6 2.0 %shard_map.86 = f32[4,32,256]{2,1,0:T(8,128)S(1)} custom-call(s32[3,32]{1,0:T(4,128)S(1)} %pad_add_fusion.meta, bf16[32,256,256]{2,1,0:T(8,128)(2,1)S(1)} %bitcast.15, f32[4,32,256]{2,1,0:T(8,128)S(1)} %get-tuple-element.16.kept_ref, f32[4,32,256]{2,1,0:T(8,128)S(1)} %pad_maximum_fusion.q_ref.rest_0_.s_ref, ...), custom_call_target="tpu_custom_call" | custom-call | flops 268435456 | bytes 4194304 | tf_op jit(solution)/shard_map/pallas_call | solution.py:227
  35.6 7.7 %collective-permute-done.8 = f32[4,32,256]{2,1,0:T(8,128)S(1)} collective-permute-done((f32[4,32,256]{2,1,0:T(8,128)S(1)}, f32[4,32,256]{2,1,0:T(8,128)S(1)}, u32[]{:S(2)}, u32[]{:S(2)}) %collective-permute-start.8) | collective-permute-done | bytes 131104 | tf_op jit(solution)/shard_map/ppermute | solution.py:157
  43.6 3.1 %collective-permute-start.13 = (f32[4,32,256]{2,1,0:T(8,128)S(1)}, f32[4,32,256]{2,1,0:T(8,128)S(1)}, u32[]{:S(2)}, u32[]{:S(2)}) collective-permute-start(f32[4,32,256]{2,1,0:T(8,128)S(1)} %add_add_fusion.1), channel_id=1, source_target_pairs={{0,3},{1,0},{2,1},{3,2},{4,7},{5,4},{6,5},{7,6},{8,11},{9,8},{10,9... | collective-permute-start | bytes 393224 | tf_op jit(solution)/shard_map/ppermute | solution.py:157
  46.9 2.7 %collective-permute-done.12 = f32[4,32,256]{2,1,0:T(8,128)S(1)} collective-permute-done((f32[4,32,256]{2,1,0:T(8,128)S(1)}, f32[4,32,256]{2,1,0:T(8,128)S(1)}, u32[]{:S(2)}, u32[]{:S(2)}) %collective-permute-start.12) | collective-permute-done | bytes 131104 | tf_op jit(solution)/shard_map/ppermute | solution.py:157
  50.7 2.5 %collective-permute-done.11 = f32[4,32,256]{2,1,0:T(8,128)S(1)} collective-permute-done((f32[4,32,256]{2,1,0:T(8,128)S(1)}, f32[4,32,256]{2,1,0:T(8,128)S(1)}, u32[]{:S(2)}, u32[]{:S(2)}) %collective-permute-start.11) | collective-permute-done | bytes 131104 | tf_op jit(solution)/shard_map/ppermute | solution.py:157
  54.3 1.5 %shard_map.87 = (f32[4,32,256]{2,1,0:T(8,128)S(1)}, f32[4,32,256]{2,1,0:T(8,128)S(1)}, f32[4,32,256]{2,1,0:T(8,128)S(1)}, f32[4,32,256]{2,1,0:T(8,128)S(1)}, f32[4,32,256]{2,1,0:T(8,128)S(1)}) custom-call(s32[3,32]{1,0:T(4,128)S(1)} %pad_add_fusion.meta, bf16[32,256,256]{2,1,0:T(8,128)(2,1)S(1)} %bitcast.16, f32[4,32,256]{2,1,0:T(8,128)S(1)} %fusion.q_ref.rest_0_.y_ref), custom_call_target="tpu_custom_call" | custom-call | flops 268435456 | bytes 4194304 | tf_op jit(solution)/shard_map/pallas_call | solution.py:218
  55.8 2.3 %collective-permute-start.18 = (f32[4,32,256]{2,1,0:T(8,128)S(1)}, f32[4,32,256]{2,1,0:T(8,128)S(1)}, u32[]{:S(2)}, u32[]{:S(2)}) collective-permute-start(f32[4,32,256]{2,1,0:T(8,128)S(1)} %get-tuple-element.23), channel_id=1, source_target_pairs={{0,16},{4,20},{8,24},{12,28},{16,32},{20,36},{24,40},{28,44},{32,4... | collective-permute-start | bytes 393224 | tf_op jit(solution)/shard_map/ppermute | solution.py:157
  58.1 1.9 %collective-permute-start.20 = (f32[4,32,256]{2,1,0:T(8,128)S(1)}, f32[4,32,256]{2,1,0:T(8,128)S(1)}, u32[]{:S(2)}, u32[]{:S(2)}) collective-permute-start(f32[4,32,256]{2,1,0:T(8,128)S(1)} %get-tuple-element.25), channel_id=1, source_target_pairs={{0,64},{4,68},{8,72},{12,76},{16,80},{20,84},{24,88},{28,92},{32,9... | collective-permute-start | bytes 393224 | tf_op jit(solution)/shard_map/ppermute | solution.py:157
  61.6 5.1 %collective-permute-start.17 = (f32[4,32,256]{2,1,0:T(8,128)S(1)}, f32[4,32,256]{2,1,0:T(8,128)S(1)}, u32[]{:S(2)}, u32[]{:S(2)}) collective-permute-start(f32[4,32,256]{2,1,0:T(8,128)S(1)} %collective-permute-done.16.rest_4_), channel_id=1, source_target_pairs={{0,240},{4,244},{8,248},{12,252},{16,0},{20,4},{24,8},{28,12},{32,... | collective-permute-start | bytes 393224 | tf_op jit(solution)/shard_map/ppermute | solution.py:157
  69.2 2.0 %shard_map.88 = f32[4,32,256]{2,1,0:T(8,128)S(1)} custom-call(s32[3,32]{1,0:T(4,128)S(1)} %pad_add_fusion.meta, bf16[32,256,256]{2,1,0:T(8,128)(2,1)S(1)} %bitcast.17, f32[4,32,256]{2,1,0:T(8,128)S(1)} %get-tuple-element.21.kept_ref, f32[4,32,256]{2,1,0:T(8,128)S(1)} %fusion.q_ref.rest_0_.y_ref, f32[4,32,256]{2,1,0:T(8,128)S(1)} %collective-permute-done.15.rest_1_, ...), custom_call_target="tpu_custom_call" | custom-call | flops 268435456 | bytes 4194304 | tf_op jit(solution)/shard_map/pallas_call | solution.py:227
  71.3 4.7 %collective-permute-done.19 = f32[4,32,256]{2,1,0:T(8,128)S(1)} collective-permute-done((f32[4,32,256]{2,1,0:T(8,128)S(1)}, f32[4,32,256]{2,1,0:T(8,128)S(1)}, u32[]{:S(2)}, u32[]{:S(2)}) %collective-permute-start.19) | collective-permute-done | bytes 131104 | tf_op jit(solution)/shard_map/ppermute | solution.py:157
  76.0 2.6 %collective-permute-start.23 = (f32[4,32,256]{2,1,0:T(8,128)S(1)}, f32[4,32,256]{2,1,0:T(8,128)S(1)}, u32[]{:S(2)}, u32[]{:S(2)}) collective-permute-start(f32[4,32,256]{2,1,0:T(8,128)S(1)} %add_add_fusion), channel_id=1, source_target_pairs={{0,1},{1,2},{2,3},{3,0},{4,5},{5,6},{6,7},{7,4},{8,9},{9,10},{10,1... | collective-permute-start | bytes 393224 | tf_op jit(solution)/shard_map/ppermute | solution.py:157
  79.3 1.7 %collective-permute-start.22 = (f32[4,32,256]{2,1,0:T(8,128)S(1)}, f32[4,32,256]{2,1,0:T(8,128)S(1)}, u32[]{:S(2)}, u32[]{:S(2)}) collective-permute-start(f32[4,32,256]{2,1,0:T(8,128)S(1)} %add_add_fusion), channel_id=1, source_target_pairs={{0,2},{1,3},{2,0},{3,1},{4,6},{5,7},{6,4},{7,5},{8,10},{9,11},{10,... | collective-permute-start | bytes 393224 | tf_op jit(solution)/shard_map/ppermute | solution.py:157
  83.6 2.2 %collective-permute-done.22 = f32[4,32,256]{2,1,0:T(8,128)S(1)} collective-permute-done((f32[4,32,256]{2,1,0:T(8,128)S(1)}, f32[4,32,256]{2,1,0:T(8,128)S(1)}, u32[]{:S(2)}, u32[]{:S(2)}) %collective-permute-start.22) | collective-permute-done | bytes 131104 | tf_op jit(solution)/shard_map/ppermute | solution.py:157
  89.2 2.4 %collective-permute-start.28 = (f32[48,128]{1,0:T(8,128)S(1)}, f32[48,128]{1,0:T(8,128)S(1)}, u32[]{:S(2)}, u32[]{:S(2)}) collective-permute-start(f32[48,128]{1,0:T(8,128)S(1)} %add.130), channel_id=1, source_target_pairs={{0,192},{4,196},{8,200},{12,204},{16,208},{20,212},{24,216},{28,22... | collective-permute-start | bytes 73736 | tf_op jit(solution)/shard_map/ppermute | solution.py:157
  91.7 1.3 %collective-permute-done.26 = f32[48,128]{1,0:T(8,128)S(1)} collective-permute-done((f32[48,128]{1,0:T(8,128)S(1)}, f32[48,128]{1,0:T(8,128)S(1)}, u32[]{:S(2)}, u32[]{:S(2)}) %collective-permute-start.26) | collective-permute-done | bytes 24608 | tf_op jit(solution)/shard_map/ppermute | solution.py:157
  93.5 1.8 %collective-permute-start.30 = (f32[48,128]{1,0:T(8,128)S(1)}, f32[48,128]{1,0:T(8,128)S(1)}, u32[]{:S(2)}, u32[]{:S(2)}) collective-permute-start(f32[48,128]{1,0:T(8,128)S(1)} %add_add_fusion.3), channel_id=1, source_target_pairs={{0,48},{4,20},{8,56},{12,28},{16,0},{20,36},{24,8},{28,44},{32,16}... | collective-permute-start | bytes 73736 | tf_op jit(solution)/shard_map/ppermute | solution.py:157
  95.3 1.6 %collective-permute-start.33 = (f32[48,128]{1,0:T(8,128)S(1)}, f32[48,128]{1,0:T(8,128)S(1)}, u32[]{:S(2)}, u32[]{:S(2)}) collective-permute-start(f32[48,128]{1,0:T(8,128)S(1)} %add_add_fusion.3), channel_id=1, source_target_pairs={{0,40},{4,28},{8,48},{12,36},{16,56},{20,44},{24,0},{28,52},{32,8}... | collective-permute-start | bytes 73736 | tf_op jit(solution)/shard_map/ppermute | solution.py:157
  97.4 4.4 %collective-permute-start.29 = (f32[48,128]{1,0:T(8,128)S(1)}, f32[48,128]{1,0:T(8,128)S(1)}, u32[]{:S(2)}, u32[]{:S(2)}) collective-permute-start(f32[48,128]{1,0:T(8,128)S(1)} %add_add_fusion.3), channel_id=1, source_target_pairs={{0,32},{4,36},{8,40},{12,44},{16,48},{20,52},{24,56},{28,60},{32,0... | collective-permute-start | bytes 73736 | tf_op jit(solution)/shard_map/ppermute | solution.py:157
  102.6 2.7 %collective-permute-done.29 = f32[48,128]{1,0:T(8,128)S(1)} collective-permute-done((f32[48,128]{1,0:T(8,128)S(1)}, f32[48,128]{1,0:T(8,128)S(1)}, u32[]{:S(2)}, u32[]{:S(2)}) %collective-permute-start.29) | collective-permute-done | bytes 24608 | tf_op jit(solution)/shard_map/ppermute | solution.py:157
  105.4 4.9 %shard_map.90 = (f32[32,256]{1,0:T(8,128)}, f32[2,32,64]{2,1,0:T(8,128)}, f32[2,32,32]{2,1,0:T(8,128)}) custom-call(f32[48,128]{1,0:T(8,128)S(1)} %add_add_fusion.2.gram_ref, f32[4,32,256]{2,1,0:T(8,128)S(1)} %pad_maximum_fusion.q_ref.rest_0_.s_ref, f32[4,32,256]{2,1,0:T(8,128)S(1)} %fusion.q_ref.rest_0_.y_ref, f32[4,32,256]{2,1,0:T(8,128)S(1)} %fusion.1.z_ref), custom_call_target="tpu_custom_call" | custom-call | tf_op jit(solution)/shard_map/pallas_call | solution.py:248
  (73 shorter events, 19.0 us)
Async XLA Ops:
  0.6 7.1 %collective-permute-start = (f32[32,256]{1,0:T(8,128)}, f32[32,256]{1,0:T(8,128)S(1)}, u32[]{:S(2)}, u32[]{:S(2)}) collective-permute-start(f32[32,256]{1,0:T(8,128)} %param.11), channel_id=1, source_target_pairs={{0,1},{1,2},{2,3},{3,0},{4,5},{5,6},{6,7},{7,4},{8,9},{9,10},{10,1... | collective-permute-start | bytes 98312 | tf_op jit(solution)/shard_map/ppermute | solution.py:157
  2.2 5.6 %collective-permute-start.1 = (f32[32,256]{1,0:T(8,128)}, f32[32,256]{1,0:T(8,128)S(1)}, u32[]{:S(2)}, u32[]{:S(2)}) collective-permute-start(f32[32,256]{1,0:T(8,128)} %param.11), channel_id=1, source_target_pairs={{0,2},{1,3},{2,0},{3,1},{4,6},{5,7},{6,4},{7,5},{8,10},{9,11},{10,... | collective-permute-start | bytes 98312 | tf_op jit(solution)/shard_map/ppermute | solution.py:157
  4.9 4.1 %collective-permute-start.2 = (f32[32,256]{1,0:T(8,128)}, f32[32,256]{1,0:T(8,128)S(1)}, u32[]{:S(2)}, u32[]{:S(2)}) collective-permute-start(f32[32,256]{1,0:T(8,128)} %param.11), channel_id=1, source_target_pairs={{0,3},{1,0},{2,1},{3,2},{4,7},{5,4},{6,5},{7,6},{8,11},{9,8},{10,9... | collective-permute-start | bytes 98312 | tf_op jit(solution)/shard_map/ppermute | solution.py:157
  9.8 13.8 %collective-permute-start.3 = (f32[4,32,256]{2,1,0:T(8,128)S(1)}, f32[4,32,256]{2,1,0:T(8,128)S(1)}, u32[]{:S(2)}, u32[]{:S(2)}) collective-permute-start(f32[4,32,256]{2,1,0:T(8,128)S(1)} %pad_maximum_fusion.q_ref.rest_0_.s_ref), channel_id=1, source_target_pairs={{0,192},{4,196},{8,200},{12,204},{16,208},{20,212},{24,216},{28,22... | collective-permute-start | bytes 393224 | tf_op jit(solution)/shard_map/ppermute | solution.py:157
  12.9 12.7 %collective-permute-start.5 = (f32[4,32,256]{2,1,0:T(8,128)S(1)}, f32[4,32,256]{2,1,0:T(8,128)S(1)}, u32[]{:S(2)}, u32[]{:S(2)}) collective-permute-start(f32[4,32,256]{2,1,0:T(8,128)S(1)} %pad_maximum_fusion.q_ref.rest_0_.s_ref), channel_id=1, source_target_pairs={{0,240},{4,244},{8,248},{12,252},{16,0},{20,4},{24,8},{28,12},{32,... | collective-permute-start | bytes 393224 | tf_op jit(solution)/shard_map/ppermute | solution.py:157
  22.2 10.5 %collective-permute-start.7 = (f32[4,32,256]{2,1,0:T(8,128)S(1)}, f32[4,32,256]{2,1,0:T(8,128)S(1)}, u32[]{:S(2)}, u32[]{:S(2)}) collective-permute-start(f32[4,32,256]{2,1,0:T(8,128)S(1)} %get-tuple-element.18), channel_id=1, source_target_pairs={{0,16},{4,20},{8,24},{12,28},{16,32},{20,36},{24,40},{28,44},{32,4... | collective-permute-start | bytes 393224 | tf_op jit(solution)/shard_map/ppermute | solution.py:157
  22.3 10.5 %collective-permute-start.9 = (f32[4,32,256]{2,1,0:T(8,128)S(1)}, f32[4,32,256]{2,1,0:T(8,128)S(1)}, u32[]{:S(2)}, u32[]{:S(2)}) collective-permute-start(f32[4,32,256]{2,1,0:T(8,128)S(1)} %get-tuple-element.20), channel_id=1, source_target_pairs={{0,64},{4,68},{8,72},{12,76},{16,80},{20,84},{24,88},{28,92},{32,9... | collective-permute-start | bytes 393224 | tf_op jit(solution)/shard_map/ppermute | solution.py:157
  23.6 10.0 %collective-permute-start.4 = (f32[4,32,256]{2,1,0:T(8,128)S(1)}, f32[4,32,256]{2,1,0:T(8,128)S(1)}, u32[]{:S(2)}, u32[]{:S(2)}) collective-permute-start(f32[4,32,256]{2,1,0:T(8,128)S(1)} %collective-permute-done.3.rest_2_), channel_id=1, source_target_pairs={{0,192},{4,196},{8,200},{12,204},{16,208},{20,212},{24,216},{28,22... | collective-permute-start | bytes 393224 | tf_op jit(solution)/shard_map/ppermute | solution.py:157
  25.6 8.0 %collective-permute-start.6 = (f32[4,32,256]{2,1,0:T(8,128)S(1)}, f32[4,32,256]{2,1,0:T(8,128)S(1)}, u32[]{:S(2)}, u32[]{:S(2)}) collective-permute-start(f32[4,32,256]{2,1,0:T(8,128)S(1)} %collective-permute-done.5.rest_4_), channel_id=1, source_target_pairs={{0,240},{4,244},{8,248},{12,252},{16,0},{20,4},{24,8},{28,12},{32,... | collective-permute-start | bytes 393224 | tf_op jit(solution)/shard_map/ppermute | solution.py:157
  32.7 10.7 %collective-permute-start.8 = (f32[4,32,256]{2,1,0:T(8,128)S(1)}, f32[4,32,256]{2,1,0:T(8,128)S(1)}, u32[]{:S(2)}, u32[]{:S(2)}) collective-permute-start(f32[4,32,256]{2,1,0:T(8,128)S(1)} %add.116), channel_id=1, source_target_pairs={{0,16},{4,20},{8,24},{12,28},{16,32},{20,36},{24,40},{28,44},{32,4... | collective-permute-start | bytes 393224 | tf_op jit(solution)/shard_map/ppermute | solution.py:157
  32.8 10.5 %collective-permute-start.10 = (f32[4,32,256]{2,1,0:T(8,128)S(1)}, f32[4,32,256]{2,1,0:T(8,128)S(1)}, u32[]{:S(2)}, u32[]{:S(2)}) collective-permute-start(f32[4,32,256]{2,1,0:T(8,128)S(1)} %add.118), channel_id=1, source_target_pairs={{0,64},{4,68},{8,72},{12,76},{16,80},{20,84},{24,88},{28,92},{32,9... | collective-permute-start | bytes 393224 | tf_op jit(solution)/shard_map/ppermute | solution.py:157
  43.4 6.3 %collective-permute-start.12 = (f32[4,32,256]{2,1,0:T(8,128)S(1)}, f32[4,32,256]{2,1,0:T(8,128)S(1)}, u32[]{:S(2)}, u32[]{:S(2)}) collective-permute-start(f32[4,32,256]{2,1,0:T(8,128)S(1)} %add_add_fusion.1), channel_id=1, source_target_pairs={{0,1},{1,2},{2,3},{3,0},{4,5},{5,6},{6,7},{7,4},{8,9},{9,10},{10,1... | collective-permute-start | bytes 393224 | tf_op jit(solution)/shard_map/ppermute | solution.py:157
  43.6 7.0 %collective-permute-start.13 = (f32[4,32,256]{2,1,0:T(8,128)S(1)}, f32[4,32,256]{2,1,0:T(8,128)S(1)}, u32[]{:S(2)}, u32[]{:S(2)}) collective-permute-start(f32[4,32,256]{2,1,0:T(8,128)S(1)} %add_add_fusion.1), channel_id=1, source_target_pairs={{0,3},{1,0},{2,1},{3,2},{4,7},{5,4},{6,5},{7,6},{8,11},{9,8},{10,9... | collective-permute-start | bytes 393224 | tf_op jit(solution)/shard_map/ppermute | solution.py:157
  46.7 6.5 %collective-permute-start.11 = (f32[4,32,256]{2,1,0:T(8,128)S(1)}, f32[4,32,256]{2,1,0:T(8,128)S(1)}, u32[]{:S(2)}, u32[]{:S(2)}) collective-permute-start(f32[4,32,256]{2,1,0:T(8,128)S(1)} %add_add_fusion.1), channel_id=1, source_target_pairs={{0,2},{1,3},{2,0},{3,1},{4,6},{5,7},{6,4},{7,5},{8,10},{9,11},{10,... | collective-permute-start | bytes 393224 | tf_op jit(solution)/shard_map/ppermute | solution.py:157
  53.3 6.8 %collective-permute-start.14 = (f32[4,32,256]{2,1,0:T(8,128)S(1)}, f32[4,32,256]{2,1,0:T(8,128)S(1)}, u32[]{:S(2)}, u32[]{:S(2)}) collective-permute-start(f32[4,32,256]{2,1,0:T(8,128)S(1)} %fusion.q_ref.rest_0_.y_ref), channel_id=1, source_target_pairs={{0,192},{4,196},{8,200},{12,204},{16,208},{20,212},{24,216},{28,22... | collective-permute-start | bytes 393224 | tf_op jit(solution)/shard_map/ppermute | solution.py:157
  53.5 8.1 %collective-permute-start.16 = (f32[4,32,256]{2,1,0:T(8,128)S(1)}, f32[4,32,256]{2,1,0:T(8,128)S(1)}, u32[]{:S(2)}, u32[]{:S(2)}) collective-permute-start(f32[4,32,256]{2,1,0:T(8,128)S(1)} %fusion.q_ref.rest_0_.y_ref), channel_id=1, source_target_pairs={{0,240},{4,244},{8,248},{12,252},{16,0},{20,4},{24,8},{28,12},{32,... | collective-permute-start | bytes 393224 | tf_op jit(solution)/shard_map/ppermute | solution.py:157
  55.8 10.8 %collective-permute-start.18 = (f32[4,32,256]{2,1,0:T(8,128)S(1)}, f32[4,32,256]{2,1,0:T(8,128)S(1)}, u32[]{:S(2)}, u32[]{:S(2)}) collective-permute-start(f32[4,32,256]{2,1,0:T(8,128)S(1)} %get-tuple-element.23), channel_id=1, source_target_pairs={{0,16},{4,20},{8,24},{12,28},{16,32},{20,36},{24,40},{28,44},{32,4... | collective-permute-start | bytes 393224 | tf_op jit(solution)/shard_map/ppermute | solution.py:157
  58.1 9.5 %collective-permute-start.20 = (f32[4,32,256]{2,1,0:T(8,128)S(1)}, f32[4,32,256]{2,1,0:T(8,128)S(1)}, u32[]{:S(2)}, u32[]{:S(2)}) collective-permute-start(f32[4,32,256]{2,1,0:T(8,128)S(1)} %get-tuple-element.25), channel_id=1, source_target_pairs={{0,64},{4,68},{8,72},{12,76},{16,80},{20,84},{24,88},{28,92},{32,9... | collective-permute-start | bytes 393224 | tf_op jit(solution)/shard_map/ppermute | solution.py:157
  60.1 8.3 %collective-permute-start.15 = (f32[4,32,256]{2,1,0:T(8,128)S(1)}, f32[4,32,256]{2,1,0:T(8,128)S(1)}, u32[]{:S(2)}, u32[]{:S(2)}) collective-permute-start(f32[4,32,256]{2,1,0:T(8,128)S(1)} %collective-permute-done.14.rest_2_), channel_id=1, source_target_pairs={{0,192},{4,196},{8,200},{12,204},{16,208},{20,212},{24,216},{28,22... | collective-permute-start | bytes 393224 | tf_op jit(solution)/shard_map/ppermute | solution.py:157
  61.6 7.7 %collective-permute-start.17 = (f32[4,32,256]{2,1,0:T(8,128)S(1)}, f32[4,32,256]{2,1,0:T(8,128)S(1)}, u32[]{:S(2)}, u32[]{:S(2)}) collective-permute-start(f32[4,32,256]{2,1,0:T(8,128)S(1)} %collective-permute-done.16.rest_4_), channel_id=1, source_target_pairs={{0,240},{4,244},{8,248},{12,252},{16,0},{20,4},{24,8},{28,12},{32,... | collective-permute-start | bytes 393224 | tf_op jit(solution)/shard_map/ppermute | solution.py:157
  66.7 9.3 %collective-permute-start.19 = (f32[4,32,256]{2,1,0:T(8,128)S(1)}, f32[4,32,256]{2,1,0:T(8,128)S(1)}, u32[]{:S(2)}, u32[]{:S(2)}) collective-permute-start(f32[4,32,256]{2,1,0:T(8,128)S(1)} %add.123), channel_id=1, source_target_pairs={{0,16},{4,20},{8,24},{12,28},{16,32},{20,36},{24,40},{28,44},{32,4... | collective-permute-start | bytes 393224 | tf_op jit(solution)/shard_map/ppermute | solution.py:157
  67.7 8.3 %collective-permute-start.21 = (f32[4,32,256]{2,1,0:T(8,128)S(1)}, f32[4,32,256]{2,1,0:T(8,128)S(1)}, u32[]{:S(2)}, u32[]{:S(2)}) collective-permute-start(f32[4,32,256]{2,1,0:T(8,128)S(1)} %add.125), channel_id=1, source_target_pairs={{0,64},{4,68},{8,72},{12,76},{16,80},{20,84},{24,88},{28,92},{32,9... | collective-permute-start | bytes 393224 | tf_op jit(solution)/shard_map/ppermute | solution.py:157
  76.0 6.3 %collective-permute-start.23 = (f32[4,32,256]{2,1,0:T(8,128)S(1)}, f32[4,32,256]{2,1,0:T(8,128)S(1)}, u32[]{:S(2)}, u32[]{:S(2)}) collective-permute-start(f32[4,32,256]{2,1,0:T(8,128)S(1)} %add_add_fusion), channel_id=1, source_target_pairs={{0,1},{1,2},{2,3},{3,0},{4,5},{5,6},{6,7},{7,4},{8,9},{9,10},{10,1... | collective-permute-start | bytes 393224 | tf_op jit(solution)/shard_map/ppermute | solution.py:157
  78.6 5.0 %collective-permute-start.24 = (f32[4,32,256]{2,1,0:T(8,128)S(1)}, f32[4,32,256]{2,1,0:T(8,128)S(1)}, u32[]{:S(2)}, u32[]{:S(2)}) collective-permute-start(f32[4,32,256]{2,1,0:T(8,128)S(1)} %add_add_fusion), channel_id=1, source_target_pairs={{0,3},{1,0},{2,1},{3,2},{4,7},{5,4},{6,5},{7,6},{8,11},{9,8},{10,9... | collective-permute-start | bytes 393224 | tf_op jit(solution)/shard_map/ppermute | solution.py:157
  79.3 6.5 %collective-permute-start.22 = (f32[4,32,256]{2,1,0:T(8,128)S(1)}, f32[4,32,256]{2,1,0:T(8,128)S(1)}, u32[]{:S(2)}, u32[]{:S(2)}) collective-permute-start(f32[4,32,256]{2,1,0:T(8,128)S(1)} %add_add_fusion), channel_id=1, source_target_pairs={{0,2},{1,3},{2,0},{3,1},{4,6},{5,7},{6,4},{7,5},{8,10},{9,11},{10,... | collective-permute-start | bytes 393224 | tf_op jit(solution)/shard_map/ppermute | solution.py:157
  87.7 5.3 %collective-permute-start.26 = (f32[48,128]{1,0:T(8,128)S(1)}, f32[48,128]{1,0:T(8,128)S(1)}, u32[]{:S(2)}, u32[]{:S(2)}) collective-permute-start(f32[48,128]{1,0:T(8,128)S(1)} %add.130), channel_id=1, source_target_pairs={{0,128},{4,132},{8,136},{12,140},{16,144},{20,148},{24,152},{28,15... | collective-permute-start | bytes 73736 | tf_op jit(solution)/shard_map/ppermute | solution.py:157
  88.4 5.0 %collective-permute-start.27 = (f32[48,128]{1,0:T(8,128)S(1)}, f32[48,128]{1,0:T(8,128)S(1)}, u32[]{:S(2)}, u32[]{:S(2)}) collective-permute-start(f32[48,128]{1,0:T(8,128)S(1)} %add.130), channel_id=1, source_target_pairs={{0,64},{4,68},{8,72},{12,76},{16,80},{20,84},{24,88},{28,92},{32,9... | collective-permute-start | bytes 73736 | tf_op jit(solution)/shard_map/ppermute | solution.py:157
  89.2 4.2 %collective-permute-start.28 = (f32[48,128]{1,0:T(8,128)S(1)}, f32[48,128]{1,0:T(8,128)S(1)}, u32[]{:S(2)}, u32[]{:S(2)}) collective-permute-start(f32[48,128]{1,0:T(8,128)S(1)} %add.130), channel_id=1, source_target_pairs={{0,192},{4,196},{8,200},{12,204},{16,208},{20,212},{24,216},{28,22... | collective-permute-start | bytes 73736 | tf_op jit(solution)/shard_map/ppermute | solution.py:157
  93.5 8.3 %collective-permute-start.30 = (f32[48,128]{1,0:T(8,128)S(1)}, f32[48,128]{1,0:T(8,128)S(1)}, u32[]{:S(2)}, u32[]{:S(2)}) collective-permute-start(f32[48,128]{1,0:T(8,128)S(1)} %add_add_fusion.3), channel_id=1, source_target_pairs={{0,48},{4,20},{8,56},{12,28},{16,0},{20,36},{24,8},{28,44},{32,16}... | collective-permute-start | bytes 73736 | tf_op jit(solution)/shard_map/ppermute | solution.py:157
  95.3 6.8 %collective-permute-start.33 = (f32[48,128]{1,0:T(8,128)S(1)}, f32[48,128]{1,0:T(8,128)S(1)}, u32[]{:S(2)}, u32[]{:S(2)}) collective-permute-start(f32[48,128]{1,0:T(8,128)S(1)} %add_add_fusion.3), channel_id=1, source_target_pairs={{0,40},{4,28},{8,48},{12,36},{16,56},{20,44},{24,0},{28,52},{32,8}... | collective-permute-start | bytes 73736 | tf_op jit(solution)/shard_map/ppermute | solution.py:157
  96.9 5.4 %collective-permute-start.32 = (f32[48,128]{1,0:T(8,128)S(1)}, f32[48,128]{1,0:T(8,128)S(1)}, u32[]{:S(2)}, u32[]{:S(2)}) collective-permute-start(f32[48,128]{1,0:T(8,128)S(1)} %add_add_fusion.3), channel_id=1, source_target_pairs={{0,56},{4,12},{8,0},{12,20},{16,8},{20,28},{24,16},{28,36},{32,24}... | collective-permute-start | bytes 73736 | tf_op jit(solution)/shard_map/ppermute | solution.py:157
  97.4 7.9 %collective-permute-start.29 = (f32[48,128]{1,0:T(8,128)S(1)}, f32[48,128]{1,0:T(8,128)S(1)}, u32[]{:S(2)}, u32[]{:S(2)}) collective-permute-start(f32[48,128]{1,0:T(8,128)S(1)} %add_add_fusion.3), channel_id=1, source_target_pairs={{0,32},{4,36},{8,40},{12,44},{16,48},{20,52},{24,56},{28,60},{32,0... | collective-permute-start | bytes 73736 | tf_op jit(solution)/shard_map/ppermute | solution.py:157
  (5 other events, 13.3 us)

commit v4 on v3

--- a/solution.py
+++ b/solution.py
@@ -27,6 +27,10 @@
     high = x.astype(BF16)
     low = (x - high.astype(F32)).astype(BF16)
     return jnp.concatenate([high, low], axis=0)
+
+
+def ready_kernel(tiles_ref, start_ref, start_out):
+    start_out[...] = start_ref[...]
 
 
 def backward_kernel(meta, held, q_ref, *rest):
@@ -102,6 +106,16 @@
 
     for j in range(n // w):
         at = j * w
+        if at == 2 * k:
+            x11, x22 = inverse[:k, :k], inverse[k : 2 * k, k : 2 * k]
+            u12, u13 = upper[:k, k : 2 * k], upper[:k, 2 * k : n]
+            u22, u23 = upper[k : 2 * k, k : 2 * k], upper[k : 2 * k, 2 * k : n]
+            fact_ref[0] = dot(x11, u22, NT, HIGHEST)
+            coef_ref[0, :, :k] = dot(x11, u12, NT, HIGHEST)
+            coef_ref[0, :, k:] = jnp.zeros((k, k), F32)
+            v = dot(x11, u12, TN, HIGHEST)
+            coef_ref[1, :, :k] = dot(x22, u23 - dot(u22, v, NN, HIGHEST), NT, HIGHEST)
+            coef_ref[1, :, k:] = dot(x22, u13 - dot(u12, v, NN, HIGHEST), NT, HIGHEST)
         inside = (lane >= at) & (lane < at + w)
         columns = [spread(held[j][:, at + c : at + c + 1]) for c in range(w)]
         p = [[spread(columns[b][a : a + 1, :]) if a <= b else None for b in range(w)] for a in range(w)]
@@ -136,20 +150,9 @@
                 diag = jnp.where(lane == at + b, p[a][b], diag)
             inverse[at + a : at + a + 1, :] = jnp.where(lane < at + w, row, 0.0)[:1]
             upper[at + a : at + a + 1, :] = jnp.where(lane >= at + w, row, diag * root)[:1]
-    x, u = inverse[...], upper[...]
-    u12, u13 = u[:k, k : 2 * k], u[:k, 2 * k : 3 * k]
-    u22, u23 = u[k : 2 * k, k : 2 * k], u[k : 2 * k, 2 * k : 3 * k]
-    u33 = u[2 * k : 3 * k, 2 * k : 3 * k]
-    x11, x22 = x[:k, :k], x[k : 2 * k, k : 2 * k]
-    fact_ref[0] = dot(x11, u22, NT, HIGHEST)
-    fact_ref[1] = dot(x22, u33, NT, HIGHEST)
-    coef_ref[0, :, :k] = dot(x11, u12, NT, HIGHEST)
-    coef_ref[0, :, k:] = jnp.zeros((k, k), F32)
-    v = dot(x11, u12, TN, HIGHEST)
-    coef_ref[1, :, :k] = dot(x22, u23 - dot(u22, v, NN, HIGHEST), NT, HIGHEST)
-    coef_ref[1, :, k:] = dot(x22, u13 - dot(u12, v, NN, HIGHEST), NT, HIGHEST)
+    fact_ref[1] = dot(x22, upper[2 * k :, 2 * k : n], NT, HIGHEST)
     stack = jnp.concatenate([s_ref[0], y_ref[0], z_ref[0]], axis=0)
-    next_ref[...] = dot(x[2 * k : 3 * k, : 3 * k], stack, NN, HIGHEST)
+    next_ref[...] = dot(inverse[2 * k :, :n], stack, NN, HIGHEST)
 
 
 def moved(x, axis, target):
@@ -191,6 +194,13 @@
     row = lax.rem(member - tile_row[0, 0] + blocks, blocks)
     live = (jnp.arange(slots, dtype=jnp.int32) < tile_count[0]).astype(jnp.int32)
     meta = jnp.stack([tile_round[0, 0] * blocks + column, row, live], 0)
+    own = pl.pallas_call(
+        ready_kernel,
+        out_shape=jax.ShapeDtypeStruct(start_block.shape, F32),
+        in_specs=[vmem, vmem],
+        out_specs=vmem,
+        compiler_params=params,
+    )(tiles, start_block)
     backward = pl.pallas_call(
         backward_kernel,
         out_shape=[block_shape] * (ROUNDS + 1),
@@ -227,7 +237,7 @@
         part = forward(meta, tiles, kept, q, got32, got16, got8, got4)
         return rep_sum(part + v + x)
 
-    start = jnp.stack([start_block] + [shifted(start_block, "rep", by) for by in range(1, members)], 0)
+    start = jnp.stack([own] + [shifted(start_block, "rep", by) for by in range(1, members)], 0)
     first = apply(start)
     second = apply(first)
     gram = pl.pallas_call(

time: 112 us -> 110 us (0.982)
  starting transfers between devices: 58.3 us -> 56.4 us
    ppermute x36, starting transfers between devices: 58.3 us -> 56.4 us  [moved(): return lax.ppermute(x, axis, [(i, target(i) % size) for i in range(size)])]
    ppermute x36, waiting for transfers between devices: 34 us -> 35.1 us  [moved(): return lax.ppermute(x, axis, [(i, target(i) % size) for i in range(size)])]
    unnamed x2 -> x4, local copies, waits for them, and re-layouts: 2.19 us -> 2.94 us
  transfers between devices with their start and end apart: 36 -> 36, of which waited for: 18 -> 15; matrix products, arithmetic and copies ran while one was open for 1% -> 1% of each run, Pallas kernels for 6% -> 6%
where the time goes in v4:
time: 110 us; the launch traced here: 109 us
  starting transfers between devices  56.4 us (51%)
  waiting for transfers between devices  35.1 us (32%)
  Pallas kernels  11.7 us (11%)
  local copies, waits for them, and re-layouts  3.01 us (3%)
  between operations  1.59 us (1%)
    ppermute x36, starting transfers between devices, moved(): return lax.ppermute(x, axis, [(i, target(i) % size) for i in range(size)])  56.4 us
    ppermute x36, waiting for transfers between devices, moved(): return lax.ppermute(x, axis, [(i, target(i) % size) for i in range(size)])  35.1 us
    pallas_call x1, Pallas kernels, body(): pl.pallas_call(tail_kernel, out_shape=[jax.ShapeDtypeStruct((k, edge), F3...  4.2 us
    pallas_call x2, Pallas kernels, apply(): part = forward(meta, tiles, kept, q, got32, got16, got8, got4)  4.01 us
    pallas_call x2, Pallas kernels, apply(): kept, out32, out16, out8, out4 = backward(meta, tiles, q)  2.95 us
    unnamed x4, local copies, waits for them, and re-layouts  2.94 us
  transfers between devices with their start and end apart: 36, of which 15 were waited for; matrix products, arithmetic and copies ran while one was open for 1% of the time, Pallas kernels for 6%

profile of v4, /device:TPU:32, one launch (start us, length us, event | category | flops | bytes accessed | tf_op | source)
XLA Modules:
  0.0 108.8 jit_solution(15612714128584405451)
XLA Ops:
  0.6 1.6 %collective-permute-start = (f32[32,256]{1,0:T(8,128)}, f32[32,256]{1,0:T(8,128)S(1)}, u32[]{:S(2)}, u32[]{:S(2)}) collective-permute-start(f32[32,256]{1,0:T(8,128)} %start_ref.1), channel_id=1, source_target_pairs={{0,1},{1,2},{2,3},{3,0},{4,5},{5,6},{6,7},{7,4},{8,9},{9,10},{10,1... | collective-permute-start | bytes 98312 | tf_op jit(solution)/shard_map/ppermute | solution.py:160
  2.2 2.7 %collective-permute-start.1 = (f32[32,256]{1,0:T(8,128)}, f32[32,256]{1,0:T(8,128)S(1)}, u32[]{:S(2)}, u32[]{:S(2)}) collective-permute-start(f32[32,256]{1,0:T(8,128)} %start_ref.1), channel_id=1, source_target_pairs={{0,2},{1,3},{2,0},{3,1},{4,6},{5,7},{6,4},{7,5},{8,10},{9,11},{10,... | collective-permute-start | bytes 98312 | tf_op jit(solution)/shard_map/ppermute | solution.py:160
  4.9 1.4 %collective-permute-start.2 = (f32[32,256]{1,0:T(8,128)}, f32[32,256]{1,0:T(8,128)S(1)}, u32[]{:S(2)}, u32[]{:S(2)}) collective-permute-start(f32[32,256]{1,0:T(8,128)} %start_ref.1), channel_id=1, source_target_pairs={{0,3},{1,0},{2,1},{3,2},{4,7},{5,4},{6,5},{7,6},{8,11},{9,8},{10,9... | collective-permute-start | bytes 98312 | tf_op jit(solution)/shard_map/ppermute | solution.py:160
  7.8 2.2 %copy-done = bf16[1,1,32,256,256]{4,3,2,1,0:T(8,128)(2,1)S(1)} copy-done((bf16[1,1,32,256,256]{4,3,2,1,0:T(8,128)(2,1)S(1)}, bf16[1,1,32,256,256]{4,3,2,1,0:T(8,128)(2,1)}, u32[]{:S(2)}) %copy-start) | copy-done | bytes 4194328
  10.7 3.1 %collective-permute-start.3 = (f32[4,32,256]{2,1,0:T(8,128)S(1)}, f32[4,32,256]{2,1,0:T(8,128)S(1)}, u32[]{:S(2)}, u32[]{:S(2)}) collective-permute-start(f32[4,32,256]{2,1,0:T(8,128)S(1)} %pad_maximum_fusion.q_ref.rest_0_.s_ref), channel_id=1, source_target_pairs={{0,192},{4,196},{8,200},{12,204},{16,208},{20,212},{24,216},{28,22... | collective-permute-start | bytes 393224 | tf_op jit(solution)/shard_map/ppermute | solution.py:160
  13.8 5.6 %collective-permute-start.5 = (f32[4,32,256]{2,1,0:T(8,128)S(1)}, f32[4,32,256]{2,1,0:T(8,128)S(1)}, u32[]{:S(2)}, u32[]{:S(2)}) collective-permute-start(f32[4,32,256]{2,1,0:T(8,128)S(1)} %pad_maximum_fusion.q_ref.rest_0_.s_ref), channel_id=1, source_target_pairs={{0,240},{4,244},{8,248},{12,252},{16,0},{20,4},{24,8},{28,12},{32,... | collective-permute-start | bytes 393224 | tf_op jit(solution)/shard_map/ppermute | solution.py:160
  19.4 1.5 %shard_map.86 = (f32[4,32,256]{2,1,0:T(8,128)S(1)}, f32[4,32,256]{2,1,0:T(8,128)S(1)}, f32[4,32,256]{2,1,0:T(8,128)S(1)}, f32[4,32,256]{2,1,0:T(8,128)S(1)}, f32[4,32,256]{2,1,0:T(8,128)S(1)}) custom-call(s32[3,32]{1,0:T(4,128)S(1)} %pad_add_fusion.meta, bf16[32,256,256]{2,1,0:T(8,128)(2,1)S(1)} %bitcast.15, ...), custom_call_target="tpu_custom_call" | custom-call | flops 268435456 | bytes 4194304 | tf_op jit(solution)/shard_map/pallas_call | solution.py:228
  21.0 1.3 %collective-permute-start.9 = (f32[4,32,256]{2,1,0:T(8,128)S(1)}, f32[4,32,256]{2,1,0:T(8,128)S(1)}, u32[]{:S(2)}, u32[]{:S(2)}) collective-permute-start(f32[4,32,256]{2,1,0:T(8,128)S(1)} %get-tuple-element.20), channel_id=1, source_target_pairs={{0,64},{4,68},{8,72},{12,76},{16,80},{20,84},{24,88},{28,92},{32,9... | collective-permute-start | bytes 393224 | tf_op jit(solution)/shard_map/ppermute | solution.py:160
  22.3 2.0 %collective-permute-start.4 = (f32[4,32,256]{2,1,0:T(8,128)S(1)}, f32[4,32,256]{2,1,0:T(8,128)S(1)}, u32[]{:S(2)}, u32[]{:S(2)}) collective-permute-start(f32[4,32,256]{2,1,0:T(8,128)S(1)} %collective-permute-done.3.rest_2_), channel_id=1, source_target_pairs={{0,192},{4,196},{8,200},{12,204},{16,208},{20,212},{24,216},{28,22... | collective-permute-start | bytes 393224 | tf_op jit(solution)/shard_map/ppermute | solution.py:160
  24.3 4.9 %collective-permute-start.6 = (f32[4,32,256]{2,1,0:T(8,128)S(1)}, f32[4,32,256]{2,1,0:T(8,128)S(1)}, u32[]{:S(2)}, u32[]{:S(2)}) collective-permute-start(f32[4,32,256]{2,1,0:T(8,128)S(1)} %collective-permute-done.5.rest_4_), channel_id=1, source_target_pairs={{0,240},{4,244},{8,248},{12,252},{16,0},{20,4},{24,8},{28,12},{32,... | collective-permute-start | bytes 393224 | tf_op jit(solution)/shard_map/ppermute | solution.py:160
  29.2 3.1 %collective-permute-done.7 = f32[4,32,256]{2,1,0:T(8,128)S(1)} collective-permute-done((f32[4,32,256]{2,1,0:T(8,128)S(1)}, f32[4,32,256]{2,1,0:T(8,128)S(1)}, u32[]{:S(2)}, u32[]{:S(2)}) %collective-permute-start.7) | collective-permute-done | bytes 131104 | tf_op jit(solution)/shard_map/ppermute | solution.py:160
  33.0 2.0 %shard_map.87 = f32[4,32,256]{2,1,0:T(8,128)S(1)} custom-call(s32[3,32]{1,0:T(4,128)S(1)} %pad_add_fusion.meta, bf16[32,256,256]{2,1,0:T(8,128)(2,1)S(1)} %bitcast.16, f32[4,32,256]{2,1,0:T(8,128)S(1)} %get-tuple-element.16.kept_ref, f32[4,32,256]{2,1,0:T(8,128)S(1)} %pad_maximum_fusion.q_ref.rest_0_.s_ref, ...), custom_call_target="tpu_custom_call" | custom-call | flops 268435456 | bytes 4194304 | tf_op jit(solution)/shard_map/pallas_call | solution.py:237
  35.0 7.1 %collective-permute-done.8 = f32[4,32,256]{2,1,0:T(8,128)S(1)} collective-permute-done((f32[4,32,256]{2,1,0:T(8,128)S(1)}, f32[4,32,256]{2,1,0:T(8,128)S(1)}, u32[]{:S(2)}, u32[]{:S(2)}) %collective-permute-start.8) | collective-permute-done | bytes 131104 | tf_op jit(solution)/shard_map/ppermute | solution.py:160
  42.8 2.6 %collective-permute-start.13 = (f32[4,32,256]{2,1,0:T(8,128)S(1)}, f32[4,32,256]{2,1,0:T(8,128)S(1)}, u32[]{:S(2)}, u32[]{:S(2)}) collective-permute-start(f32[4,32,256]{2,1,0:T(8,128)S(1)} %add_add_fusion.1), channel_id=1, source_target_pairs={{0,3},{1,0},{2,1},{3,2},{4,7},{5,4},{6,5},{7,6},{8,11},{9,8},{10,9... | collective-permute-start | bytes 393224 | tf_op jit(solution)/shard_map/ppermute | solution.py:160
  45.5 2.9 %collective-permute-done.12 = f32[4,32,256]{2,1,0:T(8,128)S(1)} collective-permute-done((f32[4,32,256]{2,1,0:T(8,128)S(1)}, f32[4,32,256]{2,1,0:T(8,128)S(1)}, u32[]{:S(2)}, u32[]{:S(2)}) %collective-permute-start.12) | collective-permute-done | bytes 131104 | tf_op jit(solution)/shard_map/ppermute | solution.py:160
  49.4 2.5 %collective-permute-done.11 = f32[4,32,256]{2,1,0:T(8,128)S(1)} collective-permute-done((f32[4,32,256]{2,1,0:T(8,128)S(1)}, f32[4,32,256]{2,1,0:T(8,128)S(1)}, u32[]{:S(2)}, u32[]{:S(2)}) %collective-permute-start.11) | collective-permute-done | bytes 131104 | tf_op jit(solution)/shard_map/ppermute | solution.py:160
  52.3 1.7 %collective-permute-start.16 = (f32[4,32,256]{2,1,0:T(8,128)S(1)}, f32[4,32,256]{2,1,0:T(8,128)S(1)}, u32[]{:S(2)}, u32[]{:S(2)}) collective-permute-start(f32[4,32,256]{2,1,0:T(8,128)S(1)} %fusion.q_ref.rest_0_.y_ref), channel_id=1, source_target_pairs={{0,240},{4,244},{8,248},{12,252},{16,0},{20,4},{24,8},{28,12},{32,... | collective-permute-start | bytes 393224 | tf_op jit(solution)/shard_map/ppermute | solution.py:160
  54.0 1.5 %shard_map.88 = (f32[4,32,256]{2,1,0:T(8,128)S(1)}, f32[4,32,256]{2,1,0:T(8,128)S(1)}, f32[4,32,256]{2,1,0:T(8,128)S(1)}, f32[4,32,256]{2,1,0:T(8,128)S(1)}, f32[4,32,256]{2,1,0:T(8,128)S(1)}) custom-call(s32[3,32]{1,0:T(4,128)S(1)} %pad_add_fusion.meta, bf16[32,256,256]{2,1,0:T(8,128)(2,1)S(1)} %bitcast.17, f32[4,32,256]{2,1,0:T(8,128)S(1)} %fusion.q_ref.rest_0_.y_ref), custom_call_target="tpu_custom_call" | custom-call | flops 268435456 | bytes 4194304 | tf_op jit(solution)/shard_map/pallas_call | solution.py:228
  55.4 1.4 %collective-permute-start.18 = (f32[4,32,256]{2,1,0:T(8,128)S(1)}, f32[4,32,256]{2,1,0:T(8,128)S(1)}, u32[]{:S(2)}, u32[]{:S(2)}) collective-permute-start(f32[4,32,256]{2,1,0:T(8,128)S(1)} %get-tuple-element.23), channel_id=1, source_target_pairs={{0,16},{4,20},{8,24},{12,28},{16,32},{20,36},{24,40},{28,44},{32,4... | collective-permute-start | bytes 393224 | tf_op jit(solution)/shard_map/ppermute | solution.py:160
  56.8 1.9 %collective-permute-start.20 = (f32[4,32,256]{2,1,0:T(8,128)S(1)}, f32[4,32,256]{2,1,0:T(8,128)S(1)}, u32[]{:S(2)}, u32[]{:S(2)}) collective-permute-start(f32[4,32,256]{2,1,0:T(8,128)S(1)} %get-tuple-element.25), channel_id=1, source_target_pairs={{0,64},{4,68},{8,72},{12,76},{16,80},{20,84},{24,88},{28,92},{32,9... | collective-permute-start | bytes 393224 | tf_op jit(solution)/shard_map/ppermute | solution.py:160
  60.0 6.6 %collective-permute-start.17 = (f32[4,32,256]{2,1,0:T(8,128)S(1)}, f32[4,32,256]{2,1,0:T(8,128)S(1)}, u32[]{:S(2)}, u32[]{:S(2)}) collective-permute-start(f32[4,32,256]{2,1,0:T(8,128)S(1)} %collective-permute-done.16.rest_4_), channel_id=1, source_target_pairs={{0,240},{4,244},{8,248},{12,252},{16,0},{20,4},{24,8},{28,12},{32,... | collective-permute-start | bytes 393224 | tf_op jit(solution)/shard_map/ppermute | solution.py:160
  67.8 1.4 %collective-permute-done.17.rest_3_ = f32[4,32,256]{2,1,0:T(8,128)S(1)} collective-permute-done((f32[4,32,256]{2,1,0:T(8,128)S(1)}, f32[4,32,256]{2,1,0:T(8,128)S(1)}, u32[]{:S(2)}, u32[]{:S(2)}) %collective-permute-start.17) | collective-permute-done | bytes 131104 | tf_op jit(solution)/shard_map/ppermute | solution.py:160
  69.2 2.0 %shard_map.89 = f32[4,32,256]{2,1,0:T(8,128)S(1)} custom-call(s32[3,32]{1,0:T(4,128)S(1)} %pad_add_fusion.meta, bf16[32,256,256]{2,1,0:T(8,128)(2,1)S(1)} %bitcast.18, f32[4,32,256]{2,1,0:T(8,128)S(1)} %get-tuple-element.21.kept_ref, f32[4,32,256]{2,1,0:T(8,128)S(1)} %fusion.q_ref.rest_0_.y_ref, f32[4,32,256]{2,1,0:T(8,128)S(1)} %collective-permute-done.15.rest_1_, ...), custom_call_target="tpu_custom_call" | custom-call | flops 268435456 | bytes 4194304 | tf_op jit(solution)/shard_map/pallas_call | solution.py:237
  71.2 5.6 %collective-permute-done.19 = f32[4,32,256]{2,1,0:T(8,128)S(1)} collective-permute-done((f32[4,32,256]{2,1,0:T(8,128)S(1)}, f32[4,32,256]{2,1,0:T(8,128)S(1)}, u32[]{:S(2)}, u32[]{:S(2)}) %collective-permute-start.19) | collective-permute-done | bytes 131104 | tf_op jit(solution)/shard_map/ppermute | solution.py:160
  77.4 2.8 %collective-permute-start.24 = (f32[4,32,256]{2,1,0:T(8,128)S(1)}, f32[4,32,256]{2,1,0:T(8,128)S(1)}, u32[]{:S(2)}, u32[]{:S(2)}) collective-permute-start(f32[4,32,256]{2,1,0:T(8,128)S(1)} %add_add_fusion), channel_id=1, source_target_pairs={{0,3},{1,0},{2,1},{3,2},{4,7},{5,4},{6,5},{7,6},{8,11},{9,8},{10,9... | collective-permute-start | bytes 393224 | tf_op jit(solution)/shard_map/ppermute | solution.py:160
  81.2 1.9 %collective-permute-done.23 = f32[4,32,256]{2,1,0:T(8,128)S(1)} collective-permute-done((f32[4,32,256]{2,1,0:T(8,128)S(1)}, f32[4,32,256]{2,1,0:T(8,128)S(1)}, u32[]{:S(2)}, u32[]{:S(2)}) %collective-permute-start.23) | collective-permute-done | bytes 131104 | tf_op jit(solution)/shard_map/ppermute | solution.py:160
  83.2 3.5 %collective-permute-done.22 = f32[4,32,256]{2,1,0:T(8,128)S(1)} collective-permute-done((f32[4,32,256]{2,1,0:T(8,128)S(1)}, f32[4,32,256]{2,1,0:T(8,128)S(1)}, u32[]{:S(2)}, u32[]{:S(2)}) %collective-permute-start.22) | collective-permute-done | bytes 131104 | tf_op jit(solution)/shard_map/ppermute | solution.py:160
  88.6 3.2 %collective-permute-start.28 = (f32[48,128]{1,0:T(8,128)S(1)}, f32[48,128]{1,0:T(8,128)S(1)}, u32[]{:S(2)}, u32[]{:S(2)}) collective-permute-start(f32[48,128]{1,0:T(8,128)S(1)} %add.130), channel_id=1, source_target_pairs={{0,192},{4,196},{8,200},{12,204},{16,208},{20,212},{24,216},{28,22... | collective-permute-start | bytes 73736 | tf_op jit(solution)/shard_map/ppermute | solution.py:160
  91.9 2.0 %collective-permute-done.26 = f32[48,128]{1,0:T(8,128)S(1)} collective-permute-done((f32[48,128]{1,0:T(8,128)S(1)}, f32[48,128]{1,0:T(8,128)S(1)}, u32[]{:S(2)}, u32[]{:S(2)}) %collective-permute-start.26) | collective-permute-done | bytes 24608 | tf_op jit(solution)/shard_map/ppermute | solution.py:160
  93.9 2.1 %collective-permute-start.30 = (f32[48,128]{1,0:T(8,128)S(1)}, f32[48,128]{1,0:T(8,128)S(1)}, u32[]{:S(2)}, u32[]{:S(2)}) collective-permute-start(f32[48,128]{1,0:T(8,128)S(1)} %add_add_fusion.3), channel_id=1, source_target_pairs={{0,48},{4,20},{8,56},{12,28},{16,0},{20,36},{24,8},{28,44},{32,16}... | collective-permute-start | bytes 73736 | tf_op jit(solution)/shard_map/ppermute | solution.py:160
  96.0 6.5 %collective-permute-start.29 = (f32[48,128]{1,0:T(8,128)S(1)}, f32[48,128]{1,0:T(8,128)S(1)}, u32[]{:S(2)}, u32[]{:S(2)}) collective-permute-start(f32[48,128]{1,0:T(8,128)S(1)} %add_add_fusion.3), channel_id=1, source_target_pairs={{0,32},{4,36},{8,40},{12,44},{16,48},{20,52},{24,56},{28,60},{32,0... | collective-permute-start | bytes 73736 | tf_op jit(solution)/shard_map/ppermute | solution.py:160
  104.6 4.2 %shard_map.91 = (f32[32,256]{1,0:T(8,128)}, f32[2,32,64]{2,1,0:T(8,128)}, f32[2,32,32]{2,1,0:T(8,128)}) custom-call(f32[48,128]{1,0:T(8,128)S(1)} %add_add_fusion.2.gram_ref, f32[4,32,256]{2,1,0:T(8,128)S(1)} %pad_maximum_fusion.q_ref.rest_0_.s_ref, f32[4,32,256]{2,1,0:T(8,128)S(1)} %fusion.q_ref.rest_0_.y_ref, f32[4,32,256]{2,1,0:T(8,128)S(1)} %fusion.1.z_ref), custom_call_target="tpu_custom_call" | custom-call | tf_op jit(solution)/shard_map/pallas_call | solution.py:258
  (76 shorter events, 12.2 us)
Async XLA Ops:
  0.6 10.1 %collective-permute-start = (f32[32,256]{1,0:T(8,128)}, f32[32,256]{1,0:T(8,128)S(1)}, u32[]{:S(2)}, u32[]{:S(2)}) collective-permute-start(f32[32,256]{1,0:T(8,128)} %start_ref.1), channel_id=1, source_target_pairs={{0,1},{1,2},{2,3},{3,0},{4,5},{5,6},{6,7},{7,4},{8,9},{9,10},{10,1... | collective-permute-start | bytes 98312 | tf_op jit(solution)/shard_map/ppermute | solution.py:160
  2.2 8.5 %collective-permute-start.1 = (f32[32,256]{1,0:T(8,128)}, f32[32,256]{1,0:T(8,128)S(1)}, u32[]{:S(2)}, u32[]{:S(2)}) collective-permute-start(f32[32,256]{1,0:T(8,128)} %start_ref.1), channel_id=1, source_target_pairs={{0,2},{1,3},{2,0},{3,1},{4,6},{5,7},{6,4},{7,5},{8,10},{9,11},{10,... | collective-permute-start | bytes 98312 | tf_op jit(solution)/shard_map/ppermute | solution.py:160
  4.9 5.8 %collective-permute-start.2 = (f32[32,256]{1,0:T(8,128)}, f32[32,256]{1,0:T(8,128)S(1)}, u32[]{:S(2)}, u32[]{:S(2)}) collective-permute-start(f32[32,256]{1,0:T(8,128)} %start_ref.1), channel_id=1, source_target_pairs={{0,3},{1,0},{2,1},{3,2},{4,7},{5,4},{6,5},{7,6},{8,11},{9,8},{10,9... | collective-permute-start | bytes 98312 | tf_op jit(solution)/shard_map/ppermute | solution.py:160
  10.7 11.6 %collective-permute-start.3 = (f32[4,32,256]{2,1,0:T(8,128)S(1)}, f32[4,32,256]{2,1,0:T(8,128)S(1)}, u32[]{:S(2)}, u32[]{:S(2)}) collective-permute-start(f32[4,32,256]{2,1,0:T(8,128)S(1)} %pad_maximum_fusion.q_ref.rest_0_.s_ref), channel_id=1, source_target_pairs={{0,192},{4,196},{8,200},{12,204},{16,208},{20,212},{24,216},{28,22... | collective-permute-start | bytes 393224 | tf_op jit(solution)/shard_map/ppermute | solution.py:160
  13.8 10.5 %collective-permute-start.5 = (f32[4,32,256]{2,1,0:T(8,128)S(1)}, f32[4,32,256]{2,1,0:T(8,128)S(1)}, u32[]{:S(2)}, u32[]{:S(2)}) collective-permute-start(f32[4,32,256]{2,1,0:T(8,128)S(1)} %pad_maximum_fusion.q_ref.rest_0_.s_ref), channel_id=1, source_target_pairs={{0,240},{4,244},{8,248},{12,252},{16,0},{20,4},{24,8},{28,12},{32,... | collective-permute-start | bytes 393224 | tf_op jit(solution)/shard_map/ppermute | solution.py:160
  20.9 11.4 %collective-permute-start.7 = (f32[4,32,256]{2,1,0:T(8,128)S(1)}, f32[4,32,256]{2,1,0:T(8,128)S(1)}, u32[]{:S(2)}, u32[]{:S(2)}) collective-permute-start(f32[4,32,256]{2,1,0:T(8,128)S(1)} %get-tuple-element.18), channel_id=1, source_target_pairs={{0,16},{4,20},{8,24},{12,28},{16,32},{20,36},{24,40},{28,44},{32,4... | collective-permute-start | bytes 393224 | tf_op jit(solution)/shard_map/ppermute | solution.py:160
  21.0 11.5 %collective-permute-start.9 = (f32[4,32,256]{2,1,0:T(8,128)S(1)}, f32[4,32,256]{2,1,0:T(8,128)S(1)}, u32[]{:S(2)}, u32[]{:S(2)}) collective-permute-start(f32[4,32,256]{2,1,0:T(8,128)S(1)} %get-tuple-element.20), channel_id=1, source_target_pairs={{0,64},{4,68},{8,72},{12,76},{16,80},{20,84},{24,88},{28,92},{32,9... | collective-permute-start | bytes 393224 | tf_op jit(solution)/shard_map/ppermute | solution.py:160
  22.3 10.2 %collective-permute-start.4 = (f32[4,32,256]{2,1,0:T(8,128)S(1)}, f32[4,32,256]{2,1,0:T(8,128)S(1)}, u32[]{:S(2)}, u32[]{:S(2)}) collective-permute-start(f32[4,32,256]{2,1,0:T(8,128)S(1)} %collective-permute-done.3.rest_2_), channel_id=1, source_target_pairs={{0,192},{4,196},{8,200},{12,204},{16,208},{20,212},{24,216},{28,22... | collective-permute-start | bytes 393224 | tf_op jit(solution)/shard_map/ppermute | solution.py:160
  24.3 8.7 %collective-permute-start.6 = (f32[4,32,256]{2,1,0:T(8,128)S(1)}, f32[4,32,256]{2,1,0:T(8,128)S(1)}, u32[]{:S(2)}, u32[]{:S(2)}) collective-permute-start(f32[4,32,256]{2,1,0:T(8,128)S(1)} %collective-permute-done.5.rest_4_), channel_id=1, source_target_pairs={{0,240},{4,244},{8,248},{12,252},{16,0},{20,4},{24,8},{28,12},{32,... | collective-permute-start | bytes 393224 | tf_op jit(solution)/shard_map/ppermute | solution.py:160
  32.3 9.7 %collective-permute-start.8 = (f32[4,32,256]{2,1,0:T(8,128)S(1)}, f32[4,32,256]{2,1,0:T(8,128)S(1)}, u32[]{:S(2)}, u32[]{:S(2)}) collective-permute-start(f32[4,32,256]{2,1,0:T(8,128)S(1)} %add.116), channel_id=1, source_target_pairs={{0,16},{4,20},{8,24},{12,28},{16,32},{20,36},{24,40},{28,44},{32,4... | collective-permute-start | bytes 393224 | tf_op jit(solution)/shard_map/ppermute | solution.py:160
  32.5 9.6 %collective-permute-start.10 = (f32[4,32,256]{2,1,0:T(8,128)S(1)}, f32[4,32,256]{2,1,0:T(8,128)S(1)}, u32[]{:S(2)}, u32[]{:S(2)}) collective-permute-start(f32[4,32,256]{2,1,0:T(8,128)S(1)} %add.118), channel_id=1, source_target_pairs={{0,64},{4,68},{8,72},{12,76},{16,80},{20,84},{24,88},{28,92},{32,9... | collective-permute-start | bytes 393224 | tf_op jit(solution)/shard_map/ppermute | solution.py:160
  42.1 6.3 %collective-permute-start.12 = (f32[4,32,256]{2,1,0:T(8,128)S(1)}, f32[4,32,256]{2,1,0:T(8,128)S(1)}, u32[]{:S(2)}, u32[]{:S(2)}) collective-permute-start(f32[4,32,256]{2,1,0:T(8,128)S(1)} %add_add_fusion.1), channel_id=1, source_target_pairs={{0,1},{1,2},{2,3},{3,0},{4,5},{5,6},{6,7},{7,4},{8,9},{9,10},{10,1... | collective-permute-start | bytes 393224 | tf_op jit(solution)/shard_map/ppermute | solution.py:160
  42.8 6.6 %collective-permute-start.13 = (f32[4,32,256]{2,1,0:T(8,128)S(1)}, f32[4,32,256]{2,1,0:T(8,128)S(1)}, u32[]{:S(2)}, u32[]{:S(2)}) collective-permute-start(f32[4,32,256]{2,1,0:T(8,128)S(1)} %add_add_fusion.1), channel_id=1, source_target_pairs={{0,3},{1,0},{2,1},{3,2},{4,7},{5,4},{6,5},{7,6},{8,11},{9,8},{10,9... | collective-permute-start | bytes 393224 | tf_op jit(solution)/shard_map/ppermute | solution.py:160
  45.4 6.5 %collective-permute-start.11 = (f32[4,32,256]{2,1,0:T(8,128)S(1)}, f32[4,32,256]{2,1,0:T(8,128)S(1)}, u32[]{:S(2)}, u32[]{:S(2)}) collective-permute-start(f32[4,32,256]{2,1,0:T(8,128)S(1)} %add_add_fusion.1), channel_id=1, source_target_pairs={{0,2},{1,3},{2,0},{3,1},{4,6},{5,7},{6,4},{7,5},{8,10},{9,11},{10,... | collective-permute-start | bytes 393224 | tf_op jit(solution)/shard_map/ppermute | solution.py:160
  52.0 6.8 %collective-permute-start.14 = (f32[4,32,256]{2,1,0:T(8,128)S(1)}, f32[4,32,256]{2,1,0:T(8,128)S(1)}, u32[]{:S(2)}, u32[]{:S(2)}) collective-permute-start(f32[4,32,256]{2,1,0:T(8,128)S(1)} %fusion.q_ref.rest_0_.y_ref), channel_id=1, source_target_pairs={{0,192},{4,196},{8,200},{12,204},{16,208},{20,212},{24,216},{28,22... | collective-permute-start | bytes 393224 | tf_op jit(solution)/shard_map/ppermute | solution.py:160
  52.3 7.8 %collective-permute-start.16 = (f32[4,32,256]{2,1,0:T(8,128)S(1)}, f32[4,32,256]{2,1,0:T(8,128)S(1)}, u32[]{:S(2)}, u32[]{:S(2)}) collective-permute-start(f32[4,32,256]{2,1,0:T(8,128)S(1)} %fusion.q_ref.rest_0_.y_ref), channel_id=1, source_target_pairs={{0,240},{4,244},{8,248},{12,252},{16,0},{20,4},{24,8},{28,12},{32,... | collective-permute-start | bytes 393224 | tf_op jit(solution)/shard_map/ppermute | solution.py:160
  55.4 12.1 %collective-permute-start.18 = (f32[4,32,256]{2,1,0:T(8,128)S(1)}, f32[4,32,256]{2,1,0:T(8,128)S(1)}, u32[]{:S(2)}, u32[]{:S(2)}) collective-permute-start(f32[4,32,256]{2,1,0:T(8,128)S(1)} %get-tuple-element.23), channel_id=1, source_target_pairs={{0,16},{4,20},{8,24},{12,28},{16,32},{20,36},{24,40},{28,44},{32,4... | collective-permute-start | bytes 393224 | tf_op jit(solution)/shard_map/ppermute | solution.py:160
  56.8 10.9 %collective-permute-start.20 = (f32[4,32,256]{2,1,0:T(8,128)S(1)}, f32[4,32,256]{2,1,0:T(8,128)S(1)}, u32[]{:S(2)}, u32[]{:S(2)}) collective-permute-start(f32[4,32,256]{2,1,0:T(8,128)S(1)} %get-tuple-element.25), channel_id=1, source_target_pairs={{0,64},{4,68},{8,72},{12,76},{16,80},{20,84},{24,88},{28,92},{32,9... | collective-permute-start | bytes 393224 | tf_op jit(solution)/shard_map/ppermute | solution.py:160
  58.7 9.1 %collective-permute-start.15 = (f32[4,32,256]{2,1,0:T(8,128)S(1)}, f32[4,32,256]{2,1,0:T(8,128)S(1)}, u32[]{:S(2)}, u32[]{:S(2)}) collective-permute-start(f32[4,32,256]{2,1,0:T(8,128)S(1)} %collective-permute-done.14.rest_2_), channel_id=1, source_target_pairs={{0,192},{4,196},{8,200},{12,204},{16,208},{20,212},{24,216},{28,22... | collective-permute-start | bytes 393224 | tf_op jit(solution)/shard_map/ppermute | solution.py:160
  60.0 9.2 %collective-permute-start.17 = (f32[4,32,256]{2,1,0:T(8,128)S(1)}, f32[4,32,256]{2,1,0:T(8,128)S(1)}, u32[]{:S(2)}, u32[]{:S(2)}) collective-permute-start(f32[4,32,256]{2,1,0:T(8,128)S(1)} %collective-permute-done.16.rest_4_), channel_id=1, source_target_pairs={{0,240},{4,244},{8,248},{12,252},{16,0},{20,4},{24,8},{28,12},{32,... | collective-permute-start | bytes 393224 | tf_op jit(solution)/shard_map/ppermute | solution.py:160
  67.6 9.3 %collective-permute-start.19 = (f32[4,32,256]{2,1,0:T(8,128)S(1)}, f32[4,32,256]{2,1,0:T(8,128)S(1)}, u32[]{:S(2)}, u32[]{:S(2)}) collective-permute-start(f32[4,32,256]{2,1,0:T(8,128)S(1)} %add.123), channel_id=1, source_target_pairs={{0,16},{4,20},{8,24},{12,28},{16,32},{20,36},{24,40},{28,44},{32,4... | collective-permute-start | bytes 393224 | tf_op jit(solution)/shard_map/ppermute | solution.py:160
  67.7 9.1 %collective-permute-start.21 = (f32[4,32,256]{2,1,0:T(8,128)S(1)}, f32[4,32,256]{2,1,0:T(8,128)S(1)}, u32[]{:S(2)}, u32[]{:S(2)}) collective-permute-start(f32[4,32,256]{2,1,0:T(8,128)S(1)} %add.125), channel_id=1, source_target_pairs={{0,64},{4,68},{8,72},{12,76},{16,80},{20,84},{24,88},{28,92},{32,9... | collective-permute-start | bytes 393224 | tf_op jit(solution)/shard_map/ppermute | solution.py:160
  76.9 6.3 %collective-permute-start.23 = (f32[4,32,256]{2,1,0:T(8,128)S(1)}, f32[4,32,256]{2,1,0:T(8,128)S(1)}, u32[]{:S(2)}, u32[]{:S(2)}) collective-permute-start(f32[4,32,256]{2,1,0:T(8,128)S(1)} %add_add_fusion), channel_id=1, source_target_pairs={{0,1},{1,2},{2,3},{3,0},{4,5},{5,6},{6,7},{7,4},{8,9},{9,10},{10,1... | collective-permute-start | bytes 393224 | tf_op jit(solution)/shard_map/ppermute | solution.py:160
  77.4 5.8 %collective-permute-start.24 = (f32[4,32,256]{2,1,0:T(8,128)S(1)}, f32[4,32,256]{2,1,0:T(8,128)S(1)}, u32[]{:S(2)}, u32[]{:S(2)}) collective-permute-start(f32[4,32,256]{2,1,0:T(8,128)S(1)} %add_add_fusion), channel_id=1, source_target_pairs={{0,3},{1,0},{2,1},{3,2},{4,7},{5,4},{6,5},{7,6},{8,11},{9,8},{10,9... | collective-permute-start | bytes 393224 | tf_op jit(solution)/shard_map/ppermute | solution.py:160
  80.2 6.5 %collective-permute-start.22 = (f32[4,32,256]{2,1,0:T(8,128)S(1)}, f32[4,32,256]{2,1,0:T(8,128)S(1)}, u32[]{:S(2)}, u32[]{:S(2)}) collective-permute-start(f32[4,32,256]{2,1,0:T(8,128)S(1)} %add_add_fusion), channel_id=1, source_target_pairs={{0,2},{1,3},{2,0},{3,1},{4,6},{5,7},{6,4},{7,5},{8,10},{9,11},{10,... | collective-permute-start | bytes 393224 | tf_op jit(solution)/shard_map/ppermute | solution.py:160
  88.5 5.4 %collective-permute-start.26 = (f32[48,128]{1,0:T(8,128)S(1)}, f32[48,128]{1,0:T(8,128)S(1)}, u32[]{:S(2)}, u32[]{:S(2)}) collective-permute-start(f32[48,128]{1,0:T(8,128)S(1)} %add.130), channel_id=1, source_target_pairs={{0,128},{4,132},{8,136},{12,140},{16,144},{20,148},{24,152},{28,15... | collective-permute-start | bytes 73736 | tf_op jit(solution)/shard_map/ppermute | solution.py:160
  88.5 5.4 %collective-permute-start.27 = (f32[48,128]{1,0:T(8,128)S(1)}, f32[48,128]{1,0:T(8,128)S(1)}, u32[]{:S(2)}, u32[]{:S(2)}) collective-permute-start(f32[48,128]{1,0:T(8,128)S(1)} %add.130), channel_id=1, source_target_pairs={{0,64},{4,68},{8,72},{12,76},{16,80},{20,84},{24,88},{28,92},{32,9... | collective-permute-start | bytes 73736 | tf_op jit(solution)/shard_map/ppermute | solution.py:160
  88.6 5.3 %collective-permute-start.28 = (f32[48,128]{1,0:T(8,128)S(1)}, f32[48,128]{1,0:T(8,128)S(1)}, u32[]{:S(2)}, u32[]{:S(2)}) collective-permute-start(f32[48,128]{1,0:T(8,128)S(1)} %add.130), channel_id=1, source_target_pairs={{0,192},{4,196},{8,200},{12,204},{16,208},{20,212},{24,216},{28,22... | collective-permute-start | bytes 73736 | tf_op jit(solution)/shard_map/ppermute | solution.py:160
  93.9 8.6 %collective-permute-start.30 = (f32[48,128]{1,0:T(8,128)S(1)}, f32[48,128]{1,0:T(8,128)S(1)}, u32[]{:S(2)}, u32[]{:S(2)}) collective-permute-start(f32[48,128]{1,0:T(8,128)S(1)} %add_add_fusion.3), channel_id=1, source_target_pairs={{0,48},{4,20},{8,56},{12,28},{16,0},{20,36},{24,8},{28,44},{32,16}... | collective-permute-start | bytes 73736 | tf_op jit(solution)/shard_map/ppermute | solution.py:160
  96.0 6.8 %collective-permute-start.33 = (f32[48,128]{1,0:T(8,128)S(1)}, f32[48,128]{1,0:T(8,128)S(1)}, u32[]{:S(2)}, u32[]{:S(2)}) collective-permute-start(f32[48,128]{1,0:T(8,128)S(1)} %add_add_fusion.3), channel_id=1, source_target_pairs={{0,40},{4,28},{8,48},{12,36},{16,56},{20,44},{24,0},{28,52},{32,8}... | collective-permute-start | bytes 73736 | tf_op jit(solution)/shard_map/ppermute | solution.py:160
  96.0 7.0 %collective-permute-start.32 = (f32[48,128]{1,0:T(8,128)S(1)}, f32[48,128]{1,0:T(8,128)S(1)}, u32[]{:S(2)}, u32[]{:S(2)}) collective-permute-start(f32[48,128]{1,0:T(8,128)S(1)} %add_add_fusion.3), channel_id=1, source_target_pairs={{0,56},{4,12},{8,0},{12,20},{16,8},{20,28},{24,16},{28,36},{32,24}... | collective-permute-start | bytes 73736 | tf_op jit(solution)/shard_map/ppermute | solution.py:160
  96.0 8.6 %collective-permute-start.29 = (f32[48,128]{1,0:T(8,128)S(1)}, f32[48,128]{1,0:T(8,128)S(1)}, u32[]{:S(2)}, u32[]{:S(2)}) collective-permute-start(f32[48,128]{1,0:T(8,128)S(1)} %add_add_fusion.3), channel_id=1, source_target_pairs={{0,32},{4,36},{8,40},{12,44},{16,48},{20,52},{24,56},{28,60},{32,0... | collective-permute-start | bytes 73736 | tf_op jit(solution)/shard_map/ppermute | solution.py:160
  (6 other events, 9.6 us)

commit v5 on v4

--- a/solution.py
+++ b/solution.py
@@ -51,7 +51,7 @@
 
 
 def forward_kernel(meta, held, kept_ref, *rest):
-    sources, out, (terms, total) = rest[: ROUNDS + 1], rest[ROUNDS + 1], rest[-2:]
+    sources, out, (terms, total) = rest[ROUNDS::-1], rest[ROUNDS + 1], rest[-2:]
     blocks = kept_ref.shape[0]
     trash = blocks
     for i, ref in enumerate(sources):
@@ -66,6 +66,12 @@
         half = product.shape[0] // 2
         total[target] += product[:half] + product[half:]
     out[...] = total[:blocks]
+
+
+def rep_sum_kernel(second, first, third, own, out):
+    n = own.shape[0]
+    for b in range(n):
+        out[b] = (own[b] + second[(b - 2) % n]) + (first[(b - 1) % n] + third[(b - 3) % n])
 
 
 def gram_kernel(s_ref, y_ref, z_ref, out):
@@ -193,7 +199,7 @@
     column = lax.rem(member - tile_col[0, 0] + blocks, blocks)
     row = lax.rem(member - tile_row[0, 0] + blocks, blocks)
     live = (jnp.arange(slots, dtype=jnp.int32) < tile_count[0]).astype(jnp.int32)
-    meta = jnp.stack([tile_round[0, 0] * blocks + column, row, live], 0)
+    meta = jnp.stack([(tile_round[0, 0] * blocks + column) * live, row * live, live], 0)
     own = pl.pallas_call(
         ready_kernel,
         out_shape=jax.ShapeDtypeStruct(start_block.shape, F32),
@@ -221,7 +227,13 @@
     )
 
     def rep_sum(part):
-        return sum_of_ring(part, lambda by: jnp.roll(shifted(part, "rep", by), by, axis=0))
+        return pl.pallas_call(
+            rep_sum_kernel,
+            out_shape=block_shape,
+            in_specs=[vmem] * 4,
+            out_specs=vmem,
+            compiler_params=params,
+        )(*[shifted(part, "rep", by) for by in (2, 1, 3)], part)
 
     def apply(q):
         _, quarter, _, last = offsets
@@ -234,7 +246,7 @@
         got32 = shifted(got16, "rows", -quarter)
         v = shifted(out4 + u, "rows", last)
         x = shifted(out16 + w, "rows", quarter)
-        part = forward(meta, tiles, kept, q, got32, got16, got8, got4)
+        part = forward(meta, tiles, kept, got4, got8, got16, got32, q)
         return rep_sum(part + v + x)
 
     start = jnp.stack([own] + [shifted(start_block, "rep", by) for by in range(1, members)], 0)

time: 110 us -> 107 us (0.973)
  waiting for transfers between devices: 35.1 us -> 33 us
    ppermute x36, waiting for transfers between devices: 35.1 us -> 33 us  [moved(): return lax.ppermute(x, axis, [(i, target(i) % size) for i in range(size)])]
    pallas_call x2 -> x4, Pallas kernels: 4.01 us -> 4.07 us  [the longest x2 4.02 us: apply(): part = forward(meta, tiles, kept, got4, got8, got16, got32, q)]
    unnamed x4 -> x6, local copies, waits for them, and re-layouts: 2.94 us -> 2.95 us
  transfers between devices with their start and end apart: 36 -> 36, of which waited for: 15 -> 17; matrix products, arithmetic and copies ran while one was open for 1% -> 1% of each run, Pallas kernels for 6% -> 7%
where the time goes in v5:
time: 107 us; the launch traced here: 106 us
  starting transfers between devices  56 us (52%)
  waiting for transfers between devices  33 us (31%)
  Pallas kernels  11.8 us (11%)
  local copies, waits for them, and re-layouts  2.95 us (3%)
  between operations  1.51 us (1%)
    ppermute x36, starting transfers between devices, moved(): return lax.ppermute(x, axis, [(i, target(i) % size) for i in range(size)])  56 us
    ppermute x36, waiting for transfers between devices, moved(): return lax.ppermute(x, axis, [(i, target(i) % size) for i in range(size)])  33 us
    pallas_call x1, Pallas kernels, body(): pl.pallas_call(tail_kernel, out_shape=[jax.ShapeDtypeStruct((k, edge), F3...  4.2 us
    pallas_call x2, Pallas kernels, apply(): part = forward(meta, tiles, kept, got4, got8, got16, got32, q)  4.02 us
    pallas_call x2, Pallas kernels, apply(): kept, out32, out16, out8, out4 = backward(meta, tiles, q)  2.98 us
    unnamed x6, local copies, waits for them, and re-layouts  2.95 us
  transfers between devices with their start and end apart: 36, of which 17 were waited for; matrix products, arithmetic and copies ran while one was open for 1% of the time, Pallas kernels for 7%

profile of v5, /device:TPU:32, one launch (start us, length us, event | category | flops | bytes accessed | tf_op | source)
XLA Modules:
  0.0 106.1 jit_solution(4610867221185812651)
XLA Ops:
  0.6 1.6 %collective-permute-start = (f32[32,256]{1,0:T(8,128)}, f32[32,256]{1,0:T(8,128)S(1)}, u32[]{:S(2)}, u32[]{:S(2)}) collective-permute-start(f32[32,256]{1,0:T(8,128)} %start_ref.1), channel_id=1, source_target_pairs={{0,1},{1,2},{2,3},{3,0},{4,5},{5,6},{6,7},{7,4},{8,9},{9,10},{10,1... | collective-permute-start | bytes 98312 | tf_op jit(solution)/shard_map/ppermute | solution.py:166
  2.2 2.7 %collective-permute-start.1 = (f32[32,256]{1,0:T(8,128)}, f32[32,256]{1,0:T(8,128)S(1)}, u32[]{:S(2)}, u32[]{:S(2)}) collective-permute-start(f32[32,256]{1,0:T(8,128)} %start_ref.1), channel_id=1, source_target_pairs={{0,2},{1,3},{2,0},{3,1},{4,6},{5,7},{6,4},{7,5},{8,10},{9,11},{10,... | collective-permute-start | bytes 98312 | tf_op jit(solution)/shard_map/ppermute | solution.py:166
  4.9 1.4 %collective-permute-start.2 = (f32[32,256]{1,0:T(8,128)}, f32[32,256]{1,0:T(8,128)S(1)}, u32[]{:S(2)}, u32[]{:S(2)}) collective-permute-start(f32[32,256]{1,0:T(8,128)} %start_ref.1), channel_id=1, source_target_pairs={{0,3},{1,0},{2,1},{3,2},{4,7},{5,4},{6,5},{7,6},{8,11},{9,8},{10,9... | collective-permute-start | bytes 98312 | tf_op jit(solution)/shard_map/ppermute | solution.py:166
  7.8 2.2 %copy-done = bf16[1,1,32,256,256]{4,3,2,1,0:T(8,128)(2,1)S(1)} copy-done((bf16[1,1,32,256,256]{4,3,2,1,0:T(8,128)(2,1)S(1)}, bf16[1,1,32,256,256]{4,3,2,1,0:T(8,128)(2,1)}, u32[]{:S(2)}) %copy-start) | copy-done | bytes 4194328
  10.7 7.9 %collective-permute-start.3 = (f32[4,32,256]{2,1,0:T(8,128)S(1)}, f32[4,32,256]{2,1,0:T(8,128)S(1)}, u32[]{:S(2)}, u32[]{:S(2)}) collective-permute-start(f32[4,32,256]{2,1,0:T(8,128)S(1)} %pad_maximum_fusion.q_ref.rest_4_.s_ref), channel_id=1, source_target_pairs={{0,240},{4,244},{8,248},{12,252},{16,0},{20,4},{24,8},{28,12},{32,... | collective-permute-start | bytes 393224 | tf_op jit(solution)/shard_map/ppermute | solution.py:166
  19.4 1.5 %shard_map.86 = (f32[4,32,256]{2,1,0:T(8,128)S(1)}, f32[4,32,256]{2,1,0:T(8,128)S(1)}, f32[4,32,256]{2,1,0:T(8,128)S(1)}, f32[4,32,256]{2,1,0:T(8,128)S(1)}, f32[4,32,256]{2,1,0:T(8,128)S(1)}) custom-call(s32[3,32]{1,0:T(4,128)S(1)} %pad_add_fusion.meta, bf16[32,256,256]{2,1,0:T(8,128)(2,1)S(1)} %bitcast.16, ...), custom_call_target="tpu_custom_call" | custom-call | flops 268435456 | bytes 4194304 | tf_op jit(solution)/shard_map/pallas_call | solution.py:240
  21.0 1.4 %collective-permute-start.9 = (f32[4,32,256]{2,1,0:T(8,128)S(1)}, f32[4,32,256]{2,1,0:T(8,128)S(1)}, u32[]{:S(2)}, u32[]{:S(2)}) collective-permute-start(f32[4,32,256]{2,1,0:T(8,128)S(1)} %get-tuple-element.20), channel_id=1, source_target_pairs={{0,64},{4,68},{8,72},{12,76},{16,80},{20,84},{24,88},{28,92},{32,9... | collective-permute-start | bytes 393224 | tf_op jit(solution)/shard_map/ppermute | solution.py:166
  22.4 6.2 %collective-permute-start.4 = (f32[4,32,256]{2,1,0:T(8,128)S(1)}, f32[4,32,256]{2,1,0:T(8,128)S(1)}, u32[]{:S(2)}, u32[]{:S(2)}) collective-permute-start(f32[4,32,256]{2,1,0:T(8,128)S(1)} %collective-permute-done.3.rest_0_), channel_id=1, source_target_pairs={{0,240},{4,244},{8,248},{12,252},{16,0},{20,4},{24,8},{28,12},{32,... | collective-permute-start | bytes 393224 | tf_op jit(solution)/shard_map/ppermute | solution.py:166
  29.3 3.0 %collective-permute-done.7 = f32[4,32,256]{2,1,0:T(8,128)S(1)} collective-permute-done((f32[4,32,256]{2,1,0:T(8,128)S(1)}, f32[4,32,256]{2,1,0:T(8,128)S(1)}, u32[]{:S(2)}, u32[]{:S(2)}) %collective-permute-start.7) | collective-permute-done | bytes 131104 | tf_op jit(solution)/shard_map/ppermute | solution.py:166
  33.5 2.0 %shard_map.87 = f32[4,32,256]{2,1,0:T(8,128)S(1)} custom-call(s32[3,32]{1,0:T(4,128)S(1)} %pad_add_fusion.meta, bf16[32,256,256]{2,1,0:T(8,128)(2,1)S(1)} %bitcast.17, f32[4,32,256]{2,1,0:T(8,128)S(1)} %get-tuple-element.16.kept_ref, f32[4,32,256]{2,1,0:T(8,128)S(1)} %collective-permute-done.3.rest_0_, f32[4,32,256]{2,1,0:T(8,128)S(1)} %collective-permute-done.4.rest_1_, ...), custom_call_target="tpu_custom_call" | custom-call | flops 268435456 | bytes 4194304 | tf_op jit(solution)/shard_map/pallas_call | solution.py:249
  35.5 6.7 %collective-permute-done.8 = f32[4,32,256]{2,1,0:T(8,128)S(1)} collective-permute-done((f32[4,32,256]{2,1,0:T(8,128)S(1)}, f32[4,32,256]{2,1,0:T(8,128)S(1)}, u32[]{:S(2)}, u32[]{:S(2)}) %collective-permute-start.8) | collective-permute-done | bytes 131104 | tf_op jit(solution)/shard_map/ppermute | solution.py:166
  43.8 2.2 %collective-permute-start.13 = (f32[4,32,256]{2,1,0:T(8,128)S(1)}, f32[4,32,256]{2,1,0:T(8,128)S(1)}, u32[]{:S(2)}, u32[]{:S(2)}) collective-permute-start(f32[4,32,256]{2,1,0:T(8,128)S(1)} %add_add_fusion.1.own), channel_id=1, source_target_pairs={{0,3},{1,0},{2,1},{3,2},{4,7},{5,4},{6,5},{7,6},{8,11},{9,8},{10,9... | collective-permute-start | bytes 393224 | tf_op jit(solution)/shard_map/ppermute | solution.py:166
  46.1 2.8 %collective-permute-done.11.second = f32[4,32,256]{2,1,0:T(8,128)S(1)} collective-permute-done((f32[4,32,256]{2,1,0:T(8,128)S(1)}, f32[4,32,256]{2,1,0:T(8,128)S(1)}, u32[]{:S(2)}, u32[]{:S(2)}) %collective-permute-start.11) | collective-permute-done | bytes 131104 | tf_op jit(solution)/shard_map/ppermute | solution.py:166
  50.2 1.8 %collective-permute-start.14 = (f32[4,32,256]{2,1,0:T(8,128)S(1)}, f32[4,32,256]{2,1,0:T(8,128)S(1)}, u32[]{:S(2)}, u32[]{:S(2)}) collective-permute-start(f32[4,32,256]{2,1,0:T(8,128)S(1)} %shard_map.88.q_ref.rest_4_.y_ref), channel_id=1, source_target_pairs={{0,240},{4,244},{8,248},{12,252},{16,0},{20,4},{24,8},{28,12},{32,... | collective-permute-start | bytes 393224 | tf_op jit(solution)/shard_map/ppermute | solution.py:166
  52.0 1.5 %shard_map.89 = (f32[4,32,256]{2,1,0:T(8,128)S(1)}, f32[4,32,256]{2,1,0:T(8,128)S(1)}, f32[4,32,256]{2,1,0:T(8,128)S(1)}, f32[4,32,256]{2,1,0:T(8,128)S(1)}, f32[4,32,256]{2,1,0:T(8,128)S(1)}) custom-call(s32[3,32]{1,0:T(4,128)S(1)} %pad_add_fusion.meta, bf16[32,256,256]{2,1,0:T(8,128)(2,1)S(1)} %bitcast.18, f32[4,32,256]{2,1,0:T(8,128)S(1)} %shard_map.88.q_ref.rest_4_.y_ref), custom_call_target="tpu_custom_call" | custom-call | flops 268435456 | bytes 4194304 | tf_op jit(solution)/shard_map/pallas_call | solution.py:240
  53.5 1.5 %collective-permute-start.18 = (f32[4,32,256]{2,1,0:T(8,128)S(1)}, f32[4,32,256]{2,1,0:T(8,128)S(1)}, u32[]{:S(2)}, u32[]{:S(2)}) collective-permute-start(f32[4,32,256]{2,1,0:T(8,128)S(1)} %get-tuple-element.23), channel_id=1, source_target_pairs={{0,16},{4,20},{8,24},{12,28},{16,32},{20,36},{24,40},{28,44},{32,4... | collective-permute-start | bytes 393224 | tf_op jit(solution)/shard_map/ppermute | solution.py:166
  55.0 2.0 %collective-permute-start.20 = (f32[4,32,256]{2,1,0:T(8,128)S(1)}, f32[4,32,256]{2,1,0:T(8,128)S(1)}, u32[]{:S(2)}, u32[]{:S(2)}) collective-permute-start(f32[4,32,256]{2,1,0:T(8,128)S(1)} %get-tuple-element.25), channel_id=1, source_target_pairs={{0,64},{4,68},{8,72},{12,76},{16,80},{20,84},{24,88},{28,92},{32,9... | collective-permute-start | bytes 393224 | tf_op jit(solution)/shard_map/ppermute | solution.py:166
  58.1 6.7 %collective-permute-start.15 = (f32[4,32,256]{2,1,0:T(8,128)S(1)}, f32[4,32,256]{2,1,0:T(8,128)S(1)}, u32[]{:S(2)}, u32[]{:S(2)}) collective-permute-start(f32[4,32,256]{2,1,0:T(8,128)S(1)} %collective-permute-done.14.rest_0_), channel_id=1, source_target_pairs={{0,240},{4,244},{8,248},{12,252},{16,0},{20,4},{24,8},{28,12},{32,... | collective-permute-start | bytes 393224 | tf_op jit(solution)/shard_map/ppermute | solution.py:166
  64.8 1.9 %collective-permute-done.18 = f32[4,32,256]{2,1,0:T(8,128)S(1)} collective-permute-done((f32[4,32,256]{2,1,0:T(8,128)S(1)}, f32[4,32,256]{2,1,0:T(8,128)S(1)}, u32[]{:S(2)}, u32[]{:S(2)}) %collective-permute-start.18) | collective-permute-done | bytes 131104 | tf_op jit(solution)/shard_map/ppermute | solution.py:166
  67.3 2.4 %collective-permute-done.17.rest_3_ = f32[4,32,256]{2,1,0:T(8,128)S(1)} collective-permute-done((f32[4,32,256]{2,1,0:T(8,128)S(1)}, f32[4,32,256]{2,1,0:T(8,128)S(1)}, u32[]{:S(2)}, u32[]{:S(2)}) %collective-permute-start.17) | collective-permute-done | bytes 131104 | tf_op jit(solution)/shard_map/ppermute | solution.py:166
  69.8 2.0 %shard_map.90 = f32[4,32,256]{2,1,0:T(8,128)S(1)} custom-call(s32[3,32]{1,0:T(4,128)S(1)} %pad_add_fusion.meta, bf16[32,256,256]{2,1,0:T(8,128)(2,1)S(1)} %bitcast.19, f32[4,32,256]{2,1,0:T(8,128)S(1)} %get-tuple-element.21.kept_ref, f32[4,32,256]{2,1,0:T(8,128)S(1)} %collective-permute-done.14.rest_0_, f32[4,32,256]{2,1,0:T(8,128)S(1)} %collective-permute-done.15.rest_1_, ...), custom_call_target="tpu_custom_call" | custom-call | flops 268435456 | bytes 4194304 | tf_op jit(solution)/shard_map/pallas_call | solution.py:249
  71.8 4.3 %collective-permute-done.19 = f32[4,32,256]{2,1,0:T(8,128)S(1)} collective-permute-done((f32[4,32,256]{2,1,0:T(8,128)S(1)}, f32[4,32,256]{2,1,0:T(8,128)S(1)}, u32[]{:S(2)}, u32[]{:S(2)}) %collective-permute-start.19) | collective-permute-done | bytes 131104 | tf_op jit(solution)/shard_map/ppermute | solution.py:166
  76.2 1.8 %collective-permute-start.22 = (f32[4,32,256]{2,1,0:T(8,128)S(1)}, f32[4,32,256]{2,1,0:T(8,128)S(1)}, u32[]{:S(2)}, u32[]{:S(2)}) collective-permute-start(f32[4,32,256]{2,1,0:T(8,128)S(1)} %add_add_fusion.own), channel_id=1, source_target_pairs={{0,2},{1,3},{2,0},{3,1},{4,6},{5,7},{6,4},{7,5},{8,10},{9,11},{10,... | collective-permute-start | bytes 393224 | tf_op jit(solution)/shard_map/ppermute | solution.py:166
  78.0 1.7 %collective-permute-start.23 = (f32[4,32,256]{2,1,0:T(8,128)S(1)}, f32[4,32,256]{2,1,0:T(8,128)S(1)}, u32[]{:S(2)}, u32[]{:S(2)}) collective-permute-start(f32[4,32,256]{2,1,0:T(8,128)S(1)} %add_add_fusion.own), channel_id=1, source_target_pairs={{0,1},{1,2},{2,3},{3,0},{4,5},{5,6},{6,7},{7,4},{8,9},{9,10},{10,1... | collective-permute-start | bytes 393224 | tf_op jit(solution)/shard_map/ppermute | solution.py:166
  79.7 1.5 %collective-permute-start.24 = (f32[4,32,256]{2,1,0:T(8,128)S(1)}, f32[4,32,256]{2,1,0:T(8,128)S(1)}, u32[]{:S(2)}, u32[]{:S(2)}) collective-permute-start(f32[4,32,256]{2,1,0:T(8,128)S(1)} %add_add_fusion.own), channel_id=1, source_target_pairs={{0,3},{1,0},{2,1},{3,2},{4,7},{5,4},{6,5},{7,6},{8,11},{9,8},{10,9... | collective-permute-start | bytes 393224 | tf_op jit(solution)/shard_map/ppermute | solution.py:166
  81.2 1.5 %collective-permute-done.22.second = f32[4,32,256]{2,1,0:T(8,128)S(1)} collective-permute-done((f32[4,32,256]{2,1,0:T(8,128)S(1)}, f32[4,32,256]{2,1,0:T(8,128)S(1)}, u32[]{:S(2)}, u32[]{:S(2)}) %collective-permute-start.22) | collective-permute-done | bytes 131104 | tf_op jit(solution)/shard_map/ppermute | solution.py:166
  82.7 1.5 %collective-permute-done.23.first = f32[4,32,256]{2,1,0:T(8,128)S(1)} collective-permute-done((f32[4,32,256]{2,1,0:T(8,128)S(1)}, f32[4,32,256]{2,1,0:T(8,128)S(1)}, u32[]{:S(2)}, u32[]{:S(2)}) %collective-permute-start.23) | collective-permute-done | bytes 131104 | tf_op jit(solution)/shard_map/ppermute | solution.py:166
  86.6 3.2 %collective-permute-start.28 = (f32[48,128]{1,0:T(8,128)S(1)}, f32[48,128]{1,0:T(8,128)S(1)}, u32[]{:S(2)}, u32[]{:S(2)}) collective-permute-start(f32[48,128]{1,0:T(8,128)S(1)} %add.106), channel_id=1, source_target_pairs={{0,192},{4,196},{8,200},{12,204},{16,208},{20,212},{24,216},{28,22... | collective-permute-start | bytes 73736 | tf_op jit(solution)/shard_map/ppermute | solution.py:166
  89.9 2.0 %collective-permute-done.26 = f32[48,128]{1,0:T(8,128)S(1)} collective-permute-done((f32[48,128]{1,0:T(8,128)S(1)}, f32[48,128]{1,0:T(8,128)S(1)}, u32[]{:S(2)}, u32[]{:S(2)}) %collective-permute-start.26) | collective-permute-done | bytes 24608 | tf_op jit(solution)/shard_map/ppermute | solution.py:166
  91.9 1.4 %collective-permute-start.30 = (f32[48,128]{1,0:T(8,128)S(1)}, f32[48,128]{1,0:T(8,128)S(1)}, u32[]{:S(2)}, u32[]{:S(2)}) collective-permute-start(f32[48,128]{1,0:T(8,128)S(1)} %add_add_fusion.3), channel_id=1, source_target_pairs={{0,48},{4,20},{8,56},{12,28},{16,0},{20,36},{24,8},{28,44},{32,16}... | collective-permute-start | bytes 73736 | tf_op jit(solution)/shard_map/ppermute | solution.py:166
  93.3 6.5 %collective-permute-start.29 = (f32[48,128]{1,0:T(8,128)S(1)}, f32[48,128]{1,0:T(8,128)S(1)}, u32[]{:S(2)}, u32[]{:S(2)}) collective-permute-start(f32[48,128]{1,0:T(8,128)S(1)} %add_add_fusion.3), channel_id=1, source_target_pairs={{0,32},{4,36},{8,40},{12,44},{16,48},{20,52},{24,56},{28,60},{32,0... | collective-permute-start | bytes 73736 | tf_op jit(solution)/shard_map/ppermute | solution.py:166
  101.9 4.2 %shard_map.93 = (f32[32,256]{1,0:T(8,128)}, f32[2,32,64]{2,1,0:T(8,128)}, f32[2,32,32]{2,1,0:T(8,128)}) custom-call(f32[48,128]{1,0:T(8,128)S(1)} %add_add_fusion.2.gram_ref, f32[4,32,256]{2,1,0:T(8,128)S(1)} %pad_maximum_fusion.q_ref.rest_4_.s_ref, f32[4,32,256]{2,1,0:T(8,128)S(1)} %shard_map.88.q_ref.rest_4_.y_ref, f32[4,32,256]{2,1,0:T(8,128)S(1)} %shard_map.91.z_ref), custom_call_target="tpu_custom_call" | custom-call | tf_op jit(solution)/shard_map/pallas_call | solution.py:270
  (68 shorter events, 13.5 us)
Async XLA Ops:
  0.6 10.1 %collective-permute-start = (f32[32,256]{1,0:T(8,128)}, f32[32,256]{1,0:T(8,128)S(1)}, u32[]{:S(2)}, u32[]{:S(2)}) collective-permute-start(f32[32,256]{1,0:T(8,128)} %start_ref.1), channel_id=1, source_target_pairs={{0,1},{1,2},{2,3},{3,0},{4,5},{5,6},{6,7},{7,4},{8,9},{9,10},{10,1... | collective-permute-start | bytes 98312 | tf_op jit(solution)/shard_map/ppermute | solution.py:166
  2.2 8.5 %collective-permute-start.1 = (f32[32,256]{1,0:T(8,128)}, f32[32,256]{1,0:T(8,128)S(1)}, u32[]{:S(2)}, u32[]{:S(2)}) collective-permute-start(f32[32,256]{1,0:T(8,128)} %start_ref.1), channel_id=1, source_target_pairs={{0,2},{1,3},{2,0},{3,1},{4,6},{5,7},{6,4},{7,5},{8,10},{9,11},{10,... | collective-permute-start | bytes 98312 | tf_op jit(solution)/shard_map/ppermute | solution.py:166
  4.9 5.8 %collective-permute-start.2 = (f32[32,256]{1,0:T(8,128)}, f32[32,256]{1,0:T(8,128)S(1)}, u32[]{:S(2)}, u32[]{:S(2)}) collective-permute-start(f32[32,256]{1,0:T(8,128)} %start_ref.1), channel_id=1, source_target_pairs={{0,3},{1,0},{2,1},{3,2},{4,7},{5,4},{6,5},{7,6},{8,11},{9,8},{10,9... | collective-permute-start | bytes 98312 | tf_op jit(solution)/shard_map/ppermute | solution.py:166
  10.7 11.6 %collective-permute-start.3 = (f32[4,32,256]{2,1,0:T(8,128)S(1)}, f32[4,32,256]{2,1,0:T(8,128)S(1)}, u32[]{:S(2)}, u32[]{:S(2)}) collective-permute-start(f32[4,32,256]{2,1,0:T(8,128)S(1)} %pad_maximum_fusion.q_ref.rest_4_.s_ref), channel_id=1, source_target_pairs={{0,240},{4,244},{8,248},{12,252},{16,0},{20,4},{24,8},{28,12},{32,... | collective-permute-start | bytes 393224 | tf_op jit(solution)/shard_map/ppermute | solution.py:166
  18.7 9.8 %collective-permute-start.5 = (f32[4,32,256]{2,1,0:T(8,128)S(1)}, f32[4,32,256]{2,1,0:T(8,128)S(1)}, u32[]{:S(2)}, u32[]{:S(2)}) collective-permute-start(f32[4,32,256]{2,1,0:T(8,128)S(1)} %pad_maximum_fusion.q_ref.rest_4_.s_ref), channel_id=1, source_target_pairs={{0,192},{4,196},{8,200},{12,204},{16,208},{20,212},{24,216},{28,22... | collective-permute-start | bytes 393224 | tf_op jit(solution)/shard_map/ppermute | solution.py:166
  20.9 11.4 %collective-permute-start.7 = (f32[4,32,256]{2,1,0:T(8,128)S(1)}, f32[4,32,256]{2,1,0:T(8,128)S(1)}, u32[]{:S(2)}, u32[]{:S(2)}) collective-permute-start(f32[4,32,256]{2,1,0:T(8,128)S(1)} %get-tuple-element.18), channel_id=1, source_target_pairs={{0,16},{4,20},{8,24},{12,28},{16,32},{20,36},{24,40},{28,44},{32,4... | collective-permute-start | bytes 393224 | tf_op jit(solution)/shard_map/ppermute | solution.py:166
  21.0 11.4 %collective-permute-start.9 = (f32[4,32,256]{2,1,0:T(8,128)S(1)}, f32[4,32,256]{2,1,0:T(8,128)S(1)}, u32[]{:S(2)}, u32[]{:S(2)}) collective-permute-start(f32[4,32,256]{2,1,0:T(8,128)S(1)} %get-tuple-element.20), channel_id=1, source_target_pairs={{0,64},{4,68},{8,72},{12,76},{16,80},{20,84},{24,88},{28,92},{32,9... | collective-permute-start | bytes 393224 | tf_op jit(solution)/shard_map/ppermute | solution.py:166
  22.4 10.2 %collective-permute-start.4 = (f32[4,32,256]{2,1,0:T(8,128)S(1)}, f32[4,32,256]{2,1,0:T(8,128)S(1)}, u32[]{:S(2)}, u32[]{:S(2)}) collective-permute-start(f32[4,32,256]{2,1,0:T(8,128)S(1)} %collective-permute-done.3.rest_0_), channel_id=1, source_target_pairs={{0,240},{4,244},{8,248},{12,252},{16,0},{20,4},{24,8},{28,12},{32,... | collective-permute-start | bytes 393224 | tf_op jit(solution)/shard_map/ppermute | solution.py:166
  28.5 5.0 %collective-permute-start.6 = (f32[4,32,256]{2,1,0:T(8,128)S(1)}, f32[4,32,256]{2,1,0:T(8,128)S(1)}, u32[]{:S(2)}, u32[]{:S(2)}) collective-permute-start(f32[4,32,256]{2,1,0:T(8,128)S(1)} %collective-permute-done.5.rest_2_), channel_id=1, source_target_pairs={{0,192},{4,196},{8,200},{12,204},{16,208},{20,212},{24,216},{28,22... | collective-permute-start | bytes 393224 | tf_op jit(solution)/shard_map/ppermute | solution.py:166
  32.3 9.9 %collective-permute-start.8 = (f32[4,32,256]{2,1,0:T(8,128)S(1)}, f32[4,32,256]{2,1,0:T(8,128)S(1)}, u32[]{:S(2)}, u32[]{:S(2)}) collective-permute-start(f32[4,32,256]{2,1,0:T(8,128)S(1)} %add.98), channel_id=1, source_target_pairs={{0,16},{4,20},{8,24},{12,28},{16,32},{20,36},{24,40},{28,44},{32,4... | collective-permute-start | bytes 393224 | tf_op jit(solution)/shard_map/ppermute | solution.py:166
  32.4 9.7 %collective-permute-start.10 = (f32[4,32,256]{2,1,0:T(8,128)S(1)}, f32[4,32,256]{2,1,0:T(8,128)S(1)}, u32[]{:S(2)}, u32[]{:S(2)}) collective-permute-start(f32[4,32,256]{2,1,0:T(8,128)S(1)} %add.100), channel_id=1, source_target_pairs={{0,64},{4,68},{8,72},{12,76},{16,80},{20,84},{24,88},{28,92},{32,9... | collective-permute-start | bytes 393224 | tf_op jit(solution)/shard_map/ppermute | solution.py:166
  42.2 6.7 %collective-permute-start.11 = (f32[4,32,256]{2,1,0:T(8,128)S(1)}, f32[4,32,256]{2,1,0:T(8,128)S(1)}, u32[]{:S(2)}, u32[]{:S(2)}) collective-permute-start(f32[4,32,256]{2,1,0:T(8,128)S(1)} %add_add_fusion.1.own), channel_id=1, source_target_pairs={{0,2},{1,3},{2,0},{3,1},{4,6},{5,7},{6,4},{7,5},{8,10},{9,11},{10,... | collective-permute-start | bytes 393224 | tf_op jit(solution)/shard_map/ppermute | solution.py:166
  42.8 7.4 %collective-permute-start.12 = (f32[4,32,256]{2,1,0:T(8,128)S(1)}, f32[4,32,256]{2,1,0:T(8,128)S(1)}, u32[]{:S(2)}, u32[]{:S(2)}) collective-permute-start(f32[4,32,256]{2,1,0:T(8,128)S(1)} %add_add_fusion.1.own), channel_id=1, source_target_pairs={{0,1},{1,2},{2,3},{3,0},{4,5},{5,6},{6,7},{7,4},{8,9},{9,10},{10,1... | collective-permute-start | bytes 393224 | tf_op jit(solution)/shard_map/ppermute | solution.py:166
  43.8 6.4 %collective-permute-start.13 = (f32[4,32,256]{2,1,0:T(8,128)S(1)}, f32[4,32,256]{2,1,0:T(8,128)S(1)}, u32[]{:S(2)}, u32[]{:S(2)}) collective-permute-start(f32[4,32,256]{2,1,0:T(8,128)S(1)} %add_add_fusion.1.own), channel_id=1, source_target_pairs={{0,3},{1,0},{2,1},{3,2},{4,7},{5,4},{6,5},{7,6},{8,11},{9,8},{10,9... | collective-permute-start | bytes 393224 | tf_op jit(solution)/shard_map/ppermute | solution.py:166
  50.2 7.9 %collective-permute-start.14 = (f32[4,32,256]{2,1,0:T(8,128)S(1)}, f32[4,32,256]{2,1,0:T(8,128)S(1)}, u32[]{:S(2)}, u32[]{:S(2)}) collective-permute-start(f32[4,32,256]{2,1,0:T(8,128)S(1)} %shard_map.88.q_ref.rest_4_.y_ref), channel_id=1, source_target_pairs={{0,240},{4,244},{8,248},{12,252},{16,0},{20,4},{24,8},{28,12},{32,... | collective-permute-start | bytes 393224 | tf_op jit(solution)/shard_map/ppermute | solution.py:166
  52.0 12.8 %collective-permute-start.16 = (f32[4,32,256]{2,1,0:T(8,128)S(1)}, f32[4,32,256]{2,1,0:T(8,128)S(1)}, u32[]{:S(2)}, u32[]{:S(2)}) collective-permute-start(f32[4,32,256]{2,1,0:T(8,128)S(1)} %shard_map.88.q_ref.rest_4_.y_ref), channel_id=1, source_target_pairs={{0,192},{4,196},{8,200},{12,204},{16,208},{20,212},{24,216},{28,22... | collective-permute-start | bytes 393224 | tf_op jit(solution)/shard_map/ppermute | solution.py:166
  53.5 13.2 %collective-permute-start.18 = (f32[4,32,256]{2,1,0:T(8,128)S(1)}, f32[4,32,256]{2,1,0:T(8,128)S(1)}, u32[]{:S(2)}, u32[]{:S(2)}) collective-permute-start(f32[4,32,256]{2,1,0:T(8,128)S(1)} %get-tuple-element.23), channel_id=1, source_target_pairs={{0,16},{4,20},{8,24},{12,28},{16,32},{20,36},{24,40},{28,44},{32,4... | collective-permute-start | bytes 393224 | tf_op jit(solution)/shard_map/ppermute | solution.py:166
  55.0 11.8 %collective-permute-start.20 = (f32[4,32,256]{2,1,0:T(8,128)S(1)}, f32[4,32,256]{2,1,0:T(8,128)S(1)}, u32[]{:S(2)}, u32[]{:S(2)}) collective-permute-start(f32[4,32,256]{2,1,0:T(8,128)S(1)} %get-tuple-element.25), channel_id=1, source_target_pairs={{0,64},{4,68},{8,72},{12,76},{16,80},{20,84},{24,88},{28,92},{32,9... | collective-permute-start | bytes 393224 | tf_op jit(solution)/shard_map/ppermute | solution.py:166
  58.1 9.2 %collective-permute-start.15 = (f32[4,32,256]{2,1,0:T(8,128)S(1)}, f32[4,32,256]{2,1,0:T(8,128)S(1)}, u32[]{:S(2)}, u32[]{:S(2)}) collective-permute-start(f32[4,32,256]{2,1,0:T(8,128)S(1)} %collective-permute-done.14.rest_0_), channel_id=1, source_target_pairs={{0,240},{4,244},{8,248},{12,252},{16,0},{20,4},{24,8},{28,12},{32,... | collective-permute-start | bytes 393224 | tf_op jit(solution)/shard_map/ppermute | solution.py:166
  64.8 5.0 %collective-permute-start.17 = (f32[4,32,256]{2,1,0:T(8,128)S(1)}, f32[4,32,256]{2,1,0:T(8,128)S(1)}, u32[]{:S(2)}, u32[]{:S(2)}) collective-permute-start(f32[4,32,256]{2,1,0:T(8,128)S(1)} %collective-permute-done.16.rest_2_), channel_id=1, source_target_pairs={{0,192},{4,196},{8,200},{12,204},{16,208},{20,212},{24,216},{28,22... | collective-permute-start | bytes 393224 | tf_op jit(solution)/shard_map/ppermute | solution.py:166
  66.8 9.4 %collective-permute-start.19 = (f32[4,32,256]{2,1,0:T(8,128)S(1)}, f32[4,32,256]{2,1,0:T(8,128)S(1)}, u32[]{:S(2)}, u32[]{:S(2)}) collective-permute-start(f32[4,32,256]{2,1,0:T(8,128)S(1)} %add.102), channel_id=1, source_target_pairs={{0,16},{4,20},{8,24},{12,28},{16,32},{20,36},{24,40},{28,44},{32,4... | collective-permute-start | bytes 393224 | tf_op jit(solution)/shard_map/ppermute | solution.py:166
  66.9 9.2 %collective-permute-start.21 = (f32[4,32,256]{2,1,0:T(8,128)S(1)}, f32[4,32,256]{2,1,0:T(8,128)S(1)}, u32[]{:S(2)}, u32[]{:S(2)}) collective-permute-start(f32[4,32,256]{2,1,0:T(8,128)S(1)} %add.104), channel_id=1, source_target_pairs={{0,64},{4,68},{8,72},{12,76},{16,80},{20,84},{24,88},{28,92},{32,9... | collective-permute-start | bytes 393224 | tf_op jit(solution)/shard_map/ppermute | solution.py:166
  76.2 6.6 %collective-permute-start.22 = (f32[4,32,256]{2,1,0:T(8,128)S(1)}, f32[4,32,256]{2,1,0:T(8,128)S(1)}, u32[]{:S(2)}, u32[]{:S(2)}) collective-permute-start(f32[4,32,256]{2,1,0:T(8,128)S(1)} %add_add_fusion.own), channel_id=1, source_target_pairs={{0,2},{1,3},{2,0},{3,1},{4,6},{5,7},{6,4},{7,5},{8,10},{9,11},{10,... | collective-permute-start | bytes 393224 | tf_op jit(solution)/shard_map/ppermute | solution.py:166
  78.0 6.2 %collective-permute-start.23 = (f32[4,32,256]{2,1,0:T(8,128)S(1)}, f32[4,32,256]{2,1,0:T(8,128)S(1)}, u32[]{:S(2)}, u32[]{:S(2)}) collective-permute-start(f32[4,32,256]{2,1,0:T(8,128)S(1)} %add_add_fusion.own), channel_id=1, source_target_pairs={{0,1},{1,2},{2,3},{3,0},{4,5},{5,6},{6,7},{7,4},{8,9},{9,10},{10,1... | collective-permute-start | bytes 393224 | tf_op jit(solution)/shard_map/ppermute | solution.py:166
  79.7 5.0 %collective-permute-start.24 = (f32[4,32,256]{2,1,0:T(8,128)S(1)}, f32[4,32,256]{2,1,0:T(8,128)S(1)}, u32[]{:S(2)}, u32[]{:S(2)}) collective-permute-start(f32[4,32,256]{2,1,0:T(8,128)S(1)} %add_add_fusion.own), channel_id=1, source_target_pairs={{0,3},{1,0},{2,1},{3,2},{4,7},{5,4},{6,5},{7,6},{8,11},{9,8},{10,9... | collective-permute-start | bytes 393224 | tf_op jit(solution)/shard_map/ppermute | solution.py:166
  86.5 5.4 %collective-permute-start.26 = (f32[48,128]{1,0:T(8,128)S(1)}, f32[48,128]{1,0:T(8,128)S(1)}, u32[]{:S(2)}, u32[]{:S(2)}) collective-permute-start(f32[48,128]{1,0:T(8,128)S(1)} %add.106), channel_id=1, source_target_pairs={{0,128},{4,132},{8,136},{12,140},{16,144},{20,148},{24,152},{28,15... | collective-permute-start | bytes 73736 | tf_op jit(solution)/shard_map/ppermute | solution.py:166
  86.5 5.4 %collective-permute-start.27 = (f32[48,128]{1,0:T(8,128)S(1)}, f32[48,128]{1,0:T(8,128)S(1)}, u32[]{:S(2)}, u32[]{:S(2)}) collective-permute-start(f32[48,128]{1,0:T(8,128)S(1)} %add.106), channel_id=1, source_target_pairs={{0,64},{4,68},{8,72},{12,76},{16,80},{20,84},{24,88},{28,92},{32,9... | collective-permute-start | bytes 73736 | tf_op jit(solution)/shard_map/ppermute | solution.py:166
  86.6 5.3 %collective-permute-start.28 = (f32[48,128]{1,0:T(8,128)S(1)}, f32[48,128]{1,0:T(8,128)S(1)}, u32[]{:S(2)}, u32[]{:S(2)}) collective-permute-start(f32[48,128]{1,0:T(8,128)S(1)} %add.106), channel_id=1, source_target_pairs={{0,192},{4,196},{8,200},{12,204},{16,208},{20,212},{24,216},{28,22... | collective-permute-start | bytes 73736 | tf_op jit(solution)/shard_map/ppermute | solution.py:166
  91.9 7.9 %collective-permute-start.30 = (f32[48,128]{1,0:T(8,128)S(1)}, f32[48,128]{1,0:T(8,128)S(1)}, u32[]{:S(2)}, u32[]{:S(2)}) collective-permute-start(f32[48,128]{1,0:T(8,128)S(1)} %add_add_fusion.3), channel_id=1, source_target_pairs={{0,48},{4,20},{8,56},{12,28},{16,0},{20,36},{24,8},{28,44},{32,16}... | collective-permute-start | bytes 73736 | tf_op jit(solution)/shard_map/ppermute | solution.py:166
  93.3 7.1 %collective-permute-start.33 = (f32[48,128]{1,0:T(8,128)S(1)}, f32[48,128]{1,0:T(8,128)S(1)}, u32[]{:S(2)}, u32[]{:S(2)}) collective-permute-start(f32[48,128]{1,0:T(8,128)S(1)} %add_add_fusion.3), channel_id=1, source_target_pairs={{0,40},{4,28},{8,48},{12,36},{16,56},{20,44},{24,0},{28,52},{32,8}... | collective-permute-start | bytes 73736 | tf_op jit(solution)/shard_map/ppermute | solution.py:166
  93.3 7.1 %collective-permute-start.32 = (f32[48,128]{1,0:T(8,128)S(1)}, f32[48,128]{1,0:T(8,128)S(1)}, u32[]{:S(2)}, u32[]{:S(2)}) collective-permute-start(f32[48,128]{1,0:T(8,128)S(1)} %add_add_fusion.3), channel_id=1, source_target_pairs={{0,56},{4,12},{8,0},{12,20},{16,8},{20,28},{24,16},{28,36},{32,24}... | collective-permute-start | bytes 73736 | tf_op jit(solution)/shard_map/ppermute | solution.py:166
  93.3 8.6 %collective-permute-start.29 = (f32[48,128]{1,0:T(8,128)S(1)}, f32[48,128]{1,0:T(8,128)S(1)}, u32[]{:S(2)}, u32[]{:S(2)}) collective-permute-start(f32[48,128]{1,0:T(8,128)S(1)} %add_add_fusion.3), channel_id=1, source_target_pairs={{0,32},{4,36},{8,40},{12,44},{16,48},{20,52},{24,56},{28,60},{32,0... | collective-permute-start | bytes 73736 | tf_op jit(solution)/shard_map/ppermute | solution.py:166
  (7 other events, 40.4 us)

commit v6 on v5

--- a/solution.py
+++ b/solution.py
@@ -74,11 +74,14 @@
         out[b] = (own[b] + second[(b - 2) % n]) + (first[(b - 1) % n] + third[(b - 3) % n])
 
 
-def gram_kernel(s_ref, y_ref, z_ref, out):
+def gram_kernel(second, first, third, own, s_ref, y_ref, z_own, out):
     blocks, k, width = s_ref.shape
     grams = []
     for b in range(blocks):
-        stack = jnp.concatenate([s_ref[b], y_ref[b], z_ref[b], jnp.zeros((k, width), F32)], axis=0)
+        z = (own[b] + second[(b - 2) % blocks]) + (first[(b - 1) % blocks] + third[(b - 3) % blocks])
+        if b == 0:
+            z_own[0] = z
+        stack = jnp.concatenate([s_ref[b], y_ref[b], z, jnp.zeros((k, width), F32)], axis=0)
         grams.append(dot(stack[: 3 * k], stack, NT, HIGHEST))
     half = blocks // 2
     pairs = [grams[i] + grams[i + half] for i in range(half)]
@@ -226,6 +229,9 @@
         cost_estimate=cost,
     )
 
+    def rep_parts(part):
+        return *[shifted(part, "rep", by) for by in (2, 1, 3)], part
+
     def rep_sum(part):
         return pl.pallas_call(
             rep_sum_kernel,
@@ -233,7 +239,7 @@
             in_specs=[vmem] * 4,
             out_specs=vmem,
             compiler_params=params,
-        )(*[shifted(part, "rep", by) for by in (2, 1, 3)], part)
+        )(*rep_parts(part))
 
     def apply(q):
         _, quarter, _, last = offsets
@@ -247,18 +253,20 @@
         v = shifted(out4 + u, "rows", last)
         x = shifted(out16 + w, "rows", quarter)
         part = forward(meta, tiles, kept, got4, got8, got16, got32, q)
-        return rep_sum(part + v + x)
+        return part + v + x
 
     start = jnp.stack([own] + [shifted(start_block, "rep", by) for by in range(1, members)], 0)
-    first = apply(start)
-    second = apply(first)
-    gram = pl.pallas_call(
+    first = rep_sum(apply(start))
+    second, gram = pl.pallas_call(
         gram_kernel,
-        out_shape=jax.ShapeDtypeStruct((k + k // 2, 4 * k), F32),
-        in_specs=[vmem] * 3,
-        out_specs=vmem,
-        compiler_params=params,
-    )(start, first, second)
+        out_shape=[
+            jax.ShapeDtypeStruct((1, k, edge), F32),
+            jax.ShapeDtypeStruct((k + k // 2, 4 * k), F32),
+        ],
+        in_specs=[vmem] * 6,
+        out_specs=[vmem] * 2,
+        compiler_params=params,
+    )(*rep_parts(apply(first)), start, first)
     gram = gram + moved(gram, "rows", lambda i: i ^ 1)
     gram = sum_of_ring(gram, lambda by: shifted(gram, "rows", by * (devices // 4)))
     def along_z(by):

time: 107 us -> 107 us (level)
  no operation moved by 1% of the time
where the time goes in v6:
time: 107 us; the launch traced here: 106 us
  starting transfers between devices  55.7 us (52%)
  waiting for transfers between devices  33.4 us (31%)
  Pallas kernels  11.8 us (11%)
  local copies, waits for them, and re-layouts  2.95 us (3%)
  between operations  1.51 us (1%)
    ppermute x36, starting transfers between devices, moved(): return lax.ppermute(x, axis, [(i, target(i) % size) for i in range(size)])  55.7 us
    ppermute x36, waiting for transfers between devices, moved(): return lax.ppermute(x, axis, [(i, target(i) % size) for i in range(size)])  33.4 us
    pallas_call x1, Pallas kernels, body(): pl.pallas_call(tail_kernel, out_shape=[jax.ShapeDtypeStruct((k, edge), F3...  4.2 us
    pallas_call x2, Pallas kernels, apply(): part = forward(meta, tiles, kept, got4, got8, got16, got32, q)  4.02 us
    pallas_call x2, Pallas kernels, apply(): kept, out32, out16, out8, out4 = backward(meta, tiles, q)  2.97 us
    unnamed x6, local copies, waits for them, and re-layouts  2.95 us
  transfers between devices with their start and end apart: 36, of which 17 were waited for; matrix products, arithmetic and copies ran while one was open for 1% of the time, Pallas kernels for 7%

profile of v6, /device:TPU:32, one launch (start us, length us, event | category | flops | bytes accessed | tf_op | source)
XLA Modules:
  0.0 106.2 jit_solution(12289746029998468798)
XLA Ops:
  0.6 1.6 %collective-permute-start = (f32[32,256]{1,0:T(8,128)}, f32[32,256]{1,0:T(8,128)S(1)}, u32[]{:S(2)}, u32[]{:S(2)}) collective-permute-start(f32[32,256]{1,0:T(8,128)} %start_ref.1), channel_id=1, source_target_pairs={{0,1},{1,2},{2,3},{3,0},{4,5},{5,6},{6,7},{7,4},{8,9},{9,10},{10,1... | collective-permute-start | bytes 98312 | tf_op jit(solution)/shard_map/ppermute | solution.py:169
  2.2 2.7 %collective-permute-start.1 = (f32[32,256]{1,0:T(8,128)}, f32[32,256]{1,0:T(8,128)S(1)}, u32[]{:S(2)}, u32[]{:S(2)}) collective-permute-start(f32[32,256]{1,0:T(8,128)} %start_ref.1), channel_id=1, source_target_pairs={{0,2},{1,3},{2,0},{3,1},{4,6},{5,7},{6,4},{7,5},{8,10},{9,11},{10,... | collective-permute-start | bytes 98312 | tf_op jit(solution)/shard_map/ppermute | solution.py:169
  4.9 1.4 %collective-permute-start.2 = (f32[32,256]{1,0:T(8,128)}, f32[32,256]{1,0:T(8,128)S(1)}, u32[]{:S(2)}, u32[]{:S(2)}) collective-permute-start(f32[32,256]{1,0:T(8,128)} %start_ref.1), channel_id=1, source_target_pairs={{0,3},{1,0},{2,1},{3,2},{4,7},{5,4},{6,5},{7,6},{8,11},{9,8},{10,9... | collective-permute-start | bytes 98312 | tf_op jit(solution)/shard_map/ppermute | solution.py:169
  7.8 2.2 %copy-done = bf16[1,1,32,256,256]{4,3,2,1,0:T(8,128)(2,1)S(1)} copy-done((bf16[1,1,32,256,256]{4,3,2,1,0:T(8,128)(2,1)S(1)}, bf16[1,1,32,256,256]{4,3,2,1,0:T(8,128)(2,1)}, u32[]{:S(2)}) %copy-start) | copy-done | bytes 4194328
  10.7 7.9 %collective-permute-start.3 = (f32[4,32,256]{2,1,0:T(8,128)S(1)}, f32[4,32,256]{2,1,0:T(8,128)S(1)}, u32[]{:S(2)}, u32[]{:S(2)}) collective-permute-start(f32[4,32,256]{2,1,0:T(8,128)S(1)} %pad_maximum_fusion.q_ref.rest_4_.s_ref), channel_id=1, source_target_pairs={{0,240},{4,244},{8,248},{12,252},{16,0},{20,4},{24,8},{28,12},{32,... | collective-permute-start | bytes 393224 | tf_op jit(solution)/shard_map/ppermute | solution.py:169
  19.4 1.5 %shard_map.86 = (f32[4,32,256]{2,1,0:T(8,128)S(1)}, f32[4,32,256]{2,1,0:T(8,128)S(1)}, f32[4,32,256]{2,1,0:T(8,128)S(1)}, f32[4,32,256]{2,1,0:T(8,128)S(1)}, f32[4,32,256]{2,1,0:T(8,128)S(1)}) custom-call(s32[3,32]{1,0:T(4,128)S(1)} %pad_add_fusion.meta, bf16[32,256,256]{2,1,0:T(8,128)(2,1)S(1)} %bitcast.16, ...), custom_call_target="tpu_custom_call" | custom-call | flops 268435456 | bytes 4194304 | tf_op jit(solution)/shard_map/pallas_call | solution.py:246
  21.0 1.4 %collective-permute-start.9 = (f32[4,32,256]{2,1,0:T(8,128)S(1)}, f32[4,32,256]{2,1,0:T(8,128)S(1)}, u32[]{:S(2)}, u32[]{:S(2)}) collective-permute-start(f32[4,32,256]{2,1,0:T(8,128)S(1)} %get-tuple-element.22), channel_id=1, source_target_pairs={{0,64},{4,68},{8,72},{12,76},{16,80},{20,84},{24,88},{28,92},{32,9... | collective-permute-start | bytes 393224 | tf_op jit(solution)/shard_map/ppermute | solution.py:169
  22.3 6.2 %collective-permute-start.4 = (f32[4,32,256]{2,1,0:T(8,128)S(1)}, f32[4,32,256]{2,1,0:T(8,128)S(1)}, u32[]{:S(2)}, u32[]{:S(2)}) collective-permute-start(f32[4,32,256]{2,1,0:T(8,128)S(1)} %collective-permute-done.3.rest_0_), channel_id=1, source_target_pairs={{0,240},{4,244},{8,248},{12,252},{16,0},{20,4},{24,8},{28,12},{32,... | collective-permute-start | bytes 393224 | tf_op jit(solution)/shard_map/ppermute | solution.py:169
  29.2 3.1 %collective-permute-done.7 = f32[4,32,256]{2,1,0:T(8,128)S(1)} collective-permute-done((f32[4,32,256]{2,1,0:T(8,128)S(1)}, f32[4,32,256]{2,1,0:T(8,128)S(1)}, u32[]{:S(2)}, u32[]{:S(2)}) %collective-permute-start.7) | collective-permute-done | bytes 131104 | tf_op jit(solution)/shard_map/ppermute | solution.py:169
  33.5 2.0 %shard_map.87 = f32[4,32,256]{2,1,0:T(8,128)S(1)} custom-call(s32[3,32]{1,0:T(4,128)S(1)} %pad_add_fusion.meta, bf16[32,256,256]{2,1,0:T(8,128)(2,1)S(1)} %bitcast.17, f32[4,32,256]{2,1,0:T(8,128)S(1)} %get-tuple-element.18.kept_ref, f32[4,32,256]{2,1,0:T(8,128)S(1)} %collective-permute-done.3.rest_0_, f32[4,32,256]{2,1,0:T(8,128)S(1)} %collective-permute-done.4.rest_1_, ...), custom_call_target="tpu_custom_call" | custom-call | flops 268435456 | bytes 4194304 | tf_op jit(solution)/shard_map/pallas_call | solution.py:255
  35.5 6.7 %collective-permute-done.8 = f32[4,32,256]{2,1,0:T(8,128)S(1)} collective-permute-done((f32[4,32,256]{2,1,0:T(8,128)S(1)}, f32[4,32,256]{2,1,0:T(8,128)S(1)}, u32[]{:S(2)}, u32[]{:S(2)}) %collective-permute-start.8) | collective-permute-done | bytes 131104 | tf_op jit(solution)/shard_map/ppermute | solution.py:169
  43.8 2.3 %collective-permute-start.13 = (f32[4,32,256]{2,1,0:T(8,128)S(1)}, f32[4,32,256]{2,1,0:T(8,128)S(1)}, u32[]{:S(2)}, u32[]{:S(2)}) collective-permute-start(f32[4,32,256]{2,1,0:T(8,128)S(1)} %add_add_fusion.1.own), channel_id=1, source_target_pairs={{0,3},{1,0},{2,1},{3,2},{4,7},{5,4},{6,5},{7,6},{8,11},{9,8},{10,9... | collective-permute-start | bytes 393224 | tf_op jit(solution)/shard_map/ppermute | solution.py:169
  46.1 2.8 %collective-permute-done.11.second = f32[4,32,256]{2,1,0:T(8,128)S(1)} collective-permute-done((f32[4,32,256]{2,1,0:T(8,128)S(1)}, f32[4,32,256]{2,1,0:T(8,128)S(1)}, u32[]{:S(2)}, u32[]{:S(2)}) %collective-permute-start.11) | collective-permute-done | bytes 131104 | tf_op jit(solution)/shard_map/ppermute | solution.py:169
  50.2 1.8 %collective-permute-start.14 = (f32[4,32,256]{2,1,0:T(8,128)S(1)}, f32[4,32,256]{2,1,0:T(8,128)S(1)}, u32[]{:S(2)}, u32[]{:S(2)}) collective-permute-start(f32[4,32,256]{2,1,0:T(8,128)S(1)} %shard_map.88.q_ref.rest_4_.y_ref), channel_id=1, source_target_pairs={{0,240},{4,244},{8,248},{12,252},{16,0},{20,4},{24,8},{28,12},{32,... | collective-permute-start | bytes 393224 | tf_op jit(solution)/shard_map/ppermute | solution.py:169
  52.0 1.5 %shard_map.89 = (f32[4,32,256]{2,1,0:T(8,128)S(1)}, f32[4,32,256]{2,1,0:T(8,128)S(1)}, f32[4,32,256]{2,1,0:T(8,128)S(1)}, f32[4,32,256]{2,1,0:T(8,128)S(1)}, f32[4,32,256]{2,1,0:T(8,128)S(1)}) custom-call(s32[3,32]{1,0:T(4,128)S(1)} %pad_add_fusion.meta, bf16[32,256,256]{2,1,0:T(8,128)(2,1)S(1)} %bitcast.18, f32[4,32,256]{2,1,0:T(8,128)S(1)} %shard_map.88.q_ref.rest_4_.y_ref), custom_call_target="tpu_custom_call" | custom-call | flops 268435456 | bytes 4194304 | tf_op jit(solution)/shard_map/pallas_call | solution.py:246
  53.6 1.4 %collective-permute-start.18 = (f32[4,32,256]{2,1,0:T(8,128)S(1)}, f32[4,32,256]{2,1,0:T(8,128)S(1)}, u32[]{:S(2)}, u32[]{:S(2)}) collective-permute-start(f32[4,32,256]{2,1,0:T(8,128)S(1)} %get-tuple-element.25), channel_id=1, source_target_pairs={{0,16},{4,20},{8,24},{12,28},{16,32},{20,36},{24,40},{28,44},{32,4... | collective-permute-start | bytes 393224 | tf_op jit(solution)/shard_map/ppermute | solution.py:169
  55.0 2.0 %collective-permute-start.20 = (f32[4,32,256]{2,1,0:T(8,128)S(1)}, f32[4,32,256]{2,1,0:T(8,128)S(1)}, u32[]{:S(2)}, u32[]{:S(2)}) collective-permute-start(f32[4,32,256]{2,1,0:T(8,128)S(1)} %get-tuple-element.27), channel_id=1, source_target_pairs={{0,64},{4,68},{8,72},{12,76},{16,80},{20,84},{24,88},{28,92},{32,9... | collective-permute-start | bytes 393224 | tf_op jit(solution)/shard_map/ppermute | solution.py:169
  58.2 6.7 %collective-permute-start.15 = (f32[4,32,256]{2,1,0:T(8,128)S(1)}, f32[4,32,256]{2,1,0:T(8,128)S(1)}, u32[]{:S(2)}, u32[]{:S(2)}) collective-permute-start(f32[4,32,256]{2,1,0:T(8,128)S(1)} %collective-permute-done.14.rest_0_), channel_id=1, source_target_pairs={{0,240},{4,244},{8,248},{12,252},{16,0},{20,4},{24,8},{28,12},{32,... | collective-permute-start | bytes 393224 | tf_op jit(solution)/shard_map/ppermute | solution.py:169
  64.9 1.9 %collective-permute-done.18 = f32[4,32,256]{2,1,0:T(8,128)S(1)} collective-permute-done((f32[4,32,256]{2,1,0:T(8,128)S(1)}, f32[4,32,256]{2,1,0:T(8,128)S(1)}, u32[]{:S(2)}, u32[]{:S(2)}) %collective-permute-start.18) | collective-permute-done | bytes 131104 | tf_op jit(solution)/shard_map/ppermute | solution.py:169
  67.4 2.4 %collective-permute-done.17.rest_3_ = f32[4,32,256]{2,1,0:T(8,128)S(1)} collective-permute-done((f32[4,32,256]{2,1,0:T(8,128)S(1)}, f32[4,32,256]{2,1,0:T(8,128)S(1)}, u32[]{:S(2)}, u32[]{:S(2)}) %collective-permute-start.17) | collective-permute-done | bytes 131104 | tf_op jit(solution)/shard_map/ppermute | solution.py:169
  69.8 2.0 %shard_map.90 = f32[4,32,256]{2,1,0:T(8,128)S(1)} custom-call(s32[3,32]{1,0:T(4,128)S(1)} %pad_add_fusion.meta, bf16[32,256,256]{2,1,0:T(8,128)(2,1)S(1)} %bitcast.19, f32[4,32,256]{2,1,0:T(8,128)S(1)} %get-tuple-element.23.kept_ref, f32[4,32,256]{2,1,0:T(8,128)S(1)} %collective-permute-done.14.rest_0_, f32[4,32,256]{2,1,0:T(8,128)S(1)} %collective-permute-done.15.rest_1_, ...), custom_call_target="tpu_custom_call" | custom-call | flops 268435456 | bytes 4194304 | tf_op jit(solution)/shard_map/pallas_call | solution.py:255
  71.8 4.6 %collective-permute-done.19 = f32[4,32,256]{2,1,0:T(8,128)S(1)} collective-permute-done((f32[4,32,256]{2,1,0:T(8,128)S(1)}, f32[4,32,256]{2,1,0:T(8,128)S(1)}, u32[]{:S(2)}, u32[]{:S(2)}) %collective-permute-start.19) | collective-permute-done | bytes 131104 | tf_op jit(solution)/shard_map/ppermute | solution.py:169
  76.5 1.5 %collective-permute-start.22 = (f32[4,32,256]{2,1,0:T(8,128)S(1)}, f32[4,32,256]{2,1,0:T(8,128)S(1)}, u32[]{:S(2)}, u32[]{:S(2)}) collective-permute-start(f32[4,32,256]{2,1,0:T(8,128)S(1)} %add_add_fusion.own), channel_id=1, source_target_pairs={{0,2},{1,3},{2,0},{3,1},{4,6},{5,7},{6,4},{7,5},{8,10},{9,11},{10,... | collective-permute-start | bytes 393224 | tf_op jit(solution)/shard_map/ppermute | solution.py:169
  78.0 1.7 %collective-permute-start.23 = (f32[4,32,256]{2,1,0:T(8,128)S(1)}, f32[4,32,256]{2,1,0:T(8,128)S(1)}, u32[]{:S(2)}, u32[]{:S(2)}) collective-permute-start(f32[4,32,256]{2,1,0:T(8,128)S(1)} %add_add_fusion.own), channel_id=1, source_target_pairs={{0,1},{1,2},{2,3},{3,0},{4,5},{5,6},{6,7},{7,4},{8,9},{9,10},{10,1... | collective-permute-start | bytes 393224 | tf_op jit(solution)/shard_map/ppermute | solution.py:169
  79.7 1.5 %collective-permute-start.24 = (f32[4,32,256]{2,1,0:T(8,128)S(1)}, f32[4,32,256]{2,1,0:T(8,128)S(1)}, u32[]{:S(2)}, u32[]{:S(2)}) collective-permute-start(f32[4,32,256]{2,1,0:T(8,128)S(1)} %add_add_fusion.own), channel_id=1, source_target_pairs={{0,3},{1,0},{2,1},{3,2},{4,7},{5,4},{6,5},{7,6},{8,11},{9,8},{10,9... | collective-permute-start | bytes 393224 | tf_op jit(solution)/shard_map/ppermute | solution.py:169
  81.2 1.8 %collective-permute-done.22.second = f32[4,32,256]{2,1,0:T(8,128)S(1)} collective-permute-done((f32[4,32,256]{2,1,0:T(8,128)S(1)}, f32[4,32,256]{2,1,0:T(8,128)S(1)}, u32[]{:S(2)}, u32[]{:S(2)}) %collective-permute-start.22) | collective-permute-done | bytes 131104 | tf_op jit(solution)/shard_map/ppermute | solution.py:169
  83.0 1.4 %collective-permute-done.23.first = f32[4,32,256]{2,1,0:T(8,128)S(1)} collective-permute-done((f32[4,32,256]{2,1,0:T(8,128)S(1)}, f32[4,32,256]{2,1,0:T(8,128)S(1)}, u32[]{:S(2)}, u32[]{:S(2)}) %collective-permute-start.23) | collective-permute-done | bytes 131104 | tf_op jit(solution)/shard_map/ppermute | solution.py:169
  86.6 3.2 %collective-permute-start.28 = (f32[48,128]{1,0:T(8,128)S(1)}, f32[48,128]{1,0:T(8,128)S(1)}, u32[]{:S(2)}, u32[]{:S(2)}) collective-permute-start(f32[48,128]{1,0:T(8,128)S(1)} %add.106), channel_id=1, source_target_pairs={{0,192},{4,196},{8,200},{12,204},{16,208},{20,212},{24,216},{28,22... | collective-permute-start | bytes 73736 | tf_op jit(solution)/shard_map/ppermute | solution.py:169
  89.8 2.0 %collective-permute-done.26 = f32[48,128]{1,0:T(8,128)S(1)} collective-permute-done((f32[48,128]{1,0:T(8,128)S(1)}, f32[48,128]{1,0:T(8,128)S(1)}, u32[]{:S(2)}, u32[]{:S(2)}) %collective-permute-start.26) | collective-permute-done | bytes 24608 | tf_op jit(solution)/shard_map/ppermute | solution.py:169
  91.9 1.5 %collective-permute-start.30 = (f32[48,128]{1,0:T(8,128)S(1)}, f32[48,128]{1,0:T(8,128)S(1)}, u32[]{:S(2)}, u32[]{:S(2)}) collective-permute-start(f32[48,128]{1,0:T(8,128)S(1)} %add_add_fusion.3), channel_id=1, source_target_pairs={{0,48},{4,20},{8,56},{12,28},{16,0},{20,36},{24,8},{28,44},{32,16}... | collective-permute-start | bytes 73736 | tf_op jit(solution)/shard_map/ppermute | solution.py:169
  93.4 6.5 %collective-permute-start.29 = (f32[48,128]{1,0:T(8,128)S(1)}, f32[48,128]{1,0:T(8,128)S(1)}, u32[]{:S(2)}, u32[]{:S(2)}) collective-permute-start(f32[48,128]{1,0:T(8,128)S(1)} %add_add_fusion.3), channel_id=1, source_target_pairs={{0,32},{4,36},{8,40},{12,44},{16,48},{20,52},{24,56},{28,60},{32,0... | collective-permute-start | bytes 73736 | tf_op jit(solution)/shard_map/ppermute | solution.py:169
  102.0 4.2 %shard_map.92 = (f32[32,256]{1,0:T(8,128)}, f32[2,32,64]{2,1,0:T(8,128)}, f32[2,32,32]{2,1,0:T(8,128)}) custom-call(f32[48,128]{1,0:T(8,128)S(1)} %add_add_fusion.2.gram_ref, f32[4,32,256]{2,1,0:T(8,128)S(1)} %pad_maximum_fusion.q_ref.rest_4_.s_ref, f32[4,32,256]{2,1,0:T(8,128)S(1)} %shard_map.88.q_ref.rest_4_.y_ref, f32[1,32,256]{2,1,0:T(8,128)S(1)} %get-tuple-element.29.z_ref), custom_call_target="tpu_custom_call" | custom-call | tf_op jit(solution)/shard_map/pallas_call | solution.py:278
  (67 shorter events, 13.1 us)
Async XLA Ops:
  0.6 10.1 %collective-permute-start = (f32[32,256]{1,0:T(8,128)}, f32[32,256]{1,0:T(8,128)S(1)}, u32[]{:S(2)}, u32[]{:S(2)}) collective-permute-start(f32[32,256]{1,0:T(8,128)} %start_ref.1), channel_id=1, source_target_pairs={{0,1},{1,2},{2,3},{3,0},{4,5},{5,6},{6,7},{7,4},{8,9},{9,10},{10,1... | collective-permute-start | bytes 98312 | tf_op jit(solution)/shard_map/ppermute | solution.py:169
  2.2 8.5 %collective-permute-start.1 = (f32[32,256]{1,0:T(8,128)}, f32[32,256]{1,0:T(8,128)S(1)}, u32[]{:S(2)}, u32[]{:S(2)}) collective-permute-start(f32[32,256]{1,0:T(8,128)} %start_ref.1), channel_id=1, source_target_pairs={{0,2},{1,3},{2,0},{3,1},{4,6},{5,7},{6,4},{7,5},{8,10},{9,11},{10,... | collective-permute-start | bytes 98312 | tf_op jit(solution)/shard_map/ppermute | solution.py:169
  4.9 5.8 %collective-permute-start.2 = (f32[32,256]{1,0:T(8,128)}, f32[32,256]{1,0:T(8,128)S(1)}, u32[]{:S(2)}, u32[]{:S(2)}) collective-permute-start(f32[32,256]{1,0:T(8,128)} %start_ref.1), channel_id=1, source_target_pairs={{0,3},{1,0},{2,1},{3,2},{4,7},{5,4},{6,5},{7,6},{8,11},{9,8},{10,9... | collective-permute-start | bytes 98312 | tf_op jit(solution)/shard_map/ppermute | solution.py:169
  10.7 11.6 %collective-permute-start.3 = (f32[4,32,256]{2,1,0:T(8,128)S(1)}, f32[4,32,256]{2,1,0:T(8,128)S(1)}, u32[]{:S(2)}, u32[]{:S(2)}) collective-permute-start(f32[4,32,256]{2,1,0:T(8,128)S(1)} %pad_maximum_fusion.q_ref.rest_4_.s_ref), channel_id=1, source_target_pairs={{0,240},{4,244},{8,248},{12,252},{16,0},{20,4},{24,8},{28,12},{32,... | collective-permute-start | bytes 393224 | tf_op jit(solution)/shard_map/ppermute | solution.py:169
  18.7 9.8 %collective-permute-start.5 = (f32[4,32,256]{2,1,0:T(8,128)S(1)}, f32[4,32,256]{2,1,0:T(8,128)S(1)}, u32[]{:S(2)}, u32[]{:S(2)}) collective-permute-start(f32[4,32,256]{2,1,0:T(8,128)S(1)} %pad_maximum_fusion.q_ref.rest_4_.s_ref), channel_id=1, source_target_pairs={{0,192},{4,196},{8,200},{12,204},{16,208},{20,212},{24,216},{28,22... | collective-permute-start | bytes 393224 | tf_op jit(solution)/shard_map/ppermute | solution.py:169
  20.9 11.4 %collective-permute-start.7 = (f32[4,32,256]{2,1,0:T(8,128)S(1)}, f32[4,32,256]{2,1,0:T(8,128)S(1)}, u32[]{:S(2)}, u32[]{:S(2)}) collective-permute-start(f32[4,32,256]{2,1,0:T(8,128)S(1)} %get-tuple-element.20), channel_id=1, source_target_pairs={{0,16},{4,20},{8,24},{12,28},{16,32},{20,36},{24,40},{28,44},{32,4... | collective-permute-start | bytes 393224 | tf_op jit(solution)/shard_map/ppermute | solution.py:169
  21.0 11.5 %collective-permute-start.9 = (f32[4,32,256]{2,1,0:T(8,128)S(1)}, f32[4,32,256]{2,1,0:T(8,128)S(1)}, u32[]{:S(2)}, u32[]{:S(2)}) collective-permute-start(f32[4,32,256]{2,1,0:T(8,128)S(1)} %get-tuple-element.22), channel_id=1, source_target_pairs={{0,64},{4,68},{8,72},{12,76},{16,80},{20,84},{24,88},{28,92},{32,9... | collective-permute-start | bytes 393224 | tf_op jit(solution)/shard_map/ppermute | solution.py:169
  22.3 10.2 %collective-permute-start.4 = (f32[4,32,256]{2,1,0:T(8,128)S(1)}, f32[4,32,256]{2,1,0:T(8,128)S(1)}, u32[]{:S(2)}, u32[]{:S(2)}) collective-permute-start(f32[4,32,256]{2,1,0:T(8,128)S(1)} %collective-permute-done.3.rest_0_), channel_id=1, source_target_pairs={{0,240},{4,244},{8,248},{12,252},{16,0},{20,4},{24,8},{28,12},{32,... | collective-permute-start | bytes 393224 | tf_op jit(solution)/shard_map/ppermute | solution.py:169
  28.5 5.0 %collective-permute-start.6 = (f32[4,32,256]{2,1,0:T(8,128)S(1)}, f32[4,32,256]{2,1,0:T(8,128)S(1)}, u32[]{:S(2)}, u32[]{:S(2)}) collective-permute-start(f32[4,32,256]{2,1,0:T(8,128)S(1)} %collective-permute-done.5.rest_2_), channel_id=1, source_target_pairs={{0,192},{4,196},{8,200},{12,204},{16,208},{20,212},{24,216},{28,22... | collective-permute-start | bytes 393224 | tf_op jit(solution)/shard_map/ppermute | solution.py:169
  32.4 9.8 %collective-permute-start.8 = (f32[4,32,256]{2,1,0:T(8,128)S(1)}, f32[4,32,256]{2,1,0:T(8,128)S(1)}, u32[]{:S(2)}, u32[]{:S(2)}) collective-permute-start(f32[4,32,256]{2,1,0:T(8,128)S(1)} %add.98), channel_id=1, source_target_pairs={{0,16},{4,20},{8,24},{12,28},{16,32},{20,36},{24,40},{28,44},{32,4... | collective-permute-start | bytes 393224 | tf_op jit(solution)/shard_map/ppermute | solution.py:169
  32.5 9.7 %collective-permute-start.10 = (f32[4,32,256]{2,1,0:T(8,128)S(1)}, f32[4,32,256]{2,1,0:T(8,128)S(1)}, u32[]{:S(2)}, u32[]{:S(2)}) collective-permute-start(f32[4,32,256]{2,1,0:T(8,128)S(1)} %add.100), channel_id=1, source_target_pairs={{0,64},{4,68},{8,72},{12,76},{16,80},{20,84},{24,88},{28,92},{32,9... | collective-permute-start | bytes 393224 | tf_op jit(solution)/shard_map/ppermute | solution.py:169
  42.2 6.7 %collective-permute-start.11 = (f32[4,32,256]{2,1,0:T(8,128)S(1)}, f32[4,32,256]{2,1,0:T(8,128)S(1)}, u32[]{:S(2)}, u32[]{:S(2)}) collective-permute-start(f32[4,32,256]{2,1,0:T(8,128)S(1)} %add_add_fusion.1.own), channel_id=1, source_target_pairs={{0,2},{1,3},{2,0},{3,1},{4,6},{5,7},{6,4},{7,5},{8,10},{9,11},{10,... | collective-permute-start | bytes 393224 | tf_op jit(solution)/shard_map/ppermute | solution.py:169
  42.8 7.4 %collective-permute-start.12 = (f32[4,32,256]{2,1,0:T(8,128)S(1)}, f32[4,32,256]{2,1,0:T(8,128)S(1)}, u32[]{:S(2)}, u32[]{:S(2)}) collective-permute-start(f32[4,32,256]{2,1,0:T(8,128)S(1)} %add_add_fusion.1.own), channel_id=1, source_target_pairs={{0,1},{1,2},{2,3},{3,0},{4,5},{5,6},{6,7},{7,4},{8,9},{9,10},{10,1... | collective-permute-start | bytes 393224 | tf_op jit(solution)/shard_map/ppermute | solution.py:169
  43.8 6.4 %collective-permute-start.13 = (f32[4,32,256]{2,1,0:T(8,128)S(1)}, f32[4,32,256]{2,1,0:T(8,128)S(1)}, u32[]{:S(2)}, u32[]{:S(2)}) collective-permute-start(f32[4,32,256]{2,1,0:T(8,128)S(1)} %add_add_fusion.1.own), channel_id=1, source_target_pairs={{0,3},{1,0},{2,1},{3,2},{4,7},{5,4},{6,5},{7,6},{8,11},{9,8},{10,9... | collective-permute-start | bytes 393224 | tf_op jit(solution)/shard_map/ppermute | solution.py:169
  50.2 7.9 %collective-permute-start.14 = (f32[4,32,256]{2,1,0:T(8,128)S(1)}, f32[4,32,256]{2,1,0:T(8,128)S(1)}, u32[]{:S(2)}, u32[]{:S(2)}) collective-permute-start(f32[4,32,256]{2,1,0:T(8,128)S(1)} %shard_map.88.q_ref.rest_4_.y_ref), channel_id=1, source_target_pairs={{0,240},{4,244},{8,248},{12,252},{16,0},{20,4},{24,8},{28,12},{32,... | collective-permute-start | bytes 393224 | tf_op jit(solution)/shard_map/ppermute | solution.py:169
  52.0 12.8 %collective-permute-start.16 = (f32[4,32,256]{2,1,0:T(8,128)S(1)}, f32[4,32,256]{2,1,0:T(8,128)S(1)}, u32[]{:S(2)}, u32[]{:S(2)}) collective-permute-start(f32[4,32,256]{2,1,0:T(8,128)S(1)} %shard_map.88.q_ref.rest_4_.y_ref), channel_id=1, source_target_pairs={{0,192},{4,196},{8,200},{12,204},{16,208},{20,212},{24,216},{28,22... | collective-permute-start | bytes 393224 | tf_op jit(solution)/shard_map/ppermute | solution.py:169
  53.6 13.2 %collective-permute-start.18 = (f32[4,32,256]{2,1,0:T(8,128)S(1)}, f32[4,32,256]{2,1,0:T(8,128)S(1)}, u32[]{:S(2)}, u32[]{:S(2)}) collective-permute-start(f32[4,32,256]{2,1,0:T(8,128)S(1)} %get-tuple-element.25), channel_id=1, source_target_pairs={{0,16},{4,20},{8,24},{12,28},{16,32},{20,36},{24,40},{28,44},{32,4... | collective-permute-start | bytes 393224 | tf_op jit(solution)/shard_map/ppermute | solution.py:169
  55.0 11.9 %collective-permute-start.20 = (f32[4,32,256]{2,1,0:T(8,128)S(1)}, f32[4,32,256]{2,1,0:T(8,128)S(1)}, u32[]{:S(2)}, u32[]{:S(2)}) collective-permute-start(f32[4,32,256]{2,1,0:T(8,128)S(1)} %get-tuple-element.27), channel_id=1, source_target_pairs={{0,64},{4,68},{8,72},{12,76},{16,80},{20,84},{24,88},{28,92},{32,9... | collective-permute-start | bytes 393224 | tf_op jit(solution)/shard_map/ppermute | solution.py:169
  58.2 9.2 %collective-permute-start.15 = (f32[4,32,256]{2,1,0:T(8,128)S(1)}, f32[4,32,256]{2,1,0:T(8,128)S(1)}, u32[]{:S(2)}, u32[]{:S(2)}) collective-permute-start(f32[4,32,256]{2,1,0:T(8,128)S(1)} %collective-permute-done.14.rest_0_), channel_id=1, source_target_pairs={{0,240},{4,244},{8,248},{12,252},{16,0},{20,4},{24,8},{28,12},{32,... | collective-permute-start | bytes 393224 | tf_op jit(solution)/shard_map/ppermute | solution.py:169
  64.9 5.0 %collective-permute-start.17 = (f32[4,32,256]{2,1,0:T(8,128)S(1)}, f32[4,32,256]{2,1,0:T(8,128)S(1)}, u32[]{:S(2)}, u32[]{:S(2)}) collective-permute-start(f32[4,32,256]{2,1,0:T(8,128)S(1)} %collective-permute-done.16.rest_2_), channel_id=1, source_target_pairs={{0,192},{4,196},{8,200},{12,204},{16,208},{20,212},{24,216},{28,22... | collective-permute-start | bytes 393224 | tf_op jit(solution)/shard_map/ppermute | solution.py:169
  66.8 9.6 %collective-permute-start.19 = (f32[4,32,256]{2,1,0:T(8,128)S(1)}, f32[4,32,256]{2,1,0:T(8,128)S(1)}, u32[]{:S(2)}, u32[]{:S(2)}) collective-permute-start(f32[4,32,256]{2,1,0:T(8,128)S(1)} %add.102), channel_id=1, source_target_pairs={{0,16},{4,20},{8,24},{12,28},{16,32},{20,36},{24,40},{28,44},{32,4... | collective-permute-start | bytes 393224 | tf_op jit(solution)/shard_map/ppermute | solution.py:169
  66.9 9.5 %collective-permute-start.21 = (f32[4,32,256]{2,1,0:T(8,128)S(1)}, f32[4,32,256]{2,1,0:T(8,128)S(1)}, u32[]{:S(2)}, u32[]{:S(2)}) collective-permute-start(f32[4,32,256]{2,1,0:T(8,128)S(1)} %add.104), channel_id=1, source_target_pairs={{0,64},{4,68},{8,72},{12,76},{16,80},{20,84},{24,88},{28,92},{32,9... | collective-permute-start | bytes 393224 | tf_op jit(solution)/shard_map/ppermute | solution.py:169
  76.5 6.6 %collective-permute-start.22 = (f32[4,32,256]{2,1,0:T(8,128)S(1)}, f32[4,32,256]{2,1,0:T(8,128)S(1)}, u32[]{:S(2)}, u32[]{:S(2)}) collective-permute-start(f32[4,32,256]{2,1,0:T(8,128)S(1)} %add_add_fusion.own), channel_id=1, source_target_pairs={{0,2},{1,3},{2,0},{3,1},{4,6},{5,7},{6,4},{7,5},{8,10},{9,11},{10,... | collective-permute-start | bytes 393224 | tf_op jit(solution)/shard_map/ppermute | solution.py:169
  78.0 6.4 %collective-permute-start.23 = (f32[4,32,256]{2,1,0:T(8,128)S(1)}, f32[4,32,256]{2,1,0:T(8,128)S(1)}, u32[]{:S(2)}, u32[]{:S(2)}) collective-permute-start(f32[4,32,256]{2,1,0:T(8,128)S(1)} %add_add_fusion.own), channel_id=1, source_target_pairs={{0,1},{1,2},{2,3},{3,0},{4,5},{5,6},{6,7},{7,4},{8,9},{9,10},{10,1... | collective-permute-start | bytes 393224 | tf_op jit(solution)/shard_map/ppermute | solution.py:169
  79.7 5.0 %collective-permute-start.24 = (f32[4,32,256]{2,1,0:T(8,128)S(1)}, f32[4,32,256]{2,1,0:T(8,128)S(1)}, u32[]{:S(2)}, u32[]{:S(2)}) collective-permute-start(f32[4,32,256]{2,1,0:T(8,128)S(1)} %add_add_fusion.own), channel_id=1, source_target_pairs={{0,3},{1,0},{2,1},{3,2},{4,7},{5,4},{6,5},{7,6},{8,11},{9,8},{10,9... | collective-permute-start | bytes 393224 | tf_op jit(solution)/shard_map/ppermute | solution.py:169
  86.5 5.4 %collective-permute-start.26 = (f32[48,128]{1,0:T(8,128)S(1)}, f32[48,128]{1,0:T(8,128)S(1)}, u32[]{:S(2)}, u32[]{:S(2)}) collective-permute-start(f32[48,128]{1,0:T(8,128)S(1)} %add.106), channel_id=1, source_target_pairs={{0,128},{4,132},{8,136},{12,140},{16,144},{20,148},{24,152},{28,15... | collective-permute-start | bytes 73736 | tf_op jit(solution)/shard_map/ppermute | solution.py:169
  86.5 5.4 %collective-permute-start.27 = (f32[48,128]{1,0:T(8,128)S(1)}, f32[48,128]{1,0:T(8,128)S(1)}, u32[]{:S(2)}, u32[]{:S(2)}) collective-permute-start(f32[48,128]{1,0:T(8,128)S(1)} %add.106), channel_id=1, source_target_pairs={{0,64},{4,68},{8,72},{12,76},{16,80},{20,84},{24,88},{28,92},{32,9... | collective-permute-start | bytes 73736 | tf_op jit(solution)/shard_map/ppermute | solution.py:169
  86.6 5.3 %collective-permute-start.28 = (f32[48,128]{1,0:T(8,128)S(1)}, f32[48,128]{1,0:T(8,128)S(1)}, u32[]{:S(2)}, u32[]{:S(2)}) collective-permute-start(f32[48,128]{1,0:T(8,128)S(1)} %add.106), channel_id=1, source_target_pairs={{0,192},{4,196},{8,200},{12,204},{16,208},{20,212},{24,216},{28,22... | collective-permute-start | bytes 73736 | tf_op jit(solution)/shard_map/ppermute | solution.py:169
  91.9 8.0 %collective-permute-start.30 = (f32[48,128]{1,0:T(8,128)S(1)}, f32[48,128]{1,0:T(8,128)S(1)}, u32[]{:S(2)}, u32[]{:S(2)}) collective-permute-start(f32[48,128]{1,0:T(8,128)S(1)} %add_add_fusion.3), channel_id=1, source_target_pairs={{0,48},{4,20},{8,56},{12,28},{16,0},{20,36},{24,8},{28,44},{32,16}... | collective-permute-start | bytes 73736 | tf_op jit(solution)/shard_map/ppermute | solution.py:169
  93.4 7.1 %collective-permute-start.33 = (f32[48,128]{1,0:T(8,128)S(1)}, f32[48,128]{1,0:T(8,128)S(1)}, u32[]{:S(2)}, u32[]{:S(2)}) collective-permute-start(f32[48,128]{1,0:T(8,128)S(1)} %add_add_fusion.3), channel_id=1, source_target_pairs={{0,40},{4,28},{8,48},{12,36},{16,56},{20,44},{24,0},{28,52},{32,8}... | collective-permute-start | bytes 73736 | tf_op jit(solution)/shard_map/ppermute | solution.py:169
  93.4 7.1 %collective-permute-start.32 = (f32[48,128]{1,0:T(8,128)S(1)}, f32[48,128]{1,0:T(8,128)S(1)}, u32[]{:S(2)}, u32[]{:S(2)}) collective-permute-start(f32[48,128]{1,0:T(8,128)S(1)} %add_add_fusion.3), channel_id=1, source_target_pairs={{0,56},{4,12},{8,0},{12,20},{16,8},{20,28},{24,16},{28,36},{32,24}... | collective-permute-start | bytes 73736 | tf_op jit(solution)/shard_map/ppermute | solution.py:169
  93.4 8.6 %collective-permute-start.29 = (f32[48,128]{1,0:T(8,128)S(1)}, f32[48,128]{1,0:T(8,128)S(1)}, u32[]{:S(2)}, u32[]{:S(2)}) collective-permute-start(f32[48,128]{1,0:T(8,128)S(1)} %add_add_fusion.3), channel_id=1, source_target_pairs={{0,32},{4,36},{8,40},{12,44},{16,48},{20,52},{24,56},{28,60},{32,0... | collective-permute-start | bytes 73736 | tf_op jit(solution)/shard_map/ppermute | solution.py:169
  (7 other events, 40.5 us)

commit v7 on v6

--- a/solution.py
+++ b/solution.py
@@ -198,18 +198,22 @@
     def scratch(sources, targets):
         return [pltpu.VMEM((sources, 2 * k, edge), BF16), pltpu.VMEM((targets + 1, k, edge), F32)]
 
+    own = pl.pallas_call(
+        ready_kernel,
+        out_shape=jax.ShapeDtypeStruct(start_block.shape, F32),
+        in_specs=[vmem, vmem],
+        out_specs=vmem,
+        compiler_params=params,
+    )(tiles, start_block)
+    start = jnp.stack([own] + [shifted(start_block, "rep", by) for by in range(1, members)], 0)
+    tile_row, tile_col, tile_round, tile_count, _ = lax.optimization_barrier(
+        (tile_row, tile_col, tile_round, tile_count, start)
+    )
     member = lax.axis_index("rep")
     column = lax.rem(member - tile_col[0, 0] + blocks, blocks)
     row = lax.rem(member - tile_row[0, 0] + blocks, blocks)
     live = (jnp.arange(slots, dtype=jnp.int32) < tile_count[0]).astype(jnp.int32)
     meta = jnp.stack([(tile_round[0, 0] * blocks + column) * live, row * live, live], 0)
-    own = pl.pallas_call(
-        ready_kernel,
-        out_shape=jax.ShapeDtypeStruct(start_block.shape, F32),
-        in_specs=[vmem, vmem],
-        out_specs=vmem,
-        compiler_params=params,
-    )(tiles, start_block)
     backward = pl.pallas_call(
         backward_kernel,
         out_shape=[block_shape] * (ROUNDS + 1),
@@ -255,7 +259,6 @@
         part = forward(meta, tiles, kept, got4, got8, got16, got32, q)
         return part + v + x
 
-    start = jnp.stack([own] + [shifted(start_block, "rep", by) for by in range(1, members)], 0)
     first = rep_sum(apply(start))
     second, gram = pl.pallas_call(
         gram_kernel,

time: 107 us -> 109 us (1.019)
  local copies, waits for them, and re-layouts: 2.95 us -> 5.14 us
    unnamed x6 -> x14, local copies, waits for them, and re-layouts: 2.95 us -> 5.14 us
  transfers between devices with their start and end apart: 36 -> 36, of which waited for: 17 -> 15; matrix products, arithmetic and copies ran while one was open for 1% -> 0% of each run, Pallas kernels for 7% -> 7%
where the time goes in v7:
time: 109 us; the launch traced here: 108 us
  starting transfers between devices  55 us (50%)
  waiting for transfers between devices  34.1 us (31%)
  Pallas kernels  11.8 us (11%)
  local copies, waits for them, and re-layouts  5.14 us (5%)
  between operations  1.58 us (1%)
    ppermute x36, starting transfers between devices, moved(): return lax.ppermute(x, axis, [(i, target(i) % size) for i in range(size)])  55 us
    ppermute x36, waiting for transfers between devices, moved(): return lax.ppermute(x, axis, [(i, target(i) % size) for i in range(size)])  34.1 us
    unnamed x14, local copies, waits for them, and re-layouts  5.14 us
    pallas_call x1, Pallas kernels, body(): pl.pallas_call(tail_kernel, out_shape=[jax.ShapeDtypeStruct((k, edge), F3...  4.2 us
    pallas_call x2, Pallas kernels, apply(): part = forward(meta, tiles, kept, got4, got8, got16, got32, q)  4.02 us
    pallas_call x2, Pallas kernels, apply(): kept, out32, out16, out8, out4 = backward(meta, tiles, q)  2.99 us
  transfers between devices with their start and end apart: 36, of which 15 were waited for; matrix products, arithmetic and copies ran while one was open for 0% of the time, Pallas kernels for 7%

profile of v7, /device:TPU:32, one launch (start us, length us, event | category | flops | bytes accessed | tf_op | source)
XLA Modules:
  0.0 107.8 jit_solution(5804716092831463762)
XLA Ops:
  0.7 1.6 %collective-permute-start = (f32[32,256]{1,0:T(8,128)}, f32[32,256]{1,0:T(8,128)S(1)}, u32[]{:S(2)}, u32[]{:S(2)}) collective-permute-start(f32[32,256]{1,0:T(8,128)} %start_ref.1), channel_id=1, source_target_pairs={{0,1},{1,2},{2,3},{3,0},{4,5},{5,6},{6,7},{7,4},{8,9},{9,10},{10,1... | collective-permute-start | bytes 98312 | tf_op jit(solution)/shard_map/ppermute | solution.py:169
  2.2 2.7 %collective-permute-start.1 = (f32[32,256]{1,0:T(8,128)}, f32[32,256]{1,0:T(8,128)S(1)}, u32[]{:S(2)}, u32[]{:S(2)}) collective-permute-start(f32[32,256]{1,0:T(8,128)} %start_ref.1), channel_id=1, source_target_pairs={{0,2},{1,3},{2,0},{3,1},{4,6},{5,7},{6,4},{7,5},{8,10},{9,11},{10,... | collective-permute-start | bytes 98312 | tf_op jit(solution)/shard_map/ppermute | solution.py:169
  5.0 1.4 %collective-permute-start.2 = (f32[32,256]{1,0:T(8,128)}, f32[32,256]{1,0:T(8,128)S(1)}, u32[]{:S(2)}, u32[]{:S(2)}) collective-permute-start(f32[32,256]{1,0:T(8,128)} %start_ref.1), channel_id=1, source_target_pairs={{0,3},{1,0},{2,1},{3,2},{4,7},{5,4},{6,5},{7,6},{8,11},{9,8},{10,9... | collective-permute-start | bytes 98312 | tf_op jit(solution)/shard_map/ppermute | solution.py:169
  7.1 2.2 %copy-done = bf16[1,1,32,256,256]{4,3,2,1,0:T(8,128)(2,1)S(1)} copy-done((bf16[1,1,32,256,256]{4,3,2,1,0:T(8,128)(2,1)S(1)}, bf16[1,1,32,256,256]{4,3,2,1,0:T(8,128)(2,1)}, u32[]{:S(2)}) %copy-start) | copy-done | bytes 4194328
  10.1 7.9 %collective-permute-start.3 = (f32[4,32,256]{2,1,0:T(8,128)S(1)}, f32[4,32,256]{2,1,0:T(8,128)S(1)}, u32[]{:S(2)}, u32[]{:S(2)}) collective-permute-start(f32[4,32,256]{2,1,0:T(8,128)S(1)} %pad_maximum_fusion.q_ref.rest_4_.s_ref), channel_id=1, source_target_pairs={{0,240},{4,244},{8,248},{12,252},{16,0},{20,4},{24,8},{28,12},{32,... | collective-permute-start | bytes 393224 | tf_op jit(solution)/shard_map/ppermute | solution.py:169
  18.8 2.2 %copy-done.1 = bf16[1,1,32,256,256]{4,3,2,1,0:T(8,128)(2,1)S(1)} copy-done((bf16[1,1,32,256,256]{4,3,2,1,0:T(8,128)(2,1)S(1)}, bf16[1,1,32,256,256]{4,3,2,1,0:T(8,128)(2,1)}, u32[]{:S(2)}) %copy-start.1) | copy-done | bytes 4194328
  21.0 1.5 %shard_map.86 = (f32[4,32,256]{2,1,0:T(8,128)S(1)}, f32[4,32,256]{2,1,0:T(8,128)S(1)}, f32[4,32,256]{2,1,0:T(8,128)S(1)}, f32[4,32,256]{2,1,0:T(8,128)S(1)}, f32[4,32,256]{2,1,0:T(8,128)S(1)}) custom-call(s32[3,32]{1,0:T(4,128)S(1)} %pad_add_fusion.meta, bf16[32,256,256]{2,1,0:T(8,128)(2,1)S(1)} %bitcast.16, ...), custom_call_target="tpu_custom_call" | custom-call | flops 268435456 | bytes 4194304 | tf_op jit(solution)/shard_map/pallas_call | solution.py:250
  22.5 1.4 %collective-permute-start.9 = (f32[4,32,256]{2,1,0:T(8,128)S(1)}, f32[4,32,256]{2,1,0:T(8,128)S(1)}, u32[]{:S(2)}, u32[]{:S(2)}) collective-permute-start(f32[4,32,256]{2,1,0:T(8,128)S(1)} %get-tuple-element.30), channel_id=1, source_target_pairs={{0,64},{4,68},{8,72},{12,76},{16,80},{20,84},{24,88},{28,92},{32,9... | collective-permute-start | bytes 393224 | tf_op jit(solution)/shard_map/ppermute | solution.py:169
  23.9 6.2 %collective-permute-start.4 = (f32[4,32,256]{2,1,0:T(8,128)S(1)}, f32[4,32,256]{2,1,0:T(8,128)S(1)}, u32[]{:S(2)}, u32[]{:S(2)}) collective-permute-start(f32[4,32,256]{2,1,0:T(8,128)S(1)} %collective-permute-done.3.rest_0_), channel_id=1, source_target_pairs={{0,240},{4,244},{8,248},{12,252},{16,0},{20,4},{24,8},{28,12},{32,... | collective-permute-start | bytes 393224 | tf_op jit(solution)/shard_map/ppermute | solution.py:169
  30.8 3.1 %collective-permute-done.7 = f32[4,32,256]{2,1,0:T(8,128)S(1)} collective-permute-done((f32[4,32,256]{2,1,0:T(8,128)S(1)}, f32[4,32,256]{2,1,0:T(8,128)S(1)}, u32[]{:S(2)}, u32[]{:S(2)}) %collective-permute-start.7) | collective-permute-done | bytes 131104 | tf_op jit(solution)/shard_map/ppermute | solution.py:169
  35.0 2.0 %shard_map.87 = f32[4,32,256]{2,1,0:T(8,128)S(1)} custom-call(s32[3,32]{1,0:T(4,128)S(1)} %pad_add_fusion.meta, bf16[32,256,256]{2,1,0:T(8,128)(2,1)S(1)} %bitcast.17, f32[4,32,256]{2,1,0:T(8,128)S(1)} %get-tuple-element.26.kept_ref, f32[4,32,256]{2,1,0:T(8,128)S(1)} %collective-permute-done.3.rest_0_, f32[4,32,256]{2,1,0:T(8,128)S(1)} %collective-permute-done.4.rest_1_, ...), custom_call_target="tpu_custom_call" | custom-call | flops 268435456 | bytes 4194304 | tf_op jit(solution)/shard_map/pallas_call | solution.py:259
  37.0 6.4 %collective-permute-done.8 = f32[4,32,256]{2,1,0:T(8,128)S(1)} collective-permute-done((f32[4,32,256]{2,1,0:T(8,128)S(1)}, f32[4,32,256]{2,1,0:T(8,128)S(1)}, u32[]{:S(2)}, u32[]{:S(2)}) %collective-permute-start.8) | collective-permute-done | bytes 131104 | tf_op jit(solution)/shard_map/ppermute | solution.py:169
  44.1 1.5 %collective-permute-start.12 = (f32[4,32,256]{2,1,0:T(8,128)S(1)}, f32[4,32,256]{2,1,0:T(8,128)S(1)}, u32[]{:S(2)}, u32[]{:S(2)}) collective-permute-start(f32[4,32,256]{2,1,0:T(8,128)S(1)} %add_add_fusion.1.own), channel_id=1, source_target_pairs={{0,1},{1,2},{2,3},{3,0},{4,5},{5,6},{6,7},{7,4},{8,9},{9,10},{10,1... | collective-permute-start | bytes 393224 | tf_op jit(solution)/shard_map/ppermute | solution.py:169
  45.6 1.8 %collective-permute-start.13 = (f32[4,32,256]{2,1,0:T(8,128)S(1)}, f32[4,32,256]{2,1,0:T(8,128)S(1)}, u32[]{:S(2)}, u32[]{:S(2)}) collective-permute-start(f32[4,32,256]{2,1,0:T(8,128)S(1)} %add_add_fusion.1.own), channel_id=1, source_target_pairs={{0,3},{1,0},{2,1},{3,2},{4,7},{5,4},{6,5},{7,6},{8,11},{9,8},{10,9... | collective-permute-start | bytes 393224 | tf_op jit(solution)/shard_map/ppermute | solution.py:169
  47.4 2.8 %collective-permute-done.11.second = f32[4,32,256]{2,1,0:T(8,128)S(1)} collective-permute-done((f32[4,32,256]{2,1,0:T(8,128)S(1)}, f32[4,32,256]{2,1,0:T(8,128)S(1)}, u32[]{:S(2)}, u32[]{:S(2)}) %collective-permute-start.11) | collective-permute-done | bytes 131104 | tf_op jit(solution)/shard_map/ppermute | solution.py:169
  51.5 2.0 %collective-permute-start.14 = (f32[4,32,256]{2,1,0:T(8,128)S(1)}, f32[4,32,256]{2,1,0:T(8,128)S(1)}, u32[]{:S(2)}, u32[]{:S(2)}) collective-permute-start(f32[4,32,256]{2,1,0:T(8,128)S(1)} %shard_map.88.q_ref.rest_4_.y_ref), channel_id=1, source_target_pairs={{0,240},{4,244},{8,248},{12,252},{16,0},{20,4},{24,8},{28,12},{32,... | collective-permute-start | bytes 393224 | tf_op jit(solution)/shard_map/ppermute | solution.py:169
  53.6 1.5 %shard_map.89 = (f32[4,32,256]{2,1,0:T(8,128)S(1)}, f32[4,32,256]{2,1,0:T(8,128)S(1)}, f32[4,32,256]{2,1,0:T(8,128)S(1)}, f32[4,32,256]{2,1,0:T(8,128)S(1)}, f32[4,32,256]{2,1,0:T(8,128)S(1)}) custom-call(s32[3,32]{1,0:T(4,128)S(1)} %pad_add_fusion.meta, bf16[32,256,256]{2,1,0:T(8,128)(2,1)S(1)} %bitcast.18, f32[4,32,256]{2,1,0:T(8,128)S(1)} %shard_map.88.q_ref.rest_4_.y_ref), custom_call_target="tpu_custom_call" | custom-call | flops 268435456 | bytes 4194304 | tf_op jit(solution)/shard_map/pallas_call | solution.py:250
  56.3 2.0 %collective-permute-start.20 = (f32[4,32,256]{2,1,0:T(8,128)S(1)}, f32[4,32,256]{2,1,0:T(8,128)S(1)}, u32[]{:S(2)}, u32[]{:S(2)}) collective-permute-start(f32[4,32,256]{2,1,0:T(8,128)S(1)} %get-tuple-element.35), channel_id=1, source_target_pairs={{0,64},{4,68},{8,72},{12,76},{16,80},{20,84},{24,88},{28,92},{32,9... | collective-permute-start | bytes 393224 | tf_op jit(solution)/shard_map/ppermute | solution.py:169
  58.5 6.7 %collective-permute-start.15 = (f32[4,32,256]{2,1,0:T(8,128)S(1)}, f32[4,32,256]{2,1,0:T(8,128)S(1)}, u32[]{:S(2)}, u32[]{:S(2)}) collective-permute-start(f32[4,32,256]{2,1,0:T(8,128)S(1)} %collective-permute-done.14.rest_0_), channel_id=1, source_target_pairs={{0,240},{4,244},{8,248},{12,252},{16,0},{20,4},{24,8},{28,12},{32,... | collective-permute-start | bytes 393224 | tf_op jit(solution)/shard_map/ppermute | solution.py:169
  65.3 3.2 %collective-permute-done.18 = f32[4,32,256]{2,1,0:T(8,128)S(1)} collective-permute-done((f32[4,32,256]{2,1,0:T(8,128)S(1)}, f32[4,32,256]{2,1,0:T(8,128)S(1)}, u32[]{:S(2)}, u32[]{:S(2)}) %collective-permute-start.18) | collective-permute-done | bytes 131104 | tf_op jit(solution)/shard_map/ppermute | solution.py:169
  68.7 1.5 %collective-permute-done.17.rest_3_ = f32[4,32,256]{2,1,0:T(8,128)S(1)} collective-permute-done((f32[4,32,256]{2,1,0:T(8,128)S(1)}, f32[4,32,256]{2,1,0:T(8,128)S(1)}, u32[]{:S(2)}, u32[]{:S(2)}) %collective-permute-start.17) | collective-permute-done | bytes 131104 | tf_op jit(solution)/shard_map/ppermute | solution.py:169
  70.2 2.0 %shard_map.90 = f32[4,32,256]{2,1,0:T(8,128)S(1)} custom-call(s32[3,32]{1,0:T(4,128)S(1)} %pad_add_fusion.meta, bf16[32,256,256]{2,1,0:T(8,128)(2,1)S(1)} %bitcast.19, f32[4,32,256]{2,1,0:T(8,128)S(1)} %get-tuple-element.31.kept_ref, f32[4,32,256]{2,1,0:T(8,128)S(1)} %collective-permute-done.14.rest_0_, f32[4,32,256]{2,1,0:T(8,128)S(1)} %collective-permute-done.15.rest_1_, ...), custom_call_target="tpu_custom_call" | custom-call | flops 268435456 | bytes 4194304 | tf_op jit(solution)/shard_map/pallas_call | solution.py:259
  72.2 5.8 %collective-permute-done.19 = f32[4,32,256]{2,1,0:T(8,128)S(1)} collective-permute-done((f32[4,32,256]{2,1,0:T(8,128)S(1)}, f32[4,32,256]{2,1,0:T(8,128)S(1)}, u32[]{:S(2)}, u32[]{:S(2)}) %collective-permute-start.19) | collective-permute-done | bytes 131104 | tf_op jit(solution)/shard_map/ppermute | solution.py:169
  78.8 1.7 %collective-permute-start.23 = (f32[4,32,256]{2,1,0:T(8,128)S(1)}, f32[4,32,256]{2,1,0:T(8,128)S(1)}, u32[]{:S(2)}, u32[]{:S(2)}) collective-permute-start(f32[4,32,256]{2,1,0:T(8,128)S(1)} %add_add_fusion.own), channel_id=1, source_target_pairs={{0,1},{1,2},{2,3},{3,0},{4,5},{5,6},{6,7},{7,4},{8,9},{9,10},{10,1... | collective-permute-start | bytes 393224 | tf_op jit(solution)/shard_map/ppermute | solution.py:169
  80.5 1.5 %collective-permute-start.24 = (f32[4,32,256]{2,1,0:T(8,128)S(1)}, f32[4,32,256]{2,1,0:T(8,128)S(1)}, u32[]{:S(2)}, u32[]{:S(2)}) collective-permute-start(f32[4,32,256]{2,1,0:T(8,128)S(1)} %add_add_fusion.own), channel_id=1, source_target_pairs={{0,3},{1,0},{2,1},{3,2},{4,7},{5,4},{6,5},{7,6},{8,11},{9,8},{10,9... | collective-permute-start | bytes 393224 | tf_op jit(solution)/shard_map/ppermute | solution.py:169
  82.0 2.7 %collective-permute-done.22.second = f32[4,32,256]{2,1,0:T(8,128)S(1)} collective-permute-done((f32[4,32,256]{2,1,0:T(8,128)S(1)}, f32[4,32,256]{2,1,0:T(8,128)S(1)}, u32[]{:S(2)}, u32[]{:S(2)}) %collective-permute-start.22) | collective-permute-done | bytes 131104 | tf_op jit(solution)/shard_map/ppermute | solution.py:169
  84.7 1.3 %collective-permute-done.23.first = f32[4,32,256]{2,1,0:T(8,128)S(1)} collective-permute-done((f32[4,32,256]{2,1,0:T(8,128)S(1)}, f32[4,32,256]{2,1,0:T(8,128)S(1)}, u32[]{:S(2)}, u32[]{:S(2)}) %collective-permute-start.23) | collective-permute-done | bytes 131104 | tf_op jit(solution)/shard_map/ppermute | solution.py:169
  88.0 3.2 %collective-permute-start.28 = (f32[48,128]{1,0:T(8,128)S(1)}, f32[48,128]{1,0:T(8,128)S(1)}, u32[]{:S(2)}, u32[]{:S(2)}) collective-permute-start(f32[48,128]{1,0:T(8,128)S(1)} %add.106), channel_id=1, source_target_pairs={{0,192},{4,196},{8,200},{12,204},{16,208},{20,212},{24,216},{28,22... | collective-permute-start | bytes 73736 | tf_op jit(solution)/shard_map/ppermute | solution.py:169
  91.2 2.0 %collective-permute-done.26 = f32[48,128]{1,0:T(8,128)S(1)} collective-permute-done((f32[48,128]{1,0:T(8,128)S(1)}, f32[48,128]{1,0:T(8,128)S(1)}, u32[]{:S(2)}, u32[]{:S(2)}) %collective-permute-start.26) | collective-permute-done | bytes 24608 | tf_op jit(solution)/shard_map/ppermute | solution.py:169
  93.3 1.8 %collective-permute-start.30 = (f32[48,128]{1,0:T(8,128)S(1)}, f32[48,128]{1,0:T(8,128)S(1)}, u32[]{:S(2)}, u32[]{:S(2)}) collective-permute-start(f32[48,128]{1,0:T(8,128)S(1)} %add_add_fusion.3), channel_id=1, source_target_pairs={{0,48},{4,20},{8,56},{12,28},{16,0},{20,36},{24,8},{28,44},{32,16}... | collective-permute-start | bytes 73736 | tf_op jit(solution)/shard_map/ppermute | solution.py:169
  95.0 6.5 %collective-permute-start.29 = (f32[48,128]{1,0:T(8,128)S(1)}, f32[48,128]{1,0:T(8,128)S(1)}, u32[]{:S(2)}, u32[]{:S(2)}) collective-permute-start(f32[48,128]{1,0:T(8,128)S(1)} %add_add_fusion.3), channel_id=1, source_target_pairs={{0,32},{4,36},{8,40},{12,44},{16,48},{20,52},{24,56},{28,60},{32,0... | collective-permute-start | bytes 73736 | tf_op jit(solution)/shard_map/ppermute | solution.py:169
  103.6 4.2 %shard_map.92 = (f32[32,256]{1,0:T(8,128)}, f32[2,32,64]{2,1,0:T(8,128)}, f32[2,32,32]{2,1,0:T(8,128)}) custom-call(f32[48,128]{1,0:T(8,128)S(1)} %add_add_fusion.2.gram_ref, f32[4,32,256]{2,1,0:T(8,128)S(1)} %pad_maximum_fusion.q_ref.rest_4_.s_ref, f32[4,32,256]{2,1,0:T(8,128)S(1)} %shard_map.88.q_ref.rest_4_.y_ref, f32[1,32,256]{2,1,0:T(8,128)S(1)} %get-tuple-element.37.z_ref), custom_call_target="tpu_custom_call" | custom-call | tf_op jit(solution)/shard_map/pallas_call | solution.py:281
  (75 shorter events, 11.9 us)
Async XLA Ops:
  0.7 9.4 %collective-permute-start = (f32[32,256]{1,0:T(8,128)}, f32[32,256]{1,0:T(8,128)S(1)}, u32[]{:S(2)}, u32[]{:S(2)}) collective-permute-start(f32[32,256]{1,0:T(8,128)} %start_ref.1), channel_id=1, source_target_pairs={{0,1},{1,2},{2,3},{3,0},{4,5},{5,6},{6,7},{7,4},{8,9},{9,10},{10,1... | collective-permute-start | bytes 98312 | tf_op jit(solution)/shard_map/ppermute | solution.py:169
  2.2 7.8 %collective-permute-start.1 = (f32[32,256]{1,0:T(8,128)}, f32[32,256]{1,0:T(8,128)S(1)}, u32[]{:S(2)}, u32[]{:S(2)}) collective-permute-start(f32[32,256]{1,0:T(8,128)} %start_ref.1), channel_id=1, source_target_pairs={{0,2},{1,3},{2,0},{3,1},{4,6},{5,7},{6,4},{7,5},{8,10},{9,11},{10,... | collective-permute-start | bytes 98312 | tf_op jit(solution)/shard_map/ppermute | solution.py:169
  5.0 5.1 %collective-permute-start.2 = (f32[32,256]{1,0:T(8,128)}, f32[32,256]{1,0:T(8,128)S(1)}, u32[]{:S(2)}, u32[]{:S(2)}) collective-permute-start(f32[32,256]{1,0:T(8,128)} %start_ref.1), channel_id=1, source_target_pairs={{0,3},{1,0},{2,1},{3,2},{4,7},{5,4},{6,5},{7,6},{8,11},{9,8},{10,9... | collective-permute-start | bytes 98312 | tf_op jit(solution)/shard_map/ppermute | solution.py:169
  10.1 13.8 %collective-permute-start.3 = (f32[4,32,256]{2,1,0:T(8,128)S(1)}, f32[4,32,256]{2,1,0:T(8,128)S(1)}, u32[]{:S(2)}, u32[]{:S(2)}) collective-permute-start(f32[4,32,256]{2,1,0:T(8,128)S(1)} %pad_maximum_fusion.q_ref.rest_4_.s_ref), channel_id=1, source_target_pairs={{0,240},{4,244},{8,248},{12,252},{16,0},{20,4},{24,8},{28,12},{32,... | collective-permute-start | bytes 393224 | tf_op jit(solution)/shard_map/ppermute | solution.py:169
  18.0 12.1 %collective-permute-start.5 = (f32[4,32,256]{2,1,0:T(8,128)S(1)}, f32[4,32,256]{2,1,0:T(8,128)S(1)}, u32[]{:S(2)}, u32[]{:S(2)}) collective-permute-start(f32[4,32,256]{2,1,0:T(8,128)S(1)} %pad_maximum_fusion.q_ref.rest_4_.s_ref), channel_id=1, source_target_pairs={{0,192},{4,196},{8,200},{12,204},{16,208},{20,212},{24,216},{28,22... | collective-permute-start | bytes 393224 | tf_op jit(solution)/shard_map/ppermute | solution.py:169
  22.5 11.4 %collective-permute-start.7 = (f32[4,32,256]{2,1,0:T(8,128)S(1)}, f32[4,32,256]{2,1,0:T(8,128)S(1)}, u32[]{:S(2)}, u32[]{:S(2)}) collective-permute-start(f32[4,32,256]{2,1,0:T(8,128)S(1)} %get-tuple-element.28), channel_id=1, source_target_pairs={{0,16},{4,20},{8,24},{12,28},{16,32},{20,36},{24,40},{28,44},{32,4... | collective-permute-start | bytes 393224 | tf_op jit(solution)/shard_map/ppermute | solution.py:169
  22.5 11.4 %collective-permute-start.9 = (f32[4,32,256]{2,1,0:T(8,128)S(1)}, f32[4,32,256]{2,1,0:T(8,128)S(1)}, u32[]{:S(2)}, u32[]{:S(2)}) collective-permute-start(f32[4,32,256]{2,1,0:T(8,128)S(1)} %get-tuple-element.30), channel_id=1, source_target_pairs={{0,64},{4,68},{8,72},{12,76},{16,80},{20,84},{24,88},{28,92},{32,9... | collective-permute-start | bytes 393224 | tf_op jit(solution)/shard_map/ppermute | solution.py:169
  23.9 10.2 %collective-permute-start.4 = (f32[4,32,256]{2,1,0:T(8,128)S(1)}, f32[4,32,256]{2,1,0:T(8,128)S(1)}, u32[]{:S(2)}, u32[]{:S(2)}) collective-permute-start(f32[4,32,256]{2,1,0:T(8,128)S(1)} %collective-permute-done.3.rest_0_), channel_id=1, source_target_pairs={{0,240},{4,244},{8,248},{12,252},{16,0},{20,4},{24,8},{28,12},{32,... | collective-permute-start | bytes 393224 | tf_op jit(solution)/shard_map/ppermute | solution.py:169
  30.1 5.0 %collective-permute-start.6 = (f32[4,32,256]{2,1,0:T(8,128)S(1)}, f32[4,32,256]{2,1,0:T(8,128)S(1)}, u32[]{:S(2)}, u32[]{:S(2)}) collective-permute-start(f32[4,32,256]{2,1,0:T(8,128)S(1)} %collective-permute-done.5.rest_2_), channel_id=1, source_target_pairs={{0,192},{4,196},{8,200},{12,204},{16,208},{20,212},{24,216},{28,22... | collective-permute-start | bytes 393224 | tf_op jit(solution)/shard_map/ppermute | solution.py:169
  33.9 9.6 %collective-permute-start.8 = (f32[4,32,256]{2,1,0:T(8,128)S(1)}, f32[4,32,256]{2,1,0:T(8,128)S(1)}, u32[]{:S(2)}, u32[]{:S(2)}) collective-permute-start(f32[4,32,256]{2,1,0:T(8,128)S(1)} %add.98), channel_id=1, source_target_pairs={{0,16},{4,20},{8,24},{12,28},{16,32},{20,36},{24,40},{28,44},{32,4... | collective-permute-start | bytes 393224 | tf_op jit(solution)/shard_map/ppermute | solution.py:169
  34.0 9.5 %collective-permute-start.10 = (f32[4,32,256]{2,1,0:T(8,128)S(1)}, f32[4,32,256]{2,1,0:T(8,128)S(1)}, u32[]{:S(2)}, u32[]{:S(2)}) collective-permute-start(f32[4,32,256]{2,1,0:T(8,128)S(1)} %add.100), channel_id=1, source_target_pairs={{0,64},{4,68},{8,72},{12,76},{16,80},{20,84},{24,88},{28,92},{32,9... | collective-permute-start | bytes 393224 | tf_op jit(solution)/shard_map/ppermute | solution.py:169
  43.5 6.7 %collective-permute-start.11 = (f32[4,32,256]{2,1,0:T(8,128)S(1)}, f32[4,32,256]{2,1,0:T(8,128)S(1)}, u32[]{:S(2)}, u32[]{:S(2)}) collective-permute-start(f32[4,32,256]{2,1,0:T(8,128)S(1)} %add_add_fusion.1.own), channel_id=1, source_target_pairs={{0,2},{1,3},{2,0},{3,1},{4,6},{5,7},{6,4},{7,5},{8,10},{9,11},{10,... | collective-permute-start | bytes 393224 | tf_op jit(solution)/shard_map/ppermute | solution.py:169
  44.1 7.4 %collective-permute-start.12 = (f32[4,32,256]{2,1,0:T(8,128)S(1)}, f32[4,32,256]{2,1,0:T(8,128)S(1)}, u32[]{:S(2)}, u32[]{:S(2)}) collective-permute-start(f32[4,32,256]{2,1,0:T(8,128)S(1)} %add_add_fusion.1.own), channel_id=1, source_target_pairs={{0,1},{1,2},{2,3},{3,0},{4,5},{5,6},{6,7},{7,4},{8,9},{9,10},{10,1... | collective-permute-start | bytes 393224 | tf_op jit(solution)/shard_map/ppermute | solution.py:169
  45.6 5.9 %collective-permute-start.13 = (f32[4,32,256]{2,1,0:T(8,128)S(1)}, f32[4,32,256]{2,1,0:T(8,128)S(1)}, u32[]{:S(2)}, u32[]{:S(2)}) collective-permute-start(f32[4,32,256]{2,1,0:T(8,128)S(1)} %add_add_fusion.1.own), channel_id=1, source_target_pairs={{0,3},{1,0},{2,1},{3,2},{4,7},{5,4},{6,5},{7,6},{8,11},{9,8},{10,9... | collective-permute-start | bytes 393224 | tf_op jit(solution)/shard_map/ppermute | solution.py:169
  51.5 7.0 %collective-permute-start.14 = (f32[4,32,256]{2,1,0:T(8,128)S(1)}, f32[4,32,256]{2,1,0:T(8,128)S(1)}, u32[]{:S(2)}, u32[]{:S(2)}) collective-permute-start(f32[4,32,256]{2,1,0:T(8,128)S(1)} %shard_map.88.q_ref.rest_4_.y_ref), channel_id=1, source_target_pairs={{0,240},{4,244},{8,248},{12,252},{16,0},{20,4},{24,8},{28,12},{32,... | collective-permute-start | bytes 393224 | tf_op jit(solution)/shard_map/ppermute | solution.py:169
  53.6 11.7 %collective-permute-start.16 = (f32[4,32,256]{2,1,0:T(8,128)S(1)}, f32[4,32,256]{2,1,0:T(8,128)S(1)}, u32[]{:S(2)}, u32[]{:S(2)}) collective-permute-start(f32[4,32,256]{2,1,0:T(8,128)S(1)} %shard_map.88.q_ref.rest_4_.y_ref), channel_id=1, source_target_pairs={{0,192},{4,196},{8,200},{12,204},{16,208},{20,212},{24,216},{28,22... | collective-permute-start | bytes 393224 | tf_op jit(solution)/shard_map/ppermute | solution.py:169
  55.1 13.4 %collective-permute-start.18 = (f32[4,32,256]{2,1,0:T(8,128)S(1)}, f32[4,32,256]{2,1,0:T(8,128)S(1)}, u32[]{:S(2)}, u32[]{:S(2)}) collective-permute-start(f32[4,32,256]{2,1,0:T(8,128)S(1)} %get-tuple-element.33), channel_id=1, source_target_pairs={{0,16},{4,20},{8,24},{12,28},{16,32},{20,36},{24,40},{28,44},{32,4... | collective-permute-start | bytes 393224 | tf_op jit(solution)/shard_map/ppermute | solution.py:169
  56.3 12.3 %collective-permute-start.20 = (f32[4,32,256]{2,1,0:T(8,128)S(1)}, f32[4,32,256]{2,1,0:T(8,128)S(1)}, u32[]{:S(2)}, u32[]{:S(2)}) collective-permute-start(f32[4,32,256]{2,1,0:T(8,128)S(1)} %get-tuple-element.35), channel_id=1, source_target_pairs={{0,64},{4,68},{8,72},{12,76},{16,80},{20,84},{24,88},{28,92},{32,9... | collective-permute-start | bytes 393224 | tf_op jit(solution)/shard_map/ppermute | solution.py:169
  58.5 10.2 %collective-permute-start.15 = (f32[4,32,256]{2,1,0:T(8,128)S(1)}, f32[4,32,256]{2,1,0:T(8,128)S(1)}, u32[]{:S(2)}, u32[]{:S(2)}) collective-permute-start(f32[4,32,256]{2,1,0:T(8,128)S(1)} %collective-permute-done.14.rest_0_), channel_id=1, source_target_pairs={{0,240},{4,244},{8,248},{12,252},{16,0},{20,4},{24,8},{28,12},{32,... | collective-permute-start | bytes 393224 | tf_op jit(solution)/shard_map/ppermute | solution.py:169
  65.3 5.0 %collective-permute-start.17 = (f32[4,32,256]{2,1,0:T(8,128)S(1)}, f32[4,32,256]{2,1,0:T(8,128)S(1)}, u32[]{:S(2)}, u32[]{:S(2)}) collective-permute-start(f32[4,32,256]{2,1,0:T(8,128)S(1)} %collective-permute-done.16.rest_2_), channel_id=1, source_target_pairs={{0,192},{4,196},{8,200},{12,204},{16,208},{20,212},{24,216},{28,22... | collective-permute-start | bytes 393224 | tf_op jit(solution)/shard_map/ppermute | solution.py:169
  68.5 9.5 %collective-permute-start.19 = (f32[4,32,256]{2,1,0:T(8,128)S(1)}, f32[4,32,256]{2,1,0:T(8,128)S(1)}, u32[]{:S(2)}, u32[]{:S(2)}) collective-permute-start(f32[4,32,256]{2,1,0:T(8,128)S(1)} %add.102), channel_id=1, source_target_pairs={{0,16},{4,20},{8,24},{12,28},{16,32},{20,36},{24,40},{28,44},{32,4... | collective-permute-start | bytes 393224 | tf_op jit(solution)/shard_map/ppermute | solution.py:169
  68.6 9.4 %collective-permute-start.21 = (f32[4,32,256]{2,1,0:T(8,128)S(1)}, f32[4,32,256]{2,1,0:T(8,128)S(1)}, u32[]{:S(2)}, u32[]{:S(2)}) collective-permute-start(f32[4,32,256]{2,1,0:T(8,128)S(1)} %add.104), channel_id=1, source_target_pairs={{0,64},{4,68},{8,72},{12,76},{16,80},{20,84},{24,88},{28,92},{32,9... | collective-permute-start | bytes 393224 | tf_op jit(solution)/shard_map/ppermute | solution.py:169
  78.1 6.7 %collective-permute-start.22 = (f32[4,32,256]{2,1,0:T(8,128)S(1)}, f32[4,32,256]{2,1,0:T(8,128)S(1)}, u32[]{:S(2)}, u32[]{:S(2)}) collective-permute-start(f32[4,32,256]{2,1,0:T(8,128)S(1)} %add_add_fusion.own), channel_id=1, source_target_pairs={{0,2},{1,3},{2,0},{3,1},{4,6},{5,7},{6,4},{7,5},{8,10},{9,11},{10,... | collective-permute-start | bytes 393224 | tf_op jit(solution)/shard_map/ppermute | solution.py:169
  78.8 7.3 %collective-permute-start.23 = (f32[4,32,256]{2,1,0:T(8,128)S(1)}, f32[4,32,256]{2,1,0:T(8,128)S(1)}, u32[]{:S(2)}, u32[]{:S(2)}) collective-permute-start(f32[4,32,256]{2,1,0:T(8,128)S(1)} %add_add_fusion.own), channel_id=1, source_target_pairs={{0,1},{1,2},{2,3},{3,0},{4,5},{5,6},{6,7},{7,4},{8,9},{9,10},{10,1... | collective-permute-start | bytes 393224 | tf_op jit(solution)/shard_map/ppermute | solution.py:169
  80.5 5.5 %collective-permute-start.24 = (f32[4,32,256]{2,1,0:T(8,128)S(1)}, f32[4,32,256]{2,1,0:T(8,128)S(1)}, u32[]{:S(2)}, u32[]{:S(2)}) collective-permute-start(f32[4,32,256]{2,1,0:T(8,128)S(1)} %add_add_fusion.own), channel_id=1, source_target_pairs={{0,3},{1,0},{2,1},{3,2},{4,7},{5,4},{6,5},{7,6},{8,11},{9,8},{10,9... | collective-permute-start | bytes 393224 | tf_op jit(solution)/shard_map/ppermute | solution.py:169
  87.9 5.4 %collective-permute-start.26 = (f32[48,128]{1,0:T(8,128)S(1)}, f32[48,128]{1,0:T(8,128)S(1)}, u32[]{:S(2)}, u32[]{:S(2)}) collective-permute-start(f32[48,128]{1,0:T(8,128)S(1)} %add.106), channel_id=1, source_target_pairs={{0,128},{4,132},{8,136},{12,140},{16,144},{20,148},{24,152},{28,15... | collective-permute-start | bytes 73736 | tf_op jit(solution)/shard_map/ppermute | solution.py:169
  87.9 5.4 %collective-permute-start.27 = (f32[48,128]{1,0:T(8,128)S(1)}, f32[48,128]{1,0:T(8,128)S(1)}, u32[]{:S(2)}, u32[]{:S(2)}) collective-permute-start(f32[48,128]{1,0:T(8,128)S(1)} %add.106), channel_id=1, source_target_pairs={{0,64},{4,68},{8,72},{12,76},{16,80},{20,84},{24,88},{28,92},{32,9... | collective-permute-start | bytes 73736 | tf_op jit(solution)/shard_map/ppermute | solution.py:169
  88.0 5.3 %collective-permute-start.28 = (f32[48,128]{1,0:T(8,128)S(1)}, f32[48,128]{1,0:T(8,128)S(1)}, u32[]{:S(2)}, u32[]{:S(2)}) collective-permute-start(f32[48,128]{1,0:T(8,128)S(1)} %add.106), channel_id=1, source_target_pairs={{0,192},{4,196},{8,200},{12,204},{16,208},{20,212},{24,216},{28,22... | collective-permute-start | bytes 73736 | tf_op jit(solution)/shard_map/ppermute | solution.py:169
  93.3 8.3 %collective-permute-start.30 = (f32[48,128]{1,0:T(8,128)S(1)}, f32[48,128]{1,0:T(8,128)S(1)}, u32[]{:S(2)}, u32[]{:S(2)}) collective-permute-start(f32[48,128]{1,0:T(8,128)S(1)} %add_add_fusion.3), channel_id=1, source_target_pairs={{0,48},{4,20},{8,56},{12,28},{16,0},{20,36},{24,8},{28,44},{32,16}... | collective-permute-start | bytes 73736 | tf_op jit(solution)/shard_map/ppermute | solution.py:169
  95.0 7.1 %collective-permute-start.33 = (f32[48,128]{1,0:T(8,128)S(1)}, f32[48,128]{1,0:T(8,128)S(1)}, u32[]{:S(2)}, u32[]{:S(2)}) collective-permute-start(f32[48,128]{1,0:T(8,128)S(1)} %add_add_fusion.3), channel_id=1, source_target_pairs={{0,40},{4,28},{8,48},{12,36},{16,56},{20,44},{24,0},{28,52},{32,8}... | collective-permute-start | bytes 73736 | tf_op jit(solution)/shard_map/ppermute | solution.py:169
  95.0 7.1 %collective-permute-start.32 = (f32[48,128]{1,0:T(8,128)S(1)}, f32[48,128]{1,0:T(8,128)S(1)}, u32[]{:S(2)}, u32[]{:S(2)}) collective-permute-start(f32[48,128]{1,0:T(8,128)S(1)} %add_add_fusion.3), channel_id=1, source_target_pairs={{0,56},{4,12},{8,0},{12,20},{16,8},{20,28},{24,16},{28,36},{32,24}... | collective-permute-start | bytes 73736 | tf_op jit(solution)/shard_map/ppermute | solution.py:169
  95.0 8.6 %collective-permute-start.29 = (f32[48,128]{1,0:T(8,128)S(1)}, f32[48,128]{1,0:T(8,128)S(1)}, u32[]{:S(2)}, u32[]{:S(2)}) collective-permute-start(f32[48,128]{1,0:T(8,128)S(1)} %add_add_fusion.3), channel_id=1, source_target_pairs={{0,32},{4,36},{8,40},{12,44},{16,48},{20,52},{24,56},{28,60},{32,0... | collective-permute-start | bytes 73736 | tf_op jit(solution)/shard_map/ppermute | solution.py:169
  (11 other events, 96.8 us)
